TPU v7x, 32 devices: a whole 2x2x4 slice. The times are simulated.
32 devices in a mesh: seq: 8 (over z, x), fsdp: 4 (over y, core).
Axes of the slice: x: 2, y: 2, z: 4, core: 2. Of those that a mesh axis runs over, the one named last changes fastest.
Arguments:
- tokens: bfloat16 [8, 2048, 768], P('fsdp', 'seq'), may hold values from -6 to 6
- cotangent: bfloat16 [8, 2048, 768], P('fsdp', 'seq'), may hold values from -6 to 6
- segments: int32 [8, 2048], P('fsdp'), may hold values from 0 to 7, never falling along the last dimension, each value on 1 to 2000 neighbouring positions
- routes: int32 [8, 2048, 2], P('fsdp', 'seq'), may hold values from 0 to 15, all different within a row
- norm_attn: bfloat16 [768], P('fsdp'), may hold values from 0.5 to 1.5
- w_qkv: bfloat16 [768, 2304], P('fsdp'), may hold values from -0.21875 to 0.21875
- w_o: bfloat16 [768, 768], P('fsdp'), may hold values from -1.75 to 1.75
- rel_bias: bfloat16 [32, 12], P('fsdp'), may hold values from -4 to 4
- norm_ffn: bfloat16 [768], P('fsdp'), may hold values from 0.5 to 1.5
- router: bfloat16 [768, 16], P('fsdp'), may hold values from -0.15625 to 0.15625
- w_in: bfloat16 [3072, 16, 768], P('fsdp', 'seq'), may hold values from -0.21875 to 0.21875
- w_out: bfloat16 [3072, 16, 768], P('fsdp', 'seq'), may hold values from -0.109375 to 0.109375
- b_out: bfloat16 [16, 768], P('seq', 'fsdp'), may hold values from -0.5 to 0.5
Outputs:
- output: bfloat16 [8, 2048, 768], P('fsdp', 'seq')
- grad_tokens: float32 [8, 2048, 768], P('fsdp', 'seq')
- grad_norm_attn: float32 [768], P('fsdp')
- grad_w_qkv: float32 [768, 2304], P('fsdp')
- grad_w_o: float32 [768, 768], P('fsdp')
- grad_rel_bias: float32 [32, 12], P('fsdp')
- grad_norm_ffn: float32 [768], P('fsdp')
- grad_router: float32 [768, 16], P('fsdp')
- grad_w_in: float32 [3072, 16, 768], P('fsdp', 'seq')
- grad_w_out: float32 [3072, 16, 768], P('fsdp', 'seq')
- grad_b_out: float32 [16, 768], P('seq', 'fsdp')
Inputs may be any that keep to these rules, and one draw needn't show every extreme that they name: `segments`: document numbers never fall along a sequence; a sequence has at most 8 documents, each of 1 to 2000 positions, one of exactly 2000. `routes`: the 2 experts of a token differ; every expert is named by some token.
All inputs are finite; a program needn't handle non-finite values.
Results may differ from a plain program's by a relative error of at most 0.02.
Values may be sent and summed in bfloat16 or wider, within the bound.
No kernel may reach another device: no remote copies, remote signals or barrier semaphores. Data moves between devices by JAX's collectives and lax.ppermute only.
A program may use at most 384 MiB of HBM per device.

v0:
```python
import math

import jax
import jax.numpy as jnp
from jax import lax
from jax.sharding import PartitionSpec as P

D = 768
HEADS = 12
HEAD_DIM = 64
TOP = 2
EXP_DEV = 2
SEQ_LEN = 2048
QBLK = 512
BUCKETS = 32


bucket_edges = tuple((int(math.ceil(16 * 8 ** (step_k / 16))) for step_k in range(1, 16)))
neg_fill = -1e30


def shortened(value):
    return jax.tree.map(lambda a: a.astype(jnp.bfloat16) if a.dtype == jnp.float32 else a, value)


def bucket_of(distance):
    far_part = 16 + sum(((distance >= edge_value).astype(jnp.int32) for edge_value in bucket_edges))
    return jnp.where(distance < 16, distance, far_part)


def normed(values, norm_gain):
    return values * lax.rsqrt(jnp.mean(values * values, -1, keepdims=True) + 1e-06) * norm_gain


def gelu_tanh(values):
    return jax.nn.gelu(values, approximate=True)


def gate_softmax(chosen):
    row_top = jnp.max(chosen, -1, keepdims=True)
    exp_terms = jnp.exp(chosen - row_top)
    return exp_terms / jnp.sum(exp_terms, -1, keepdims=True)


def masked_scores(query_rows, key_all, column, seg_pair, row_start):
    key_width = row_start + QBLK
    band_start = max(row_start - 128, 0)
    raw_scores = jnp.einsum(
        "qd,kd->qk", query_rows, key_all[:key_width], preferred_element_type=jnp.float32
    ) * HEAD_DIM ** (-0.5)
    rows_at = row_start + lax.broadcasted_iota(jnp.int32, (QBLK, key_width), 0)
    cols_at = lax.broadcasted_iota(jnp.int32, (QBLK, key_width), 1)
    distance = rows_at - cols_at
    bucket = bucket_of(jnp.maximum(distance[:, band_start:], 0))
    band_terms = sum(
        (jnp.where(bucket == index_b, column[index_b], 0.0) for index_b in range(BUCKETS))
    )
    far_terms = jnp.full((QBLK, band_start), column[BUCKETS - 1], jnp.float32)
    rel_terms = jnp.concatenate([far_terms, band_terms], 1)
    same_doc = seg_pair[row_start:key_width][:, None] == seg_pair[:key_width][None, :]
    allowed = (distance >= 0) & same_doc
    return (jnp.where(allowed, raw_scores + rel_terms, neg_fill), bucket)


def pair_forward(operands):
    query_all, key_all, value_all, seg_pair, column = operands
    outputs, totals = ([], [])
    for block_index in range(SEQ_LEN // QBLK):
        row_start = block_index * QBLK
        scores, bucket = masked_scores(
            query_all[row_start : row_start + QBLK], key_all, column, seg_pair, row_start
        )
        row_peak = jnp.max(scores, -1, keepdims=True)
        lse_block = row_peak + jnp.log(jnp.sum(jnp.exp(scores - row_peak), -1, keepdims=True))
        attn_probs = jnp.exp(scores - lse_block).astype(jnp.bfloat16)
        block_out = jnp.dot(
            attn_probs, value_all[: row_start + QBLK], preferred_element_type=jnp.float32
        )
        outputs.append(block_out.astype(jnp.bfloat16))
        totals.append(lse_block[:, 0])
    return (jnp.concatenate(outputs, 0), jnp.concatenate(totals, 0))


def pair_backward(operands):
    query_all, key_all, value_all, seg_pair, column, lse_pair, grad_out = operands
    scale_factor = HEAD_DIM ** (-0.5)
    query_grads = []
    grad_key = jnp.zeros(key_all.shape, jnp.float32)
    grad_value = jnp.zeros(value_all.shape, jnp.float32)
    grad_column = jnp.zeros((BUCKETS,), jnp.float32)
    for block_index in range(SEQ_LEN // QBLK):
        row_start = block_index * QBLK
        key_width = row_start + QBLK
        query_rows = query_all[row_start:key_width]
        grad_rows = grad_out[row_start:key_width]
        scores, band_bucket = masked_scores(query_rows, key_all, column, seg_pair, row_start)
        attn_probs = jnp.exp(scores - lse_pair[row_start:key_width][:, None])
        grad_probs = jnp.einsum(
            "qd,kd->qk", grad_rows, value_all[:key_width], preferred_element_type=jnp.float32
        )
        row_delta = jnp.sum(attn_probs * grad_probs, -1, keepdims=True)
        grad_scores = (attn_probs * (grad_probs - row_delta)).astype(jnp.bfloat16)
        query_grads.append(
            jnp.dot(grad_scores, key_all[:key_width], preferred_element_type=jnp.float32)
            * scale_factor
        )
        grad_key = grad_key.at[:key_width].add(
            jnp.einsum("qk,qd->kd", grad_scores, query_rows, preferred_element_type=jnp.float32)
            * scale_factor
        )
        grad_value = grad_value.at[:key_width].add(
            jnp.einsum(
                "qk,qd->kd",
                attn_probs.astype(jnp.bfloat16),
                grad_rows,
                preferred_element_type=jnp.float32,
            )
        )
        band_start = max(row_start - 128, 0)
        band_values = grad_scores[:, band_start:].astype(jnp.float32)
        near_sums = jnp.stack(
            [
                jnp.sum(jnp.where(band_bucket == index_b, band_values, 0.0))
                for index_b in range(BUCKETS - 1)
            ]
        )
        whole_sum = jnp.sum(grad_scores.astype(jnp.float32))
        grad_column = grad_column + jnp.concatenate(
            [near_sums, (whole_sum - jnp.sum(near_sums))[None]]
        )
    grad_query = jnp.concatenate(query_grads, 0)
    return (
        grad_query.astype(jnp.bfloat16),
        grad_key.astype(jnp.bfloat16),
        grad_value.astype(jnp.bfloat16),
        grad_column,
    )


def per_device(
    tokens,
    cotangent,
    segments,
    routes,
    norm_attn,
    w_qkv,
    w_o,
    rel_bias,
    norm_ffn,
    router,
    w_in,
    w_out,
    b_out,
):
    seq_count = lax.axis_size("seq")
    group_seqs, slab_len = (tokens.shape[0], tokens.shape[1])
    token_count = group_seqs * slab_len
    pair_count = group_seqs * HEADS // seq_count
    gain_attn, qkv_full, proj_full, bias_full, gain_ffn, router_full, bout_full = (
        lax.all_gather(norm_attn, "fsdp", axis=0, tiled=True),
        lax.all_gather(w_qkv, "fsdp", axis=0, tiled=True),
        lax.all_gather(w_o, "fsdp", axis=0, tiled=True),
        lax.all_gather(rel_bias, "fsdp", axis=0, tiled=True),
        lax.all_gather(norm_ffn, "fsdp", axis=0, tiled=True),
        lax.all_gather(router, "fsdp", axis=0, tiled=True),
        lax.all_gather(b_out, "fsdp", axis=1, tiled=True),
    )
    expert_count = router_full.shape[1]
    capacity = max(2, 9 * token_count * TOP // (8 * expert_count))
    tokens_f = tokens.astype(jnp.float32).reshape(token_count, D)
    first_norm, pull_first = jax.vjp(normed, tokens_f, gain_attn.astype(jnp.float32))
    first_low = first_norm.astype(jnp.bfloat16).reshape(group_seqs, slab_len, D)
    qkv_weight = qkv_full.reshape(D, 3, HEADS, HEAD_DIM)
    projected = jnp.einsum(
        "gsm,mthd->tghsd", first_low, qkv_weight, preferred_element_type=jnp.float32
    )
    projected = projected.astype(jnp.bfloat16).reshape(3, group_seqs * HEADS, slab_len * HEAD_DIM)
    per_head = lax.all_to_all(projected, "seq", split_axis=1, concat_axis=2, tiled=True).reshape(
        3, pair_count, SEQ_LEN, HEAD_DIM
    )
    pair_ids = lax.axis_index("seq") * pair_count + jnp.arange(pair_count, dtype=jnp.int32)
    seg_pairs = jnp.take(segments, pair_ids // HEADS, axis=0)
    head_match = (pair_ids % HEADS)[None, :] == jnp.arange(HEADS, dtype=jnp.int32)[:, None]
    bias_table = bias_full.astype(jnp.float32)
    columns = jnp.sum(jnp.where(head_match[None], bias_table[:, :, None], 0.0), 1).T
    attended, lse_all = lax.map(
        pair_forward, (per_head[0], per_head[1], per_head[2], seg_pairs, columns)
    )
    back_tokens = lax.all_to_all(
        shortened(attended.reshape(pair_count, SEQ_LEN * HEAD_DIM)),
        "seq",
        split_axis=1,
        concat_axis=0,
        tiled=True,
    )
    attended_tok = back_tokens.reshape(group_seqs, HEADS, slab_len, HEAD_DIM)
    proj_weight = proj_full.reshape(HEADS, HEAD_DIM, D)
    attn_out = jnp.einsum(
        "ghsd,hdm->gsm", attended_tok, proj_weight, preferred_element_type=jnp.float32
    )
    residual_mid = tokens_f + attn_out.reshape(token_count, D)
    second_norm, pull_second = jax.vjp(normed, residual_mid, gain_ffn.astype(jnp.float32))
    second_low = second_norm.astype(jnp.bfloat16)
    logits = jnp.dot(second_low, router_full, preferred_element_type=jnp.float32)
    route_pairs = routes.reshape(token_count, TOP)
    expert_iota = jnp.arange(expert_count, dtype=jnp.int32)
    picked = route_pairs[:, :, None] == expert_iota[None, None, :]
    chosen = jnp.sum(jnp.where(picked, logits[:, None, :], 0.0), -1)
    gates, pull_gates = jax.vjp(gate_softmax, chosen)
    flat_routes = route_pairs.reshape(token_count * TOP)
    pair_total = token_count * TOP
    hit_table = (flat_routes[:, None] == expert_iota[None, :]).astype(jnp.int32)
    pair_rank = jnp.sum(jnp.cumsum(hit_table, 0) * hit_table, 1) - 1
    kept_pair = pair_rank < capacity
    pair_slot = jnp.where(kept_pair, flat_routes * capacity + pair_rank, 0)
    slot_total = expert_count * capacity
    slot_pair = (
        jnp.full((slot_total,), -1, jnp.int32)
        .at[jnp.where(kept_pair, pair_slot, slot_total)]
        .set(jnp.arange(pair_total, dtype=jnp.int32), mode="drop")
    )
    filled = slot_pair >= 0
    slot_token = jnp.maximum(slot_pair, 0) // TOP
    zero_half = jnp.zeros((), jnp.bfloat16)
    dispatched = jnp.where(filled[:, None], jnp.take(second_low, slot_token, axis=0), zero_half)
    at_experts = lax.all_to_all(
        dispatched.reshape(expert_count, capacity, D),
        "seq",
        split_axis=0,
        concat_axis=1,
        tiled=True,
    )
    in_full, out_full = (
        lax.all_gather(w_in, "fsdp", axis=0, tiled=True),
        lax.all_gather(w_out, "fsdp", axis=0, tiled=True),
    )
    expert_bias = bout_full.astype(jnp.float32)
    pre_list, act_list, result_list = ([], [], [])
    for expert_index in range(EXP_DEV):
        pre_one = jnp.einsum(
            "rd,fd->rf",
            at_experts[expert_index],
            in_full[:, expert_index],
            preferred_element_type=jnp.float32,
        )
        act_one = gelu_tanh(pre_one).astype(jnp.bfloat16)
        result_one = (
            jnp.dot(act_one, out_full[:, expert_index], preferred_element_type=jnp.float32)
            + expert_bias[expert_index]
        )
        pre_list.append(pre_one)
        act_list.append(act_one)
        result_list.append(result_one.astype(jnp.bfloat16))
    returned = lax.all_to_all(
        jnp.stack(result_list), "seq", split_axis=1, concat_axis=0, tiled=True
    ).reshape(slot_total, D)
    pair_rows = jnp.where(kept_pair[:, None], jnp.take(returned, pair_slot, axis=0), zero_half)
    pair_rows = pair_rows.astype(jnp.float32).reshape(token_count, TOP, D)
    moe_out = jnp.sum(gates[:, :, None] * pair_rows, 1)
    output = (residual_mid + moe_out).astype(jnp.bfloat16).reshape(group_seqs, slab_len, D)
    grad_top = cotangent.astype(jnp.float32).reshape(token_count, D)
    grad_gates = jnp.sum(grad_top[:, None, :] * pair_rows, -1)
    slot_gate = jnp.take(gates.reshape(pair_total), jnp.maximum(slot_pair, 0))
    slot_grads = jnp.where(
        filled[:, None], jnp.take(grad_top, slot_token, axis=0) * slot_gate[:, None], 0.0
    )
    slot_grads = slot_grads.astype(jnp.bfloat16).reshape(expert_count, capacity, D)
    grad_at_experts = lax.all_to_all(slot_grads, "seq", split_axis=0, concat_axis=1, tiled=True)
    in_back, out_back = (
        lax.all_gather(w_in, "fsdp", axis=0, tiled=True),
        lax.all_gather(w_out, "fsdp", axis=0, tiled=True),
    )
    grad_pre_list, grad_rows_list = ([], [])
    for expert_index in range(EXP_DEV):
        grad_act = jnp.einsum(
            "rd,fd->rf",
            grad_at_experts[expert_index],
            out_back[:, expert_index],
            preferred_element_type=jnp.float32,
        )
        grad_pre_f = jax.vjp(gelu_tanh, pre_list[expert_index])[1](grad_act)[0]
        grad_pre = grad_pre_f.astype(jnp.bfloat16)
        grad_pre_list.append(grad_pre)
        grad_rows_list.append(
            jnp.dot(grad_pre, in_back[:, expert_index], preferred_element_type=jnp.float32).astype(
                jnp.bfloat16
            )
        )
    grad_b_local = jnp.sum(grad_at_experts.astype(jnp.float32), 1)
    term_list = []
    for expert_index in range(EXP_DEV):
        grad_slice = grad_pre_list[expert_index]
        act_slice = act_list[expert_index]
        term_in = jnp.einsum(
            "rf,rd->fd", grad_slice, at_experts[expert_index], preferred_element_type=jnp.float32
        )
        term_out = jnp.einsum(
            "rf,rd->fd",
            act_slice,
            grad_at_experts[expert_index],
            preferred_element_type=jnp.float32,
        )
        term_list.append(jnp.stack([term_in, term_out], 1))
    weight_grads = lax.psum_scatter(
        jnp.stack(term_list, 1).astype(jnp.bfloat16), "fsdp", scatter_dimension=0, tiled=True
    ).astype(jnp.float32)
    returned_grads = lax.all_to_all(
        jnp.stack(grad_rows_list), "seq", split_axis=1, concat_axis=0, tiled=True
    ).reshape(slot_total, D)
    grad_from_experts = jnp.where(
        kept_pair[:, None], jnp.take(returned_grads, pair_slot, axis=0), zero_half
    )
    grad_from_experts = jnp.sum(
        grad_from_experts.astype(jnp.float32).reshape(token_count, TOP, D), 1
    )
    grad_chosen = pull_gates(grad_gates)[0]
    grad_logits = jnp.sum(jnp.where(picked, grad_chosen[:, :, None], 0.0), 1).astype(jnp.bfloat16)
    grad_router = jnp.einsum(
        "tm,te->me", second_low, grad_logits, preferred_element_type=jnp.float32
    )
    grad_second = grad_from_experts + jnp.einsum(
        "te,me->tm", grad_logits, router_full, preferred_element_type=jnp.float32
    )
    grad_mid_norm, grad_gain_ffn = pull_second(grad_second)
    grad_mid = grad_top + grad_mid_norm
    grad_attn_low = grad_mid.astype(jnp.bfloat16).reshape(group_seqs, slab_len, D)
    grad_proj = jnp.einsum(
        "ghsd,gsm->hdm", attended_tok, grad_attn_low, preferred_element_type=jnp.float32
    ).reshape(D, D)
    grad_attended = jnp.einsum(
        "gsm,hdm->ghsd", grad_attn_low, proj_weight, preferred_element_type=jnp.float32
    )
    grad_attended = grad_attended.astype(jnp.bfloat16).reshape(
        group_seqs * HEADS, slab_len * HEAD_DIM
    )
    grad_heads = lax.all_to_all(
        grad_attended, "seq", split_axis=0, concat_axis=1, tiled=True
    ).reshape(pair_count, SEQ_LEN, HEAD_DIM)
    grad_query, grad_key, grad_value, grad_columns = lax.map(
        pair_backward,
        (per_head[0], per_head[1], per_head[2], seg_pairs, columns, lse_all, grad_heads),
    )
    grad_stack = jnp.stack([grad_query, grad_key, grad_value]).reshape(
        3, pair_count, SEQ_LEN * HEAD_DIM
    )
    grad_projected = (
        lax.all_to_all(shortened(grad_stack), "seq", split_axis=2, concat_axis=1, tiled=True)
        .astype(grad_stack.dtype)
        .reshape(3, group_seqs, HEADS, slab_len, HEAD_DIM)
    )
    grad_qkv = jnp.einsum(
        "gsm,tghsd->mthd", first_low, grad_projected, preferred_element_type=jnp.float32
    ).reshape(D, 3 * D)
    grad_first = jnp.einsum(
        "tghsd,mthd->gsm", grad_projected, qkv_weight, preferred_element_type=jnp.float32
    ).reshape(token_count, D)
    grad_tok_norm, grad_gain_attn = pull_first(grad_first)
    grad_tokens = (grad_mid + grad_tok_norm).reshape(group_seqs, slab_len, D)
    grad_bias_local = jnp.sum(jnp.where(head_match[None], grad_columns.T[:, None, :], 0.0), 2)
    (
        owned_gain_attn,
        owned_qkv,
        owned_proj,
        owned_bias,
        owned_gain_ffn,
        owned_router,
        grad_b_owned,
    ) = (
        lax.psum_scatter(
            grad_gain_attn.astype(jnp.bfloat16), "fsdp", scatter_dimension=0, tiled=True
        ).astype(jnp.float32),
        lax.psum_scatter(
            grad_qkv.astype(jnp.bfloat16), "fsdp", scatter_dimension=0, tiled=True
        ).astype(jnp.float32),
        lax.psum_scatter(
            grad_proj.astype(jnp.bfloat16), "fsdp", scatter_dimension=0, tiled=True
        ).astype(jnp.float32),
        lax.psum_scatter(
            grad_bias_local.astype(jnp.bfloat16), "fsdp", scatter_dimension=0, tiled=True
        ).astype(jnp.float32),
        lax.psum_scatter(
            grad_gain_ffn.astype(jnp.bfloat16), "fsdp", scatter_dimension=0, tiled=True
        ).astype(jnp.float32),
        lax.psum_scatter(
            grad_router.astype(jnp.bfloat16), "fsdp", scatter_dimension=0, tiled=True
        ).astype(jnp.float32),
        lax.psum_scatter(
            grad_b_local.astype(jnp.bfloat16), "fsdp", scatter_dimension=1, tiled=True
        ).astype(jnp.float32),
    )
    total_gain_attn, total_qkv, total_proj, total_bias, total_gain_ffn, total_router = (
        lax.psum(owned_gain_attn.astype(jnp.bfloat16), "seq").astype(jnp.float32),
        lax.psum(owned_qkv.astype(jnp.bfloat16), "seq").astype(jnp.float32),
        lax.psum(owned_proj.astype(jnp.bfloat16), "seq").astype(jnp.float32),
        lax.psum(owned_bias.astype(jnp.bfloat16), "seq").astype(jnp.float32),
        lax.psum(owned_gain_ffn.astype(jnp.bfloat16), "seq").astype(jnp.float32),
        lax.psum(owned_router.astype(jnp.bfloat16), "seq").astype(jnp.float32),
    )
    return (
        output,
        grad_tokens,
        total_gain_attn,
        total_qkv,
        total_proj,
        total_bias,
        total_gain_ffn,
        total_router,
        weight_grads[:, :, 0],
        weight_grads[:, :, 1],
        grad_b_owned,
    )


def solution(mesh):
    in_specs = (
        P("fsdp", "seq", None),
        P("fsdp", "seq", None),
        P("fsdp", None),
        P("fsdp", "seq", None),
        P("fsdp"),
        P("fsdp", None),
        P("fsdp", None),
        P("fsdp", None),
        P("fsdp"),
        P("fsdp", None),
        P("fsdp", "seq", None),
        P("fsdp", "seq", None),
        P("seq", "fsdp"),
    )
    out_specs = (
        P("fsdp", "seq", None),
        P("fsdp", "seq", None),
        P("fsdp"),
        P("fsdp", None),
        P("fsdp", None),
        P("fsdp", None),
        P("fsdp"),
        P("fsdp", None),
        P("fsdp", "seq", None),
        P("fsdp", "seq", None),
        P("seq", "fsdp"),
    )
    return jax.shard_map(
        per_device, mesh=mesh, in_specs=in_specs, out_specs=out_specs, check_vma=False
    )
```

profile of v0, /device:TPU:0, one launch (start us, length us, event | category | flops | bytes accessed | tf_op | source)
XLA Modules:
  0.0 2753.7 jit_solution(3777278263341030791)
XLA Ops:
  14.5 8.9 all-reduce.16
  24.8 18.3 all-gather.7.cloned.1.call-done
  83.3 60.3 %all-to-all-done = bf16[3,24,16384]{2,0,1:T(4,128)(2,1)S(1)} async-done(((bf16[3,24,16384]{2,0,1:T(4,128)(2,1)}), bf16[3,24,16384]{2,0,1:T(4,128)(2,1)S(1)}, u32[]{:S(2)}, u32[]{:S(2)}) %all-to-all-start) | async-done | bytes 2359328 | tf_op jit(solution)/shard_map/all_to_all | solution.py:178
  157.7 377.7 %while.41 = (s32[]{:T(128)}, bf16[3,2048,64]{1,2,0:T(8,128)(2,1)S(1)}, f32[3,2048]{1,0:T(4,128)}, s32[3,2048]{1,0:T(4,128)S(1)}, bf16[3,2048,64]{2,1,0:T(8,128)(...) while((s32[]{:T(128)}, ...), condition=%wide.region_11.12_spmd, body=%wide.region_2.11_spmd.sunk | while | flops 884151808 | bytes 56838240 | solution.py:186
  159.8 26.3 fusion.414
  186.4 26.1 select_add_fusion.15
  218.6 26.1 select_add_fusion.14
  248.6 26.1 select_add_fusion.13
  285.5 26.3 fusion.414
  312.1 26.1 select_add_fusion.15
  344.3 26.1 select_add_fusion.14
  374.3 26.1 select_add_fusion.13
  411.2 26.3 fusion.414
  437.8 26.1 select_add_fusion.15
  470.0 26.1 select_add_fusion.14
  500.0 26.1 select_add_fusion.13
  553.3 15.5 all-to-all-done.1
  591.3 36.2 %all-to-all-done.2 = bf16[16,72,768]{2,1,0:T(8,128)(2,1)S(1)} async-done(((bf16[16,72,768]{2,1,0:T(8,128)(2,1)}), bf16[16,72,768]{2,1,0:T(8,128)(2,1)S(1)}, u32[]{:S(2)}, u32[]{:S(2)}) %all-to-all-start.2) | async-done | bytes 1769504 | tf_op jit(solution)/shard_map/all_to_all | solution.py:226
  628.5 8.8 fusion.273
  683.1 21.4 all-to-all-done.3
  727.6 45.1 %all_to_all.122 = bf16[16,72,768]{2,1,0:T(8,128)(2,1)S(1)} all-to-all(bf16[16,72,768]{2,1,0:T(8,128)(2,1)S(1)} %select_convert_fusion), channel_id=1, replica_groups=mesh['seq'=8,'fsdp'=4] {'seq'}, dimensions={0} | all-to-all | bytes 3538944 | tf_op jit(solution)/shard_map/all_to_all | solution.py:268
  773.9 12.3 fusion.263
  806.6 40.8 %all-to-all-done.5 = bf16[2,576,768]{2,0,1:T(2,128)(2,1)S(1)} async-done(((bf16[2,576,768]{2,0,1:T(2,128)(2,1)}), bf16[2,576,768]{2,0,1:T(2,128)(2,1)S(1)}, u32[]{:S(2)}, u32[]{:S(2)}) %all-to-all-start.5) | async-done | bytes 1769504 | tf_op jit(solution)/shard_map/all_to_all | solution.py:307
  879.2 25.9 all-to-all-done.6
  911.5 773.0 %while.42 = (s32[]{:T(128)}, bf16[3,2048,64]{1,2,0:T(8,128)(2,1)}, bf16[3,2048,64]{1,2,0:T(8,128)(2,1)}, bf16[3,2048,64]{1,2,0:T(8,128)(2,1)}, f32[3,32]{1,0:T(4...) while((s32[]{:T(128)}, bf16[3,2048,64]{1,2,0:T(8,128)(2,1)}, ...), condition=%wide.region_161.163_spmd, body=%wide.region_28.162_spmd.sunk | while | flops 2032205440 | bytes 128760872 | solution.py:339
  933.9 26.0 multiply_reduce_fusion.17
  992.3 25.7 select_add_fusion.18
  1054.1 25.7 select_add_fusion.17
  1117.5 25.7 select_add_fusion.16
  1185.5 26.0 multiply_reduce_fusion.17
  1243.8 25.7 select_add_fusion.18
  1305.6 25.7 select_add_fusion.17
  1369.0 25.7 select_add_fusion.16
  1437.0 26.0 multiply_reduce_fusion.17
  1495.3 25.7 select_add_fusion.18
  1557.1 25.7 select_add_fusion.17
  1620.6 25.7 select_add_fusion.16
  1698.6 123.7 %copy.231 = bf16[3,3,131072]{1,0,2:T(4,128)(2,1)} copy(bf16[3,3,131072]{2,1,0:T(4,128)(2,1)S(1)} %pad_maximum_fusion.2) | data formatting | bytes 4718592 | tf_op jit(solution)/shard_map/stack | solution.py:343
  1822.3 181.4 %reshape.3751 = bf16[8,2,73728]{2,1,0:T(2,128)(2,1)} reshape(bf16[131072,3,3]{2,1,0:T(4,128)(2,1)} %bitcast.532) | data formatting | bytes 4718592
  2011.2 50.4 %all-to-all-done.7 = bf16[8,2,73728]{2,1,0:T(2,128)(2,1)} async-done(((bf16[8,2,73728]{2,1,0:T(2,128)(2,1)}), bf16[8,2,73728]{2,1,0:T(2,128)(2,1)}, u32[]{:S(2)}, u32[]{:S(2)}) %all-to-all-start.7) | async-done | bytes 2359328 | tf_op jit(solution)/shard_map/all_to_all | solution.py:347
  2061.6 187.2 %reshape.3752 = bf16[131072,3,3]{2,1,0:T(4,128)(2,1)} reshape(bf16[8,2,73728]{2,1,0:T(2,128)(2,1)} %all-to-all-done.7) | data formatting | bytes 4718592
  2248.8 157.6 %copy.232 = bf16[3,3,8,16384]{3,1,2,0:T(4,128)(2,1)S(1)} copy(bf16[3,3,8,16384]{1,0,3,2:T(4,128)(2,1)} %bitcast.303) | data formatting | bytes 4718592 | tf_op jit(solution)/shard_map/all_to_all | solution.py:347
  2423.5 10.8 fusion.265
  2434.3 10.2 fusion.267
  2483.7 21.9 reduce-scatter.18.cloned.1.call-done
  2532.6 10.1 all-reduce.15
  2542.8 37.8 %all-reduce.13 = (bf16[192]{0:T(256)(128)(2,1)S(1)}, bf16[8,12]{1,0:T(8,128)(2,1)S(1)}, bf16[192]{0:T(256)(128)(2,1)S(1)}, bf16[192,16]{0,1:T(8,128)(2,1)S(1)}) all-reduce(bf16[192]{0:T(256)(128)(2,1)S(1)} %dynamic-slice.63, bf16[8,12]{1,0:T(8,128)(2,1)S(1)} %constant_dynamic-slice_fusion.10, ...), channel_id=1, replica_groups=mesh['seq'=8,'fsdp'=4] {'seq'}, use_global_device_ids=true, to_apply=%region_165.167 | all-reduce | flops 3552 | bytes 14208 | tf_op jit(solution)/shard_map/psum | solution.py:392
  2592.8 138.2 %reduce-scatter.14.cloned.1.call-done = bf16[768,2,2,768]{3,0,2,1:T(8,128)(2,1)} async-done(((bf16[3072,2,2,768]{3,0,2,1:T(8,128)(2,1)}), bf16[768,2,2,768]{3,0,2,1:T(8,128)(2,1)}) %reduce-scatter.14.cloned.1.call-update) | async-done | bytes 4718608 | tf_op jit(solution)/shard_map/reduce_scatter | solution.py:304
  (661 shorter events, 630.1 us)
Async XLA Ops:
  7.2 75.3 %copy-start = (s32[2,2048]{1,0:T(2,128)S(1)}, s32[2,2048]{1,0:T(2,128)}, u32[]{:S(2)}) copy-start(s32[2,2048]{1,0:T(2,128)} %param.41) | copy-start | bytes 49156
  7.2 35.9 %all-gather.7.cloned.1.call-start = ((), (), s32[]{:S(2)}) async-start(), calls=%async_computation.13 | async-start | bytes 4423680 | tf_op jit(solution)/shard_map/all_gather | solution.py:161
  7.9 564.5 %all-gather.9.cloned.1.call-start = ((), (), s32[]{:S(2)}) async-start(), calls=%async_computation.14 | async-start | bytes 1474560 | tf_op jit(solution)/shard_map/all_gather | solution.py:162
  8.7 619.9 %all-gather.11.cloned.1.call-start = ((), (), s32[]{:S(2)}) async-start(), calls=%async_computation.15 | async-start | bytes 11796480 | tf_op jit(solution)/shard_map/all_gather | solution.py:234
  12.1 11.9 copy-start.20
  67.0 76.6 %all-to-all-start = ((bf16[3,24,16384]{2,0,1:T(4,128)(2,1)}), bf16[3,24,16384]{2,0,1:T(4,128)(2,1)S(1)}, u32[]{:S(2)}, u32[]{:S(2)}) async-start(bf16[3,24,16384]{2,0,1:T(4,128)(2,1)} %reshape.3736), calls=%async_computation | async-start | bytes 6291456 | tf_op jit(solution)/shard_map/all_to_all | solution.py:178
  72.5 570.3 %all-gather.13.cloned.1.call-start = ((), (), s32[]{:S(2)}) async-start(), calls=%async_computation.16 | async-start | bytes 11796480 | tf_op jit(solution)/shard_map/all_gather | solution.py:235
  83.2 62.9 %copy-start.80 = (pred[12,3]{0,1:T(4,128)(4,1)}, pred[12,3]{0,1:T(4,128)(4,1)S(1)}, u32[]{:S(2)}) copy-start(pred[12,3]{0,1:T(4,128)(4,1)S(1)} %iota_compare_fusion.3) | copy-start | bytes 112
  539.1 29.7 %all-to-all-start.1 = ((bf16[3,8,16384]{2,0,1:T(4,128)(2,1)}), bf16[3,8,16384]{2,0,1:T(4,128)(2,1)S(1)}, u32[]{:S(2)}, u32[]{:S(2)}) async-start(bf16[3,8,16384]{2,0,1:T(4,128)(2,1)} %copy.207), calls=%async_computation.1 | async-start | bytes 2097152 | tf_op jit(solution)/shard_map/all_to_all | solution.py:189
  543.4 31.6 %copy-start.45 = (f32[768]{0:T(1024)}, f32[768]{0:T(1024)S(1)}, u32[]{:S(2)}) copy-start(f32[768]{0:T(1024)S(1)} %convert_element_type.12063) | copy-start | bytes 9220
  548.7 157.5 %copy-start.55 = (s32[1024]{0:T(1024)}, s32[1024]{0:T(1024)S(1)}, u32[]{:S(2)}) copy-start(s32[1024]{0:T(1024)S(1)} %get-tuple-element.788) | copy-start | bytes 12292
  553.2 27.7 %copy-start.58 = (pred[16,72]{1,0:T(8,128)(4,1)}, pred[16,72]{1,0:T(8,128)(4,1)S(1)}, u32[]{:S(2)}) copy-start(pred[16,72]{1,0:T(8,128)(4,1)S(1)} %broadcast_in_dim.1497) | copy-start | bytes 3460
  553.3 27.6 %copy-start.59 = (pred[16,72]{1,0:T(8,128)(4,1)}, pred[16,72]{1,0:T(8,128)(4,1)S(1)}, u32[]{:S(2)}) copy-start(pred[16,72]{1,0:T(8,128)(4,1)S(1)} %broadcast_in_dim.1495) | copy-start | bytes 3460
  576.3 106.3 %copy-start.2 = (bf16[512,768]{1,0:T(8,128)(2,1)}, bf16[512,768]{1,0:T(8,128)(2,1)S(1)}, u32[]{:S(2)}) copy-start(bf16[512,768]{1,0:T(8,128)(2,1)S(1)} %multiply_convert_fusion.6) | copy-start | bytes 2359300
  582.3 45.2 %all-to-all-start.2 = ((bf16[16,72,768]{2,1,0:T(8,128)(2,1)}), bf16[16,72,768]{2,1,0:T(8,128)(2,1)S(1)}, u32[]{:S(2)}, u32[]{:S(2)}) async-start(bf16[16,72,768]{2,1,0:T(8,128)(2,1)} %select_select_fusion), calls=%async_computation.2 | async-start | bytes 3538944 | tf_op jit(solution)/shard_map/all_to_all | solution.py:226
  659.2 45.3 %all-to-all-start.3 = ((bf16[2,576,768]{2,0,1:T(2,128)(2,1)}), bf16[2,576,768]{2,0,1:T(2,128)(2,1)}, u32[]{:S(2)}, u32[]{:S(2)}) async-start(bf16[2,576,768]{2,0,1:T(2,128)(2,1)} %copy.219), calls=%async_computation.3 | async-start | bytes 3538944 | tf_op jit(solution)/shard_map/all_to_all | solution.py:254
  669.0 13.6 copy-start.41
  682.6 27.6 %copy-start.62 = (pred[1024]{0:T(1024)(128)(4,1)}, pred[1024]{0:T(1024)(128)(4,1)S(1)}, u32[]{:S(2)}) copy-start(pred[1024]{0:T(1024)(128)(4,1)S(1)} %get-tuple-element.786) | copy-start | bytes 3076
  682.6 27.6 %copy-start.64 = (pred[1024]{0:T(1024)(128)(4,1)}, pred[1024]{0:T(1024)(128)(4,1)S(1)}, u32[]{:S(2)}) copy-start(pred[1024]{0:T(1024)(128)(4,1)S(1)} %get-tuple-element.787) | copy-start | bytes 3076
  683.0 31.3 %copy-start.50 = (f32[512]{0:T(512)}, f32[512]{0:T(512)S(1)}, u32[]{:S(2)}) copy-start(f32[512]{0:T(512)S(1)} %reduce_max.45) | copy-start | bytes 6148
  772.7 13.6 slice-start.3
  772.7 13.6 slice-start.6
  773.9 12.4 copy-start.34
  773.9 12.4 copy-start.36
  773.9 12.4 slice-start.4
  773.9 12.4 slice-start.5
  773.9 12.4 slice-start.7
  773.9 19.2 slice-start
  773.9 19.2 slice-start.1
  802.6 44.8 %all-to-all-start.5 = ((bf16[2,576,768]{2,0,1:T(2,128)(2,1)}), bf16[2,576,768]{2,0,1:T(2,128)(2,1)S(1)}, u32[]{:S(2)}, u32[]{:S(2)}) async-start(bf16[2,576,768]{2,0,1:T(2,128)(2,1)} %copy.222), calls=%async_computation.5 | async-start | bytes 3538944 | tf_op jit(solution)/shard_map/all_to_all | solution.py:307
  806.6 61.9 %copy-start.43 = (bf16[512,16]{0,1:T(8,128)(2,1)}, bf16[512,16]{0,1:T(8,128)(2,1)S(1)}, u32[]{:S(2)}) copy-start(bf16[512,16]{0,1:T(8,128)(2,1)S(1)} %select_reduce_fusion) | copy-start | bytes 49156
  875.6 29.6 %all-to-all-start.6 = ((bf16[8,3,16384]{2,1,0:T(4,128)(2,1)}), bf16[8,3,16384]{2,1,0:T(4,128)(2,1)S(1)}, u32[]{:S(2)}, u32[]{:S(2)}) async-start(bf16[8,3,16384]{2,1,0:T(4,128)(2,1)} %all_to_all.108), calls=%async_computation.6 | async-start | bytes 2097152 | tf_op jit(solution)/shard_map/all_to_all | solution.py:336
  2003.7 57.9 %all-to-all-start.7 = ((bf16[8,2,73728]{2,1,0:T(2,128)(2,1)}), bf16[8,2,73728]{2,1,0:T(2,128)(2,1)}, u32[]{:S(2)}, u32[]{:S(2)}) async-start(bf16[8,2,73728]{2,1,0:T(2,128)(2,1)} %reshape.3751), calls=%async_computation.7 | async-start | bytes 4718592 | tf_op jit(solution)/shard_map/all_to_all | solution.py:347
  2008.2 451.1 %reduce-scatter.12.cloned.1.call-start = ((), (), s32[]{:S(2)}) async-start(), calls=%async_computation.18 | async-start | bytes 1474560 | tf_op jit(solution)/shard_map/reduce_scatter | solution.py:375
  2011.2 448.9 %reduce-scatter.10.cloned.1.call-start = ((), (), s32[]{:S(2)}) async-start(), calls=%async_computation.17 | async-start | bytes 4423680 | tf_op jit(solution)/shard_map/reduce_scatter | solution.py:372
  2421.3 61.6 %reduce-scatter.16.cloned.1.call-start = ((), (), s32[]{:S(2)}) async-start(), calls=%async_computation.20 | async-start | bytes 245760
  2423.4 10.9 copy-start.35
  2423.5 82.1 %reduce-scatter.18.cloned.1.call-start = ((), (), s32[]{:S(2)}) async-start(), calls=%async_computation.21 | async-start | bytes 245760
  2434.3 10.2 copy-start.33
  2434.3 10.2 copy-start.91
  2451.6 137.9 %all-reduce.19.cloned.1.call-start = ((), (), s32[]{:S(2)}) async-start(), calls=%async_computation.22 | async-start | bytes 2359296 | tf_op jit(solution)/shard_map/psum | solution.py:393
  2460.1 270.9 %reduce-scatter.14.cloned.1.call-start = ((), (), s32[]{:S(2)}) async-start(), calls=%async_computation.19 | async-start | bytes 23592960 | tf_op jit(solution)/shard_map/reduce_scatter | solution.py:304
  2475.9 31.2 %copy-start.16 = (f32[1024,768]{1,0:T(8,128)S(1)}, f32[1024,768]{1,0:T(8,128)}, u32[]{:S(2)}) copy-start(f32[1024,768]{1,0:T(8,128)} %get-tuple-element.793) | copy-start | bytes 9437188
  2526.1 56.8 %copy-start.6 = (f32[512,768]{1,0:T(8,128)S(1)}, f32[512,768]{1,0:T(8,128)}, u32[]{:S(2)}) copy-start(f32[512,768]{1,0:T(8,128)} %copy-done.4) | copy-start | bytes 4718596
  2526.1 56.8 %copy-start.11 = (f32[512,768]{1,0:T(8,128)S(1)}, f32[512,768]{1,0:T(8,128)}, u32[]{:S(2)}) copy-start(f32[512,768]{1,0:T(8,128)} %copy-done.10) | copy-start | bytes 4718596
  2526.1 56.9 %copy-start.47 = (f32[768]{0:T(1024)S(1)}, f32[768]{0:T(1024)}, u32[]{:S(2)}) copy-start(f32[768]{0:T(1024)} %copy-done.45) | copy-start | bytes 9220
  2526.1 56.9 %copy-start.54 = (f32[512]{0:T(512)S(1)}, f32[512]{0:T(512)}, u32[]{:S(2)}) copy-start(f32[512]{0:T(512)} %copy-done.52) | copy-start | bytes 6148
  2526.1 56.9 %copy-start.57 = (f32[512]{0:T(512)S(1)}, f32[512]{0:T(512)}, u32[]{:S(2)}) copy-start(f32[512]{0:T(512)} %copy-done.56) | copy-start | bytes 6148
  (73 other events, 266.4 us)
Sparse Core Ops, SparseCore 0:
  9.6 33.4 all-gather.6
  44.7 17.4 all-gather.8
  63.8 64.2 all-gather.10
  130.1 64.2 all-gather.12
  2011.9 26.1 reduce-scatter.11
  2421.4 38.6 reduce-scatter.9
  2463.1 19.7 reduce-scatter.15
  2485.8 19.7 reduce-scatter.17
  2509.1 80.4 all-reduce.18
  2592.2 138.7 reduce-scatter.13
where the time goes:
time: 2780 us; the launch traced here: 2750 us
  local copies, waits for them, and re-layouts  852 us (31%)
  other arithmetic  625 us (22%)
  waiting for transfers between devices  439 us (16%)
  matrix products  412 us (15%)
  loops' own time  260 us (9%)
  blocking collectives  118 us (4%)
  starting transfers between devices  30 us (1%)
    add x18, other arithmetic, masked_scores(): sum((jnp.where(bucket == index_b, column[index_b], 0.0) for index_b in ra...  466 us
    unnamed x217, local copies, waits for them, and re-layouts  400 us
    another operation x1, loops' own time, per_device(): lax.map(pair_backward, (per_head[0], per_head[1], per_head[2], seg_pairs,...  259 us
    dot_general x24, matrix products, masked_scores(): jnp.einsum('qd,kd->qk', query_rows, key_all[:key_width], preferred_elemen...  214 us
    all_to_all x1, local copies, waits for them, and re-layouts, per_device(): lax.all_to_all(shortened(grad_stack), 'seq', split_axis=2, concat_axis=1,...  158 us
    reduce_scatter x1, waiting for transfers between devices, per_device(): lax.psum_scatter(jnp.stack(term_list, 1).astype(jnp.bfloat16), 'fsdp', sc...  138 us
    another operation x4, local copies, waits for them, and re-layouts, per_device(): jnp.stack([grad_query, grad_key, grad_value])  130 us
    all_to_all x1, waiting for transfers between devices, per_device(): lax.all_to_all(projected, 'seq', split_axis=1, concat_axis=2, tiled=True)  60.3 us
  transfers between devices with their start and end apart: 17, of which 13 were waited for; matrix products, arithmetic and copies ran while one was open for 34% of the time, Pallas kernels for 0%

commit v1 on v0

v1 whole, which is shorter than its diff:
```python
import functools
import math

import jax
import jax.numpy as jnp
from jax import lax
from jax.experimental import pallas as pl
from jax.experimental.pallas import tpu as pltpu
from jax.sharding import PartitionSpec as P

D = 768
HEADS = 12
HEAD_DIM = 64
TOP = 2
SEQ_LEN = 2048
BUCKETS = 32
DOCS = 8
QB = 256
BAND = QB + 128
EPS = 1e-06
NEG = -1e30
F32 = jnp.float32
BF = jnp.bfloat16
bucket_starts = tuple(range(17)) + tuple(
    int(math.ceil(16 * 8 ** (step_k / 16))) for step_k in range(1, 16)
)
VMEM_MOST = 56 << 20
COST_SHARE = 1
FILLER = 0.02
G_AFTER = 8


def dot(lhs, rhs, lhs_dim, rhs_dim):
    return lax.dot_general(
        lhs, rhs, (((lhs_dim,), (rhs_dim,)), ((), ())), preferred_element_type=F32
    )


def params():
    return pltpu.CompilerParams(vmem_limit_bytes=VMEM_MOST)


def cost(flops, bytes_accessed, transcendentals=0):
    return pl.CostEstimate(
        flops=int(flops * COST_SHARE), bytes_accessed=int(bytes_accessed * COST_SHARE),
        transcendentals=int(transcendentals * COST_SHARE),
    )


def shape(dims, dtype):
    return jax.ShapeDtypeStruct(dims, dtype)


def load_pair(qkv_ref, seg_ref, qt, kt, vt):
    slabs, _, slab = qkv_ref.shape
    for index in range(slabs):
        cols = slice(index * slab, (index + 1) * slab)
        qt[0:64, cols] = qkv_ref[index, 0:64, :] * jnp.asarray(0.125, BF)
        kt[0:64, cols] = qkv_ref[index, 64:128, :]
        vt[0:64, cols] = qkv_ref[index, 128:192, :]
    row = lax.broadcasted_iota(jnp.int32, (16, SEQ_LEN), 0)
    same = seg_ref[...] == row
    kt[64:80, :] = jnp.where(same, 1.0, 0.0).astype(BF)
    qt[64:80, :] = jnp.where(same | (row >= DOCS), 0.0, NEG).astype(BF)


def key_parts(block):
    end = (block + 1) * QB
    near = max(end - BAND, 0)
    return [(near, end)] + ([(0, near)] if near > 0 else [])


def fwd_kernel(qkv_ref, seg_ref, band_ref, o_ref, wide_ref, lse_ref, qt, kt, vt, k_rows):
    slabs, _, slab = qkv_ref.shape
    load_pair(qkv_ref, seg_ref, qt, kt, vt)
    k_rows[...] = kt[...].T
    for block in range(SEQ_LEN // QB):
        start, end = block * QB, (block + 1) * QB
        query = qt[:, start:end]
        scores = []
        for low, high in key_parts(block):
            part = dot(k_rows[low:high], query, 1, 0)
            if high == end:
                part = part + band_ref[0, BAND - (high - low) :, :]
            scores.append((low, high, part))
        peak = functools.reduce(
            jnp.maximum, [jnp.max(part, 0, keepdims=True) for _, _, part in scores]
        )
        total, out = 0.0, 0.0
        for low, high, part in scores:
            terms = jnp.exp(part - peak)
            total = total + jnp.sum(terms, 0, keepdims=True)
            out = out + dot(vt[:, low:high], terms.astype(BF), 1, 0)
        wide_ref[0, :, start:end] = out * (1.0 / total)
        lse_ref[0, :, start:end] = peak + jnp.log(total)
    for index in range(slabs):
        o_ref[index] = wide_ref[0, :, index * slab : (index + 1) * slab].astype(BF)


def bwd_kernel(
    qkv_ref, seg_ref, band_ref, wide_ref, lse_ref, do_ref, d_ref, hist_ref,
    qt, kt, vt, k_rows, v_rows, do_t, dq, dk, dv,
):
    slabs, _, slab = qkv_ref.shape
    load_pair(qkv_ref, seg_ref, qt, kt, vt)
    k_rows[...] = kt[...].T
    v_rows[...] = vt[...].T
    for index in range(slabs):
        do_t[:, index * slab : (index + 1) * slab] = do_ref[index]
    dk[...] = jnp.zeros_like(dk)
    dv[...] = jnp.zeros_like(dv)
    hist_ref[...] = jnp.zeros_like(hist_ref)
    for block in range(SEQ_LEN // QB):
        start, end = block * QB, (block + 1) * QB
        query, grad = qt[:, start:end], do_t[:, start:end]
        delta = jnp.sum(grad.astype(F32) * wide_ref[0, :, start:end], 0, keepdims=True)
        lse = lse_ref[0, :, start:end]
        grad_query = 0.0
        for low, high in key_parts(block):
            part = dot(k_rows[low:high], query, 1, 0)
            off = BAND - (high - low)
            if high == end:
                part = part + band_ref[0, off:, :]
            probs = jnp.exp(part - lse)
            grad_probs = dot(v_rows[low:high], grad, 1, 0)
            grad_scores = (probs * (grad_probs - delta)).astype(BF)
            if high == end:
                hist_ref[0, off:, :] += grad_scores.astype(F32)
            dv[:, low:high] += dot(grad, probs.astype(BF), 1, 1)
            dk[:, low:high] += dot(query[0:64], grad_scores, 1, 1)
            grad_query = grad_query + dot(kt[0:64, low:high], grad_scores, 1, 0)
        dq[:, start:end] = grad_query * 0.125
    for index in range(slabs):
        cols = slice(index * slab, (index + 1) * slab)
        d_ref[index, 0:64, :] = dq[:, cols].astype(BF)
        d_ref[index, 64:128, :] = dk[:, cols].astype(BF)
        d_ref[index, 128:192, :] = dv[:, cols].astype(BF)


def attention_specs(slabs, slab):
    qkv = pl.BlockSpec((slabs, 192, slab), lambda p: (0, p, 0))
    one = pl.BlockSpec((slabs, 64, slab), lambda p: (0, p, 0))
    seg = pl.BlockSpec((1, SEQ_LEN), lambda p: (0, 0))
    band = pl.BlockSpec((1, BAND, QB), lambda p: (p, 0, 0))
    wide = pl.BlockSpec((1, 64, SEQ_LEN), lambda p: (p, 0, 0))
    lse = pl.BlockSpec((1, 1, SEQ_LEN), lambda p: (p, 0, 0))
    return qkv, one, seg, band, wide, lse


def attention_fwd(qkv, seg, bands):
    slabs, rows, slab = qkv.shape
    pairs = rows // 192
    qkv_s, one_s, seg_s, band_s, wide_s, lse_s = attention_specs(slabs, slab)
    return pl.pallas_call(
        fwd_kernel,
        grid=(pairs,),
        out_shape=(
            shape((slabs, 64 * pairs, slab), BF),
            shape((pairs, 64, SEQ_LEN), F32),
            shape((pairs, 1, SEQ_LEN), F32),
        ),
        in_specs=[qkv_s, seg_s, band_s],
        out_specs=(one_s, wide_s, lse_s),
        scratch_shapes=[
            pltpu.VMEM((80, SEQ_LEN), BF),
            pltpu.VMEM((80, SEQ_LEN), BF),
            pltpu.VMEM((64, SEQ_LEN), BF),
            pltpu.VMEM((SEQ_LEN, 80), BF),
        ],
        compiler_params=params(),
        cost_estimate=cost(pairs * 6e9, pairs * 2e6, pairs * 2.4e6),
    )(qkv, seg, bands)


def attention_bwd(qkv, seg, bands, wide, lse, grad):
    slabs, rows, slab = qkv.shape
    pairs = rows // 192
    qkv_s, one_s, seg_s, band_s, wide_s, lse_s = attention_specs(slabs, slab)
    return pl.pallas_call(
        bwd_kernel,
        grid=(pairs,),
        out_shape=(shape(qkv.shape, BF), shape((pairs, BAND, QB), F32)),
        in_specs=[qkv_s, seg_s, band_s, wide_s, lse_s, one_s],
        out_specs=(qkv_s, band_s),
        scratch_shapes=[
            pltpu.VMEM((80, SEQ_LEN), BF),
            pltpu.VMEM((80, SEQ_LEN), BF),
            pltpu.VMEM((64, SEQ_LEN), BF),
            pltpu.VMEM((SEQ_LEN, 80), BF),
            pltpu.VMEM((SEQ_LEN, 64), BF),
            pltpu.VMEM((64, SEQ_LEN), BF),
            pltpu.VMEM((64, SEQ_LEN), F32),
            pltpu.VMEM((64, SEQ_LEN), F32),
            pltpu.VMEM((64, SEQ_LEN), F32),
        ],
        compiler_params=params(),
        cost_estimate=cost(pairs * 10e9, pairs * 3e6, pairs * 2.4e6),
    )(qkv, seg, bands, wide, lse, grad)


def rms(values):
    return lax.rsqrt(jnp.mean(values * values, -1, keepdims=True) + EPS)


def one_step(kernel, outs, operands, flops, scratch=(), smem=0):
    size = sum(math.prod(a.shape) * a.dtype.itemsize for a in (*operands, *outs))
    return pl.pallas_call(
        kernel,
        out_shape=tuple(outs),
        in_specs=[pl.BlockSpec(memory_space=pltpu.SMEM)] * smem
        + [pl.BlockSpec(memory_space=pltpu.VMEM)] * (len(operands) - smem),
        out_specs=tuple([pl.BlockSpec(memory_space=pltpu.VMEM)] * len(outs)),
        scratch_shapes=list(scratch),
        compiler_params=params(),
        cost_estimate=cost(flops * FILLER, size * FILLER),
    )(*operands)


BIAS_ROW, B_ROW, ROUTER_ROW = 2, 5, 8


def pack_kernel(hg_ref, w_ref, o_ref, attn_ref, ffn_ref, bias_ref, b_ref, router_ref, out_ref, lines):
    part = o_ref.shape[0]
    local, experts = b_ref.shape[0], router_ref.shape[1]
    width = (out_ref.shape[1] - D - 128) // 3
    pairs = width // 64
    out_ref[:, 0:D] = o_ref[...]
    lines[...] = jnp.zeros_like(lines)
    lines[0:1, 0:part] = attn_ref[...].astype(F32)
    lines[1:2, 0:part] = ffn_ref[...].astype(F32)
    lines[B_ROW : B_ROW + local, 0:part] = b_ref[...].astype(F32)
    turned = lines[...].T
    column = lax.broadcasted_iota(jnp.int32, (part, 128), 1)
    router = jnp.concatenate([router_ref[...], jnp.zeros((part, 128 - experts), BF)], 1)
    router = pltpu.roll(router.astype(F32), ROUTER_ROW, 1)
    narrow = jnp.where(column < ROUTER_ROW, turned[0:part], router)
    out_ref[:, D : D + 128] = narrow.astype(BF)
    for mine in range(D // width):

        @pl.when(hg_ref[0] == mine)
        def _():
            for which in range(3):
                source, to = which * D + mine * width, D + 128 + which * width
                out_ref[:, to : to + width] = w_ref[:, source : source + width]
            out_ref[0 : bias_ref.shape[0], D + BIAS_ROW : D + BIAS_ROW + pairs] = bias_ref[
                :, mine * pairs : (mine + 1) * pairs
            ]


def unpack_kernel(me_ref, *refs, offsets, pairs):
    part_refs, (w_ref, o_ref, small_ref, band_ref, narrow) = refs[: len(offsets)], refs[len(offsets) :]
    rows = part_refs[0].shape[0]
    for offset, ref in zip(offsets, part_refs):
        at = pl.ds(pl.multiple_of((me_ref[0] ^ offset) * rows, 32), rows)
        o_ref[at, :] = ref[:, 0:D]
        narrow[at, :] = ref[:, D : D + 128].astype(F32)
        w_ref[at, :] = ref[:, D + 128 :]
    small_ref[...] = narrow[...].T
    row = lax.broadcasted_iota(jnp.int32, (BAND, QB), 0)
    col = lax.broadcasted_iota(jnp.int32, (BAND, QB), 1)
    distance = col + (BAND - QB) - row
    per_owner = BUCKETS * rows // D
    for pair in range(pairs):
        source = BIAS_ROW + pair

        def entry(index_b):
            lane = index_b // per_owner * rows + index_b % per_owner
            return small_ref[source : source + 1, lane : lane + 1]

        last = entry(BUCKETS - 1)
        table = jnp.where(distance < 0, NEG, entry(0) - last)
        for index_b in range(1, BUCKETS):
            table = jnp.where(distance >= bucket_starts[index_b], entry(index_b) - last, table)
        band_ref[pair] = table


def project_kernel(me_ref, small_ref, w_ref, *refs, offsets):
    tok_refs, (qkv_ref, first_ref) = refs[:-2], refs[-2:]
    pairs = w_ref.shape[1] // 192
    for offset, ref in zip(offsets, tok_refs):
        at = me_ref[0] ^ offset
        x = ref[...].astype(F32)
        first = (x * rms(x) * small_ref[0:1, :]).astype(BF)
        first_ref[at] = first
        result = dot(w_ref[...], first, 0, 1).astype(BF)
        for pair in range(pairs):
            for which in range(3):
                to, source = pair * 192 + which * 64, (which * pairs + pair) * 64
                qkv_ref[at, to : to + 64, :] = result[source : source + 64, :]


def route_kernel(
    col_ref, row_ref, base_col_ref, base_row_ref, g_ref, sc_ref, sr_ref, other_ref, *gd_refs,
    experts, capacity,
):
    count = col_ref.shape[0]
    each = gd_refs[0].shape[0]
    slots = each * len(gd_refs)
    r0, r1 = col_ref[:, 0:1], col_ref[:, 1:2]
    expert = lax.broadcasted_iota(jnp.int32, (count, experts), 1)
    is0, is1 = expert == r0, expert == r1
    hits = jnp.where(is0 | is1, 1.0, 0.0).astype(BF)
    row_i = lax.broadcasted_iota(jnp.int32, (count, count), 0)
    col_i = lax.broadcasted_iota(jnp.int32, (count, count), 1)
    earlier = jnp.where(col_i < row_i, 1.0, 0.0).astype(BF)
    ranks = dot(earlier, hits, 1, 0)
    for k, own in ((0, is0), (1, is1)):
        rank = jnp.sum(jnp.where(own, ranks, 0.0), 1, keepdims=True).astype(jnp.int32)
        sc_ref[:, k : k + 1] = jnp.where(rank < capacity, base_col_ref[:, k : k + 1] + rank, -1)
    expert = lax.broadcasted_iota(jnp.int32, (experts, count), 0)
    is0, is1 = expert == row_ref[0:1, :], expert == row_ref[1:2, :]
    hits = jnp.where(is0 | is1, 1.0, 0.0).astype(BF)
    later = jnp.where(row_i < col_i, 1.0, 0.0).astype(BF)
    ranks = dot(hits, later, 1, 0)
    slot_rows = []
    for k, own in ((0, is0), (1, is1)):
        rank = jnp.sum(jnp.where(own, ranks, 0.0), 0, keepdims=True).astype(jnp.int32)
        slot_rows.append(jnp.where(rank < capacity, base_row_ref[k : k + 1, :] + rank, -1))
        sr_ref[k : k + 1, :] = slot_rows[k]
    slot = lax.broadcasted_iota(jnp.int32, (slots, count), 0)
    at0 = jnp.where(slot == slot_rows[0], 1.0, 0.0).astype(BF)
    at1 = jnp.where(slot == slot_rows[1], 1.0, 0.0).astype(BF)
    both = at0 + at1
    for index, ref in enumerate(gd_refs):
        ref[...] = dot(both[index * each : (index + 1) * each], g_ref[...], 1, 0).astype(BF)
    r0 = jnp.broadcast_to(row_ref[0:1, :], (8, count)).astype(F32).astype(BF)
    r1 = jnp.broadcast_to(row_ref[1:2, :], (8, count)).astype(F32).astype(BF)
    other_ref[...] = dot(r1, at0, 1, 1) + dot(r0, at1, 1, 1)


def middle_kernel(
    tok_ref, small_ref, w_ref, col_ref, slot_ref, chunk_ref, mid_ref, gate_ref, *disp_refs, experts
):
    groups, slab, _ = tok_ref.shape
    per_group = chunk_ref.shape[0] // groups
    each = disp_refs[0].shape[0]
    count, slots = groups * slab, each * len(disp_refs)
    for group in range(groups):
        att = chunk_ref[group * per_group : (group + 1) * per_group].reshape(D, slab)
        mid_ref[group * slab : (group + 1) * slab, :] = tok_ref[group].astype(F32) + dot(
            att, w_ref[...], 0, 0
        )
    mid = mid_ref[...]
    second = (mid * rms(mid) * small_ref[1:2, :]).astype(BF)
    logits = dot(second, small_ref[ROUTER_ROW : ROUTER_ROW + experts].astype(BF), 1, 1)
    expert = lax.broadcasted_iota(jnp.int32, logits.shape, 1)
    c0 = jnp.sum(jnp.where(expert == col_ref[:, 0:1], logits, 0.0), 1, keepdims=True)
    c1 = jnp.sum(jnp.where(expert == col_ref[:, 1:2], logits, 0.0), 1, keepdims=True)
    top = jnp.maximum(c0, c1)
    e0, e1 = jnp.exp(c0 - top), jnp.exp(c1 - top)
    gate_ref[:, 0:1] = e0 / (e0 + e1)
    gate_ref[:, 1:2] = e1 / (e0 + e1)
    slot = lax.broadcasted_iota(jnp.int32, (slots, count), 0)
    at = jnp.where((slot == slot_ref[0:1, :]) | (slot == slot_ref[1:2, :]), 1.0, 0.0).astype(BF)
    for index, ref in enumerate(disp_refs):
        ref[...] = dot(at[index * each : (index + 1) * each], second, 1, 0).astype(BF)


def split_rows(me_ref, source_ref, keep_ref, send_ref):
    half, rows, _ = keep_ref.shape
    for index in range(2 * half):
        start = pl.multiple_of((me_ref[0] ^ index) * rows, 32)
        ref = send_ref if index % 2 else keep_ref
        ref[index // 2] = source_ref[pl.ds(start, rows), :].astype(BF)


def return_kernel(
    dgate_ref, slot_ref, col_ref, gate_ref, mid_ref, g_ref, small_ref, w_ref, att_ref,
    *refs, local, experts,
):
    dd_refs, refs = refs[:local], refs[local:]
    gb_refs, refs = refs[:local], refs[local:]
    dmid_ref, datt_ref, mixed_ref, narrow, total = refs
    count = mid_ref.shape[0]
    each = dd_refs[0].shape[0]
    slots = each * local
    slabs, rows, slab = att_ref.shape
    groups = count // slab
    per_group = slabs // groups
    slot = lax.broadcasted_iota(jnp.int32, (count, slots), 1)
    own = [slot == slot_ref[:, k : k + 1] for k in range(TOP)]
    at = jnp.where(own[0] | own[1], 1.0, 0.0).astype(BF)
    dsecond = 0.0
    for index, ref in enumerate(dd_refs):
        dsecond = dsecond + dot(at[:, index * each : (index + 1) * each], ref[...], 1, 0)
    dgate = [jnp.sum(jnp.where(o, dgate_ref[...], 0.0), 1, keepdims=True) for o in own]
    gate = [gate_ref[:, k : k + 1] for k in range(TOP)]
    both = gate[0] * dgate[0] + gate[1] * dgate[1]
    expert = lax.broadcasted_iota(jnp.int32, (count, experts), 1)
    dlogits = jnp.zeros((count, experts), F32)
    for k in range(TOP):
        dlogits = jnp.where(expert == col_ref[:, k : k + 1], gate[k] * (dgate[k] - both), dlogits)
    dlogits = dlogits.astype(BF)
    mid = mid_ref[...]
    r = rms(mid)
    n = mid * r
    gain = small_ref[1:2, :]
    second = (n * gain).astype(BF)
    dsecond = dsecond + dot(dlogits, small_ref[ROUTER_ROW : ROUTER_ROW + experts].astype(BF), 1, 0)
    u = dsecond * gain
    dmid = g_ref[...].astype(F32) + r * (u - n * jnp.mean(u * n, -1, keepdims=True))
    dmid_ref[...] = dmid
    dproj = dmid.astype(BF)
    for group in range(groups):
        part = dproj[group * slab : (group + 1) * slab]
        datt = dot(w_ref[...], part, 1, 1).astype(BF)
        for index in range(per_group):
            datt_ref[group * per_group + index] = datt[index * rows : (index + 1) * rows]
        att = att_ref[group * per_group : (group + 1) * per_group].reshape(D, slab)
        term = dot(att, part, 1, 0)
        if group == 0:
            total[...] = term
        else:
            total[...] += term
    narrow[...] = jnp.zeros_like(narrow)
    narrow[0:1, :] = jnp.sum(dsecond * n, 0, keepdims=True)
    for index, ref in enumerate(gb_refs):
        narrow[1 + index : 2 + index, :] = ref[...]
    narrow[ROUTER_ROW : ROUTER_ROW + experts, :] = dot(dlogits, second, 0, 0)
    mixed_ref[:, 0:D] = total[...].astype(BF)
    mixed_ref[:, D : D + 128] = narrow[...].T.astype(BF)
    mixed_ref[:, D + 128 :] = jnp.zeros((D, 128), BF)


def qkv_grad_kernel(
    me_ref, first_ref, d_ref, band_ref, mixed_ref, keep_ref, send_ref, acc, total
):
    slabs, rows, _ = d_ref.shape
    pairs = rows // 192
    half, part, _ = keep_ref.shape
    value = 0.0
    for index in range(slabs):
        value = value + dot(d_ref[index], first_ref[index], 1, 0)
    for pair in range(pairs):
        for which in range(3):
            to, source = (which * pairs + pair) * 64, pair * 192 + which * 64
            acc[to : to + 64, :] = value[source : source + 64, :]
    total[:, rows : rows + 64] = jnp.zeros((D, 64), F32)
    total[:, rows + 64 :] = mixed_ref[...].astype(F32)
    total[:, 0:rows] = acc[...].T
    row = lax.broadcasted_iota(jnp.int32, (BAND, QB), 0)
    col = lax.broadcasted_iota(jnp.int32, (BAND, QB), 1)
    near = col + (BAND - QB) - row < 128
    bucket_at = lax.broadcasted_iota(jnp.int32, (BUCKETS, 128), 0)
    lane = lax.broadcasted_iota(jnp.int32, (BUCKETS, 128), 1)
    bucket = jnp.zeros_like(lane)
    for index_b in range(1, BUCKETS):
        bucket = jnp.where(lane >= bucket_starts[index_b], index_b, bucket)
    mask = (bucket == bucket_at) & (bucket_at < BUCKETS - 1)
    flip_row = lax.broadcasted_iota(jnp.int32, (BAND, BAND), 0)
    flip_col = lax.broadcasted_iota(jnp.int32, (BAND, BAND), 1)
    flip = jnp.where(flip_row + flip_col == BAND - 1, 1.0, 0.0).astype(BF)
    sub = lax.broadcasted_iota(jnp.int32, (BUCKETS, 1), 0)
    per_owner = BUCKETS // (2 * half)
    for pair in range(pairs):
        values = jnp.where(near, band_ref[pair], 0.0)
        high = values.astype(BF)
        values = dot(flip, high, 1, 0) + dot(flip, (values - high.astype(F32)).astype(BF), 1, 0)
        values = pltpu.roll(values, 1, 1, stride=1, stride_axis=0)
        line = jnp.sum(values, 0, keepdims=True)[:, 0:128]
        sums = jnp.sum(jnp.where(mask, line, 0.0), 1, keepdims=True)
        sums = jnp.where(sub == BUCKETS - 1, -jnp.sum(sums, 0, keepdims=True), sums)
        for owner in range(2 * half):
            total[owner * part : owner * part + per_owner, rows + pair : rows + pair + 1] = sums[
                owner * per_owner : (owner + 1) * per_owner
            ]
    split_rows(me_ref, total, keep_ref, send_ref)


def last_kernel(tok_ref, small_ref, w_ref, dmid_ref, d_ref, gtok_ref, full):
    groups, slab, _ = tok_ref.shape
    slabs, rows, _ = d_ref.shape
    per_dest = rows // 192
    per_group = slabs // groups
    for group in range(groups):
        for which in range(3):
            for head in range(HEADS):
                dest = group * per_group + head // per_dest
                row = (head % per_dest) * 192 + which * 64
                to = which * D + head * 64
                full[to : to + 64, :] = d_ref[dest, row : row + 64, :]
        x = tok_ref[group].astype(F32)
        r = rms(x)
        n = x * r
        u = dot(w_ref[...], full[...], 1, 0).T * small_ref[0:1, :]
        gtok_ref[group] = dmid_ref[group * slab : (group + 1) * slab, :] + r * (
            u - n * jnp.mean(u * n, -1, keepdims=True)
        )


def finish_kernel(mine_ref, w_ref, gain_ref, *refs, pairs, experts):
    block_refs, refs = refs[:-8], refs[-8:]
    gw_ref, gnorm_ref, gbias_ref, gwo_ref, gffn_ref, grouter_ref, mixed, square = refs
    rows = gw_ref.shape[0]
    width = pairs * 64
    buckets = gbias_ref.shape[0]
    per_group = len(block_refs)
    quarter = mixed.shape[1] // per_group
    for mine in range(per_group):

        @pl.when(mine_ref[0] == mine)
        def _():
            for offset, ref in enumerate(block_refs):
                hg = mine ^ offset
                for which in range(3):
                    to = which * D + hg * width
                    gw_ref[:, to : to + width] = ref[:, which * width : (which + 1) * width].astype(F32)
                gbias_ref[:, hg * pairs : (hg + 1) * pairs] = ref[
                    0:buckets, 3 * width : 3 * width + pairs
                ].astype(F32)
                mixed[:, hg * quarter : (hg + 1) * quarter] = ref[:, 3 * width + 64 :].astype(F32)

    gnorm = jnp.sum(gw_ref[...] * w_ref[...].astype(F32), 1, keepdims=True)
    gwo_ref[...] = mixed[:, 0:D]
    square[...] = jnp.zeros_like(square)
    square[0:rows, :] = mixed[:, D : D + 128]
    square[0:rows, 1:2] = gnorm
    lines = square[...].T[:, 0:rows]
    gffn_ref[...] = lines[0:1]
    gnorm_ref[...] = lines[1:2] / gain_ref[...].astype(F32)
    grouter_ref[...] = lines[ROUTER_ROW : ROUTER_ROW + experts]


def output_kernel(mid_ref, slot_ref, gate_ref, *refs):
    back_refs, out_ref = refs[:-1], refs[-1]
    count = mid_ref.shape[0]
    each = back_refs[0].shape[0]
    slot = lax.broadcasted_iota(jnp.int32, (count, each), 1)
    total = mid_ref[...]
    for k in range(TOP):
        rows = 0.0
        for index, ref in enumerate(back_refs):
            at = jnp.where(slot + index * each == slot_ref[:, k : k + 1], 1.0, 0.0).astype(BF)
            rows = rows + dot(at, ref[...], 1, 0)
        total = total + gate_ref[:, k : k + 1] * rows
    out_ref[...] = total.astype(BF)


def expert_kernel(
    own_ref, rows_ref, g_ref, other_ref, small_ref, w_ref,
    out_ref, dd_ref, dgate_ref, dslot_ref, act_ref, dpre_ref, gb_ref, acc_out, acc_dd,
    *, index, local, experts,
):
    step, steps = pl.program_id(0), pl.num_programs(0)
    rows = rows_ref[...]

    @pl.when(step == 0)
    def _():
        own = own_ref[0] * local + index
        logits = dot(rows, small_ref[8 : 8 + experts].astype(BF), 1, 1)
        expert = lax.broadcasted_iota(jnp.int32, logits.shape, 1)
        mine = jnp.sum(jnp.where(expert == own, logits, 0.0), 1, keepdims=True)
        theirs = jnp.sum(jnp.where(expert == other_ref[...], logits, 0.0), 1, keepdims=True)
        gate = 1.0 / (1.0 + jnp.exp(theirs - mine))
        dslot = (g_ref[...].astype(F32) * gate).astype(BF)
        dslot_ref[...] = dslot
        gb_ref[...] = jnp.sum(dslot.astype(F32), 0, keepdims=True)
        acc_out[...] = jnp.zeros_like(acc_out)
        acc_dd[...] = jnp.zeros_like(acc_dd)

    w_in, w_out = w_ref[0, 0], w_ref[0, 1]
    pre = dot(rows, w_in, 1, 1)
    dact = dot(dslot_ref[...], w_out, 1, 1)
    root = math.sqrt(2 / math.pi)
    square = pre * pre
    tanh = jnp.tanh(pre * (root + (root * 0.044715) * square))
    half = 0.5 + 0.5 * tanh
    act = (pre * half).astype(BF)
    slope = half + (pre * (half - half * half)) * (2 * root + (6 * root * 0.044715) * square)
    act_ref[0] = act
    dpre = (dact * slope).astype(BF)
    dpre_ref[0] = dpre
    acc_dd[...] += dot(dpre, w_in, 1, 0)
    acc_out[...] += dot(act, w_out, 1, 0)

    @pl.when(step == steps - 1)
    def _():
        out = (acc_out[...] + small_ref[B_ROW + index : B_ROW + index + 1, :]).astype(BF)
        out_ref[...] = out
        dd_ref[...] = acc_dd[...].astype(BF)
        dgate = jnp.sum(out.astype(F32) * g_ref[...].astype(F32), 1, keepdims=True)
        dgate = jnp.broadcast_to(dgate, (dgate.shape[0], 128)).T
        high = dgate.astype(BF).astype(F32)
        middle = (dgate - high).astype(BF).astype(F32)
        line = lax.broadcasted_iota(jnp.int32, dgate.shape, 0)
        parts = jnp.where(line == 0, high, jnp.where(line == 1, middle, dgate - high - middle))
        dgate_ref[...] = parts[0:16].astype(BF)


def expert_pass(index, local, experts, own, rows, g_rows, other, small, weights):
    count, _ = rows.shape
    parts, _, units, _ = weights.shape
    token_s = pl.BlockSpec((count, D), lambda f: (0, 0))
    narrow_s = pl.BlockSpec((count, 1), lambda f: (0, 0))
    line_s = pl.BlockSpec((16, count), lambda f: (0, 0))
    weight_s = pl.BlockSpec((1, 2, units, D), lambda f: (f, 0, 0, 0))
    bias_s = pl.BlockSpec((1, D), lambda f: (0, 0))
    hidden_s = pl.BlockSpec((1, count, units), lambda f: (f, 0, 0))
    hidden = shape((parts, count, units), BF)
    return pl.pallas_call(
        functools.partial(expert_kernel, index=index, local=local, experts=experts),
        grid=(parts,),
        out_shape=(
            shape(rows.shape, BF),
            shape(rows.shape, BF),
            shape((16, count), BF),
            shape(rows.shape, BF),
            hidden,
            hidden,
            shape((1, D), F32),
        ),
        in_specs=[
            pl.BlockSpec(memory_space=pltpu.SMEM),
            token_s,
            token_s,
            narrow_s,
            pl.BlockSpec(small.shape, lambda f: (0, 0)),
            weight_s,
        ],
        out_specs=(token_s, token_s, line_s, token_s, hidden_s, hidden_s, bias_s),
        scratch_shapes=[pltpu.VMEM((count, D), F32), pltpu.VMEM((count, D), F32)],
        compiler_params=params(),
        cost_estimate=cost(10 * count * D * units * parts, 6 * D * units * parts * 2),
    )(own, rows, g_rows, other, small, weights)


def weight_kernel(*refs, local, parts):
    out_ref = refs[-1]
    for index in range(local):
        rows_ref, dslot_ref, act_ref, dpre_ref = refs[4 * index : 4 * index + 4]

        @pl.when(pl.program_id(0) // parts == index)
        def _():
            out_ref[0, 0, 0] = dot(dpre_ref[0], rows_ref[...], 0, 0).astype(BF)
            out_ref[0, 0, 1] = dot(act_ref[0], dslot_ref[...], 0, 0).astype(BF)


def weight_grads(operands):
    local = len(operands)
    count = operands[0][0].shape[0]
    parts, _, units = operands[0][2].shape
    token_s = pl.BlockSpec((count, D), lambda i: (0, 0))

    def hidden_s(index):
        return pl.BlockSpec(
            (1, count, units),
            lambda i: (jnp.clip(i - index * parts, 0, parts - 1), 0, 0),
        )

    return pl.pallas_call(
        functools.partial(weight_kernel, local=local, parts=parts),
        grid=(local * parts,),
        out_shape=shape((parts, local, 2, units, D), BF),
        in_specs=[
            spec
            for index in range(local)
            for spec in (token_s, token_s, hidden_s(index), hidden_s(index))
        ],
        out_specs=pl.BlockSpec(
            (1, 1, 2, units, D), lambda i: (lax.rem(i, parts), i // parts, 0, 0, 0)
        ),
        compiler_params=params(),
        cost_estimate=cost(1e6, 1e6),
    )(*[a for of in operands for a in of])


def spread_kernel(*refs):
    x_refs, (in_ref, out_ref) = refs[:-2], refs[-2:]
    for index, ref in enumerate(x_refs):
        in_ref[:, index, :] = ref[0].astype(F32)
        out_ref[:, index, :] = ref[1].astype(F32)


def spread_grads(owned):
    local = len(owned)
    units = owned[0].shape[1]
    rows = min(128, units)
    out_s = pl.BlockSpec((rows, local, D), lambda i: (i, 0, 0))
    return pl.pallas_call(
        spread_kernel,
        grid=(units // rows,),
        in_specs=[pl.BlockSpec((2, rows, D), lambda i: (0, i, 0))] * local,
        out_specs=(out_s, out_s),
        out_shape=[shape((units, local, D), F32)] * 2,
        compiler_params=params(),
        cost_estimate=cost(1e6, 1e6),
    )(*owned)


def after(array, *others):
    return lax.optimization_barrier((array, *others))[0]


def swap(array, axis, bit):
    size = lax.axis_size(axis)
    return lax.ppermute(array, axis, [(i, i ^ bit) for i in range(size)])


def gather_parts(array):
    bit = lax.axis_size("fsdp") // 2
    held = [(0, array)]
    while bit:
        held = held + [(off ^ bit, swap(a, "fsdp", bit)) for off, a in held]
        bit //= 2
    return [off for off, _ in held], [a for _, a in held]


def exchange(array):
    return lax.all_to_all(array, "seq", split_axis=0, concat_axis=0, tiled=True)


def add(*arrays):
    return sum(a.astype(F32) for a in arrays).astype(BF)


def fold_first(keep, send):
    send = swap(send, "fsdp", 1)
    return [add(keep[index], send[index]) for index in range(keep.shape[0])]


def fold_rest(held):
    bit = 2
    while len(held) > 1:
        held = [add(a, swap(b, "fsdp", bit)) for a, b in zip(held[::2], held[1::2])]
        bit *= 2
    return held[0]


def slabs_of_sequence(tokens, me, per_group, packed):
    slabs = lax.axis_size("seq")
    groups = tokens.shape[0]
    if (slabs, groups, per_group) == (8, 2, 4):
        mine = lax.dynamic_index_in_dim(tokens, me // 4, 0, keepdims=False)
        theirs = lax.dynamic_index_in_dim(tokens, 1 - me // 4, 0, keepdims=False)
        far = swap(theirs, "seq", 4)
        found = {0: mine, 4: far}
        for bit in (1, 2, 3):
            found[bit] = swap(mine, "seq", bit)
        far = after(far, packed, *[found[bit] for bit in (1, 2, 3)])
        for bit in (1, 2, 3):
            found[4 ^ bit] = swap(far, "seq", bit)
        return me, list(found), list(found.values())
    rows = exchange(jnp.repeat(tokens, per_group, axis=0))
    return me * 0, list(range(slabs)), [rows[index] for index in range(slabs)]


def scalar(value):
    return value.reshape(1).astype(jnp.int32)


def per_device(
    tokens, cotangent, segments, routes, norm_attn, w_qkv, w_o, rel_bias, norm_ffn, router, w_in,
    w_out, b_out,
):
    slabs, owners = lax.axis_size("seq"), lax.axis_size("fsdp")
    me = lax.axis_index("seq")
    me_f = scalar(lax.axis_index("fsdp"))
    groups, slab = tokens.shape[0], tokens.shape[1]
    count = groups * slab
    experts, local = router.shape[1], b_out.shape[0]
    capacity = max(2, 9 * count * TOP // (8 * experts))
    slots = experts * capacity
    each = slots // local
    pairs = groups * HEADS // slabs
    per_group = HEADS // pairs
    width = pairs * HEAD_DIM
    part = D // owners
    head_group = lax.rem(me, per_group)
    grad_flat = cotangent.reshape(count, D)

    pack = one_step(
        pack_kernel,
        [shape((part, D + 128 + 3 * width), BF)],
        (
            scalar(head_group), w_qkv, w_o, norm_attn[None], norm_ffn[None], rel_bias, b_out,
            router,
        ),
        1e9,
        scratch=[pltpu.VMEM((128, 256), F32)],
        smem=1,
    )[0]
    offsets, packed = gather_parts(pack)
    base, slab_offsets, slab_rows = slabs_of_sequence(tokens, me, per_group, packed[1])
    w_columns, w_o_full, small, bands = one_step(
        functools.partial(unpack_kernel, offsets=offsets, pairs=pairs),
        [
            shape((D, 3 * width), BF),
            shape((D, D), BF),
            shape((128, D), F32),
            shape((pairs, BAND, QB), F32),
        ],
        (me_f, *packed),
        3e9,
        scratch=[pltpu.VMEM((D, 128), F32)],
        smem=1,
    )

    route_col = after(routes, slab_rows[5], small).reshape(count, TOP)
    base_col = (route_col % local) * each + (route_col // local) * capacity
    slot_col, slot_row, other, *g_slots = one_step(
        functools.partial(route_kernel, experts=experts, capacity=capacity),
        [
            shape((count, TOP), jnp.int32),
            shape((TOP, count), jnp.int32),
            shape((8, slots), F32),
        ]
        + [shape((each, D), BF)] * local,
        (route_col, route_col.T, base_col, base_col.T, grad_flat),
        5e9,
    )

    def cross(array):
        return exchange(array.reshape(slabs, capacity, D)).reshape(each, D)

    ids = other[0].reshape(local, slabs, capacity).swapaxes(0, 1).reshape(slabs, 1, -1)
    ids = jnp.pad(ids.astype(BF), ((0, 0), (0, 7), (0, D - local * capacity)))
    g_all = jnp.concatenate([a.reshape(slabs, capacity, D) for a in g_slots] + [ids], 1)
    g_all = exchange(after(g_all, *slab_rows[:G_AFTER]))

    def g_part(index):
        return g_all[:, index * capacity : (index + 1) * capacity].reshape(each, D)

    def other_part(index):
        at = slice(index * capacity, (index + 1) * capacity)
        return g_all[:, local * capacity, at].reshape(each, 1).astype(jnp.int32)

    seg = lax.dynamic_slice_in_dim(segments, me // per_group, 1, 0)
    qkv, first = one_step(
        functools.partial(project_kernel, offsets=slab_offsets),
        [shape((slabs, 3 * width, slab), BF), shape((slabs, slab, D), BF)],
        (scalar(base), small, w_columns, *slab_rows),
        4 * SEQ_LEN * D * 3 * width,
        smem=1,
    )
    out, wide, lse = attention_fwd(qkv, seg, bands)
    out, g_all = lax.optimization_barrier((out, g_all))
    att = exchange(out)
    mid, gates, *disp = one_step(
        functools.partial(middle_kernel, experts=experts),
        [shape((count, D), F32), shape((count, TOP), F32)] + [shape((each, D), BF)] * local,
        (tokens, small, w_o_full, route_col, slot_row, att),
        4 * count * D * (D + slots),
    )

    relaid = jnp.stack([w_in, w_out]).transpose(2, 0, 1, 3)
    weights = [
        lax.all_gather(relaid[index], "fsdp", axis=0, tiled=False) for index in range(local)
    ]
    w_qkv_late, _ = lax.optimization_barrier((w_qkv, att))
    w_qkv_full = lax.all_gather(w_qkv_late, "fsdp", axis=0, tiled=True)
    rows, passes = [], []
    for index in range(local):
        rows.append(cross(after(disp[index], *rows)))
    big = []
    for index in range(local):
        if index:
            arrived = rows[index]
            rows[index] = after(arrived, passes[-1][1], big[-1])
            big[-1] = after(big[-1], arrived)
        passes.append(
            expert_pass(
                index, local, experts, scalar(me), rows[index], g_part(index),
                other_part(index), small, weights[index],
            )
        )
        act, dpre = passes[-1][4], passes[-1][5]
        act = after(act, passes[-1][1])
        big.append(weight_grads([(rows[index], passes[-1][3], act, dpre)]))
    results, dd, dgate, _, _, _, grad_b = map(list, zip(*passes))
    parts = jnp.stack([a[0:3] for a in dgate], 1).reshape(3 * local, slabs, capacity)
    parts = parts.swapaxes(0, 1).reshape(slabs, 1, -1)
    parts = jnp.pad(parts, ((0, 0), (0, 7), (0, D - parts.shape[2])))
    dd_back = [cross(a) for a in dd[:-1]]
    last = jnp.concatenate([dd[-1].reshape(slabs, capacity, D), parts], 1)
    last = exchange(after(last, *dd_back))
    dd_back.append(last[:, :capacity].reshape(each, D))
    parts = last[:, capacity, : 3 * local * capacity].astype(F32)
    dgate_back = jnp.sum(parts.reshape(slabs, 3, local, capacity), 1)
    dgate_back = dgate_back.swapaxes(0, 1).reshape(1, slots)
    *dd_back, big[-1] = lax.optimization_barrier((*dd_back, big[-1]))
    big = [lax.psum_scatter(a, "fsdp", scatter_dimension=0, tiled=True)[0, 0] for a in big]
    grad_w_in, grad_w_out = spread_grads(big)

    dmid, grad_att, mixed = one_step(
        functools.partial(return_kernel, local=local, experts=experts),
        [shape((count, D), F32), shape((slabs, width, slab), BF), shape((D, D + 256), BF)],
        (
            dgate_back, slot_col, route_col, gates, mid, grad_flat, small, w_o_full, att,
            *dd_back, *grad_b,
        ),
        4 * count * D * (slots + 2 * D),
        scratch=[pltpu.VMEM((128, D), F32), pltpu.VMEM((D, D), F32)],
    )
    results_back = [cross(after(results[0], *dd_back))]
    grad_heads = exchange(after(grad_att, *results_back))
    for a in results[1:]:
        results_back.append(cross(after(a, grad_heads, *results_back)))
    d_qkv, band_sums = attention_bwd(qkv, seg, bands, wide, lse, grad_heads)
    d_back = exchange(after(d_qkv, *results_back))
    output = one_step(
        output_kernel,
        (shape((count, D), BF),),
        (after(mid, d_qkv), slot_col, gates, *results_back),
        4 * count * D * slots,
    )[0].reshape(groups, slab, D)

    keep, send = one_step(
        qkv_grad_kernel,
        [shape((owners // 2, part, 3 * width + D + 320), BF)] * 2,
        (me_f, first, d_qkv, band_sums, mixed),
        4 * SEQ_LEN * D * 3 * width,
        scratch=[pltpu.VMEM((3 * width, D), F32), pltpu.VMEM((D, 3 * width + D + 320), F32)],
        smem=1,
    )
    grad_tokens = one_step(
        last_kernel,
        [shape((groups, slab, D), F32)],
        (tokens, small, w_qkv_full, dmid, after(d_back, keep, output)),
        4 * count * D * 3 * D,
        scratch=[pltpu.VMEM((3 * D, slab), BF)],
    )[0]
    folded = fold_rest(fold_first(keep, send))
    grad_qkv, mixed = folded[:, : 3 * width + 64], folded[:, 3 * width + 64 :]
    grad_b_own = mixed[:, D + 1 : D + 1 + local].astype(F32).T
    quarter = (D + 256) // per_group

    def quarter_of(offset):
        return lax.dynamic_slice_in_dim(mixed, (head_group ^ offset) * quarter, quarter, 1)

    mixed = add(quarter_of(0), *[swap(quarter_of(k), "seq", k) for k in range(1, per_group)])
    block = after(jnp.concatenate([grad_qkv, mixed], 1), grad_tokens)
    bit = per_group
    while bit < slabs:
        block = add(block, swap(block, "seq", bit))
        bit *= 2
    blocks = [block] + [swap(block, "seq", k) for k in range(1, per_group)]
    blocks[0], grad_w_in, grad_w_out = lax.optimization_barrier((blocks[0], grad_w_in, grad_w_out))
    grad_wqkv, grad_gain_attn, grad_bias, grad_wo, grad_gain_ffn, grad_router = one_step(
        functools.partial(finish_kernel, pairs=pairs, experts=experts),
        [
            shape((part, 3 * D), F32),
            shape((1, part), F32),
            shape(rel_bias.shape, F32),
            shape((part, D), F32),
            shape((1, part), F32),
            shape((experts, part), F32),
        ],
        (scalar(head_group), w_qkv, norm_attn[None], *blocks),
        1e9,
        scratch=[pltpu.VMEM((part, D + 256), F32), pltpu.VMEM((256, 128), F32)],
        smem=1,
    )
    return (
        output,
        grad_tokens,
        grad_gain_attn[0],
        grad_wqkv,
        grad_wo,
        grad_bias,
        grad_gain_ffn[0],
        grad_router.T,
        grad_w_in,
        grad_w_out,
        grad_b_own,
    )


def solution(mesh):
    in_specs = (
        P("fsdp", "seq", None),
        P("fsdp", "seq", None),
        P("fsdp", None),
        P("fsdp", "seq", None),
        P("fsdp"),
        P("fsdp", None),
        P("fsdp", None),
        P("fsdp", None),
        P("fsdp"),
        P("fsdp", None),
        P("fsdp", "seq", None),
        P("fsdp", "seq", None),
        P("seq", "fsdp"),
    )
    out_specs = (
        P("fsdp", "seq", None),
        P("fsdp", "seq", None),
        P("fsdp"),
        P("fsdp", None),
        P("fsdp", None),
        P("fsdp", None),
        P("fsdp"),
        P("fsdp", None),
        P("fsdp", "seq", None),
        P("fsdp", "seq", None),
        P("seq", "fsdp"),
    )
    return jax.shard_map(
        per_device, mesh=mesh, in_specs=in_specs, out_specs=out_specs, check_vma=False
    )
```

time: 2780 us -> 467 us (0.17)
  local copies, waits for them, and re-layouts: 852 us -> 26.9 us
  other arithmetic: 625 us -> 9.98 us
  matrix products: 412 us -> 0 us
  waiting for transfers between devices: 439 us -> 133 us
  loops' own time: 260 us -> 0 us
  Pallas kernels: 0 us -> 167 us
  blocking collectives: 118 us -> 46.8 us
  starting transfers between devices: 30 us -> 62.4 us
    add x46 -> x1, other arithmetic: 471 us -> 0.25 us  [per_device(): base_col = route_col % local * each + route_col // local * capacity]
    dot_general x105 -> x0, matrix products: 412 us -> none  [the longest x24 214 us: masked_scores(): jnp.einsum('qd,kd->qk', query_rows, key_all[:key_width], preferred_elemen...]
    unnamed x217 -> x56, local copies, waits for them, and re-layouts: 400 us -> 9.19 us
    another operation x2 -> x0, loops' own time: 260 us -> none  [the longest x1 259 us: per_device(): lax.map(pair_backward, (per_head[0], per_head[1], per_head[2], seg_pairs,...]
    all_to_all x7 -> x8, waiting for transfers between devices: 250 us -> 66.7 us  [exchange(): return lax.all_to_all(array, 'seq', split_axis=0, concat_axis=0, tiled=True)]
    all_to_all x8 -> x0, local copies, waits for them, and re-layouts: 167 us -> none  [the longest x1 158 us: per_device(): lax.all_to_all(shortened(grad_stack), 'seq', split_axis=2, concat_axis=1,...]
    pallas_call x0 -> x17, Pallas kernels: none -> 167 us  [the longest x10 57.6 us: one_step(): pl.pallas_call(kernel, out_shape=tuple(outs), in_specs=[pl.BlockSpec(memo...]
    reduce_scatter x3 -> x2, waiting for transfers between devices: 139 us -> 0.01 us  [per_device(): lax.psum_scatter(a, 'fsdp', scatter_dimension=0, tiled=True)[0, 0]]
  transfers between devices with their start and end apart: 17 -> 32, of which waited for: 13 -> 16; matrix products, arithmetic and copies ran while one was open for 34% -> 5% of each run, Pallas kernels for 0% -> 36%
where the time goes in v1:
time: 467 us; the launch traced here: 460 us
  Pallas kernels  167 us (36%)
  waiting for transfers between devices  133 us (28%)
  starting transfers between devices  62.4 us (13%)
  blocking collectives  46.8 us (10%)
  local copies, waits for them, and re-layouts  26.9 us (6%)
  between operations  14.6 us (3%)
  other arithmetic  9.98 us (2%)
    all_to_all x8, waiting for transfers between devices, exchange(): return lax.all_to_all(array, 'seq', split_axis=0, concat_axis=0, tiled=True)  66.7 us
    ppermute x19, waiting for transfers between devices, swap(): return lax.ppermute(array, axis, [(i, i ^ bit) for i in range(size)])  65.4 us
    pallas_call x10, Pallas kernels, one_step(): pl.pallas_call(kernel, out_shape=tuple(outs), in_specs=[pl.BlockSpec(memo...  57.6 us
    all_to_all x2, blocking collectives, exchange(): return lax.all_to_all(array, 'seq', split_axis=0, concat_axis=0, tiled=True)  46.8 us
    pallas_call x2, Pallas kernels, expert_pass(): pl.pallas_call(functools.partial(expert_kernel, index=index, local=local,...  38.4 us
    all_to_all x8, starting transfers between devices, exchange(): return lax.all_to_all(array, 'seq', split_axis=0, concat_axis=0, tiled=True)  37.2 us
    ppermute x19, starting transfers between devices, swap(): return lax.ppermute(array, axis, [(i, i ^ bit) for i in range(size)])  24.4 us
    pallas_call x2, Pallas kernels, weight_grads(): pl.pallas_call(functools.partial(weight_kernel, local=local, parts=parts)...  23.8 us
  transfers between devices with their start and end apart: 32, of which 16 were waited for; matrix products, arithmetic and copies ran while one was open for 5% of the time, Pallas kernels for 36%

profile of v1, /device:TPU:0, one launch (start us, length us, event | category | flops | bytes accessed | tf_op | source)
XLA Modules:
  0.0 460.4 jit_solution(17760866434750562375)
XLA Ops:
  7.2 3.0 copy_bitcast_fusion
  10.7 2.5 fusion.16
  15.8 2.4 shard_map.212.refs_0_
  18.2 3.0 collective-permute-start
  21.3 2.7 collective-permute-start.3
  27.4 13.9 %collective-permute-done.3.refs_1_ = bf16[256,768]{1,0:T(8,128)(2,1)S(1)} collective-permute-done((bf16[256,768]{1,0:T(8,128)(2,1)S(1)}, bf16[256,768]{1,0:T(8,128)(2,1)S(1)}, u32[]{:S(2)}, u32[]{:S(2)}) %collective-permute-start.3) | collective-permute-done | bytes 393248 | tf_op jit(solution)/shard_map/ppermute | solution.py:696
  41.3 2.1 collective-permute-done.refs_1_
  44.8 6.3 %collective-permute-done.6.refs_4_ = bf16[256,768]{1,0:T(8,128)(2,1)S(1)} collective-permute-done((bf16[256,768]{1,0:T(8,128)(2,1)S(1)}, bf16[256,768]{1,0:T(8,128)(2,1)S(1)}, u32[]{:S(2)}, u32[]{:S(2)}) %collective-permute-start.6) | collective-permute-done | bytes 393248 | tf_op jit(solution)/shard_map/ppermute | solution.py:696
  56.4 4.6 %shard_map.213 = (bf16[768,576]{1,0:T(8,128)(2,1)}, bf16[768,768]{1,0:T(8,128)(2,1)}, f32[128,768]{1,0:T(8,128)}, f32[3,384,256]{2,1,0:T(8,128)}) custom-call(s32[1]{0:T(128)} %bitcast.me_ref, bf16[192,1472]{1,0:T(8,128)(2,1)} %shard_map.212.refs_0_, bf16[192,1472]{1,0:T(8,128)(2,1)} %copy-done.14, bf16[192,1472]{1,0:T(8,128)(2,1)} %copy-done.15, ...), custom_call_target="tpu_custom_call" | custom-call | flops 60000000 | bytes 117964 | tf_op jit(solution)/shard_map/pallas_call | solution.py:207
  61.0 2.0 collective-permute-done.7.refs_5_
  65.6 4.3 shard_map.214
  70.9 2.8 fusion.2
  73.7 4.7 %all-to-all-start = ((bf16[8,152,768]{2,1,0:T(8,128)(2,1)}), bf16[8,152,768]{2,1,0:T(8,128)(2,1)S(1)}, u32[]{:S(2)}, u32[]{:S(2)}) async-start(bf16[8,152,768]{2,1,0:T(8,128)(2,1)} %fusion.2), calls=%async_computation | async-start | bytes 3735552 | tf_op jit(solution)/shard_map/all_to_all | solution.py:709
  79.6 7.1 %shard_map.215 = (bf16[8,576,256]{2,1,0:T(8,128)(2,1)}, bf16[8,256,768]{2,1,0:T(8,128)(2,1)}) custom-call(s32[1]{0:T(128)} %bitcast.8.me_ref.own_ref, f32[128,768]{1,0:T(8,128)} %get-tuple-element.83.small_ref, bf16[768,576]{1,0:T(8,128)(2,1)} %get-tuple-element.88.w_ref, bf16[256,768]{1,0:T(8,128)(2,1)} %copy-done.11, bf16[256,768]{1,0:T(8,128)(2,1)} %copy-done.17, ...), custom_call_target="tpu_custom_call" | custom-call | flops 72477576 | bytes 198574 | tf_op jit(solution)/shard_map/pallas_call | solution.py:207
  86.7 16.5 %shard_map.216 = (bf16[8,192,256]{2,1,0:T(8,128)(2,1)}, f32[3,64,2048]{2,1,0:T(8,128)}, f32[3,1,2048]{2,1,0:T(1,128)}) custom-call(bf16[8,576,256]{2,1,0:T(8,128)(2,1)} %get-tuple-element.89.qkv_ref, s32[1,2048]{1,0:T(1,128)} %constant_dynamic-slice_fusion.3.seg_ref, f32[3,384,256]{2,1,0:T(8,128)} %get-tuple-element.90.band_ref), custom_call_target="tpu_custom_call" | custom-call | flops 17999998976 | bytes 6000000 | tf_op jit(solution)/shard_map/pallas_call | solution.py:154
  103.2 14.2 %all-to-all-done = bf16[8,152,768]{2,1,0:T(8,128)(2,1)S(1)} async-done(((bf16[8,152,768]{2,1,0:T(8,128)(2,1)}), bf16[8,152,768]{2,1,0:T(8,128)(2,1)S(1)}, u32[]{:S(2)}, u32[]{:S(2)}) %all-to-all-start) | async-done | bytes 1867808 | tf_op jit(solution)/shard_map/all_to_all | solution.py:709
  117.4 23.0 %all_to_all.50.chunk_ref.att_ref = bf16[8,192,256]{2,1,0:T(8,128)(2,1)} all-to-all(bf16[8,192,256]{2,1,0:T(8,128)(2,1)} %get-tuple-element.96), channel_id=1, replica_groups=mesh['seq'=8,'fsdp'=4] {'seq'}, dimensions={0} | all-to-all | bytes 1572864 | tf_op jit(solution)/shard_map/all_to_all | solution.py:709
  140.4 5.1 %shard_map.217 = (f32[512,768]{1,0:T(8,128)}, f32[512,2]{1,0:T(8,128)}, bf16[576,768]{1,0:T(8,128)(2,1)}, bf16[576,768]{1,0:T(8,128)(2,1)}) custom-call(bf16[2,256,768]{2,1,0:T(8,128)(2,1)} %tok_ref.3, f32[128,768]{1,0:T(8,128)} %get-tuple-element.83.small_ref, bf16[768,768]{1,0:T(8,128)(2,1)} %get-tuple-element.84.w_ref, s32[512,2]{1,0:T(8,128)} %bitcast.61, ...), custom_call_target="tpu_custom_call" | custom-call | flops 60397976 | bytes 130007 | tf_op jit(solution)/shard_map/pallas_call | solution.py:207
  145.5 3.6 all-to-all-start.2
  150.0 21.0 %all-to-all-done.2 = bf16[8,72,768]{2,1,0:T(8,128)(2,1)S(1)} async-done(((bf16[8,72,768]{2,1,0:T(8,128)(2,1)}), bf16[8,72,768]{2,1,0:T(8,128)(2,1)S(1)}, u32[]{:S(2)}, u32[]{:S(2)}) %all-to-all-start.2) | async-done | bytes 884768 | tf_op jit(solution)/shard_map/all_to_all | solution.py:709
  171.9 3.5 all-to-all-start.3
  177.0 18.5 %shard_map.218 = (bf16[576,768]{1,0:T(8,128)(2,1)}, bf16[576,768]{1,0:T(8,128)(2,1)}, bf16[16,576]{1,0:T(8,128)(2,1)}, bf16[576,768]{1,0:T(8,128)(2,1)}, bf16[4,...) custom-call(s32[1]{0:T(128)} %bitcast.8.me_ref.own_ref, bf16[576,768]{1,0:T(8,128)(2,1)} %bitcast.69, ...), custom_call_target="tpu_custom_call" | custom-call | flops 13589544960 | bytes 28311552 | tf_op jit(solution)/shard_map/pallas_call | solution.py:600
  195.5 11.9 %shard_map.219 = bf16[4,1,2,768,768]{4,3,2,1,0:T(8,128)(2,1)} custom-call(bf16[576,768]{1,0:T(8,128)(2,1)} %bitcast.70, bf16[576,768]{1,0:T(8,128)(2,1)} %get-tuple-element.105.refs_1_, bf16[4,576,768]{2,1,0:T(8,128)(2,1)} %get-tuple-element.107.refs_2_, bf16[4,576,768]{2,1,0:T(8,128)(2,1)} %get-tuple-element.108.refs_3_), custom_call_target="tpu_custom_call" | custom-call | flops 1000000 | bytes 1000000 | tf_op jit(solution)/shard_map/pallas_call | solution.py:650
  209.2 5.9 %all-to-all-start.4 = ((bf16[8,72,768]{2,1,0:T(8,128)(2,1)}), bf16[8,72,768]{2,1,0:T(8,128)(2,1)S(1)}, u32[]{:S(2)}, u32[]{:S(2)}) async-start(bf16[8,72,768]{2,1,0:T(8,128)(2,1)} %bitcast.25), calls=%async_computation.4 | async-start | bytes 1769472 | tf_op jit(solution)/shard_map/all_to_all | solution.py:709
  215.2 19.9 %shard_map.220 = (bf16[576,768]{1,0:T(8,128)(2,1)}, bf16[576,768]{1,0:T(8,128)(2,1)}, bf16[16,576]{1,0:T(8,128)(2,1)}, bf16[576,768]{1,0:T(8,128)(2,1)}, bf16[4,...) custom-call(s32[1]{0:T(128)} %bitcast.8.me_ref.own_ref, bf16[576,768]{1,0:T(8,128)(2,1)} %bitcast.67, ...), custom_call_target="tpu_custom_call" | custom-call | flops 13589544960 | bytes 28311552 | tf_op jit(solution)/shard_map/pallas_call | solution.py:600
  236.7 2.2 fusion.4
  238.9 5.8 %all-to-all-start.5 = ((bf16[8,80,768]{2,1,0:T(8,128)(2,1)}), bf16[8,80,768]{2,1,0:T(8,128)(2,1)S(1)}, u32[]{:S(2)}, u32[]{:S(2)}) async-start(bf16[8,80,768]{2,1,0:T(8,128)(2,1)} %fusion.4), calls=%async_computation.5 | async-start | bytes 1966080 | tf_op jit(solution)/shard_map/all_to_all | solution.py:709
  244.8 11.9 %shard_map.221 = bf16[4,1,2,768,768]{4,3,2,1,0:T(8,128)(2,1)} custom-call(bf16[576,768]{1,0:T(8,128)(2,1)} %bitcast.68, bf16[576,768]{1,0:T(8,128)(2,1)} %get-tuple-element.116.refs_1_, bf16[4,576,768]{2,1,0:T(8,128)(2,1)} %get-tuple-element.118.refs_2_, bf16[4,576,768]{2,1,0:T(8,128)(2,1)} %get-tuple-element.119.refs_3_), custom_call_target="tpu_custom_call" | custom-call | flops 1000000 | bytes 1000000 | tf_op jit(solution)/shard_map/pallas_call | solution.py:650
  256.6 10.7 %all-to-all-done.5 = bf16[8,80,768]{2,1,0:T(8,128)(2,1)S(1)} async-done(((bf16[8,80,768]{2,1,0:T(8,128)(2,1)}), bf16[8,80,768]{2,1,0:T(8,128)(2,1)S(1)}, u32[]{:S(2)}, u32[]{:S(2)}) %all-to-all-start.5) | async-done | bytes 983072 | tf_op jit(solution)/shard_map/all_to_all | solution.py:709
  268.4 3.8 all-to-all-start.6
  273.0 9.5 %shard_map.222 = (f32[512,768]{1,0:T(8,128)}, bf16[8,192,256]{2,1,0:T(8,128)(2,1)}, bf16[768,1024]{1,0:T(8,128)(2,1)}) custom-call(f32[1,1152]{1,0:T(1,128)} %reshape.175.dgate_ref, s32[512,2]{1,0:T(8,128)} %get-tuple-element.114.slot_ref, s32[512,2]{1,0:T(8,128)} %bitcast.62, f32[512,2]{1,0:T(8,128)} %get-tuple-element.115.gate_ref, ...), custom_call_target="tpu_custom_call" | custom-call | flops 84557168 | bytes 208865 | tf_op jit(solution)/shard_map/pallas_call | solution.py:207
  282.5 11.3 %all-to-all-done.6 = bf16[8,72,768]{2,1,0:T(8,128)(2,1)S(1)} async-done(((bf16[8,72,768]{2,1,0:T(8,128)(2,1)}), bf16[8,72,768]{2,1,0:T(8,128)(2,1)S(1)}, u32[]{:S(2)}, u32[]{:S(2)}) %all-to-all-start.6) | async-done | bytes 884768 | tf_op jit(solution)/shard_map/all_to_all | solution.py:709
  293.8 23.8 %all_to_all.51.do_ref = bf16[8,192,256]{2,1,0:T(8,128)(2,1)} all-to-all(bf16[8,192,256]{2,1,0:T(8,128)(2,1)} %get-tuple-element.127), channel_id=1, replica_groups=mesh['seq'=8,'fsdp'=4] {'seq'}, dimensions={0} | all-to-all | bytes 1572864 | tf_op jit(solution)/shard_map/all_to_all | solution.py:709
  317.7 3.6 all-to-all-start.8
  321.3 23.3 %shard_map.223 = (bf16[8,576,256]{2,1,0:T(8,128)(2,1)}, f32[3,384,256]{2,1,0:T(8,128)}) custom-call(bf16[8,576,256]{2,1,0:T(8,128)(2,1)} %get-tuple-element.89.qkv_ref, s32[1,2048]{1,0:T(1,128)} %constant_dynamic-slice_fusion.3.seg_ref, f32[3,384,256]{2,1,0:T(8,128)} %get-tuple-element.90.band_ref, f32[3,64,2048]{2,1,0:T(8,128)} %get-tuple-element.98.wide_ref, ...), custom_call_target="tpu_custom_call" | custom-call | flops 30000001024 | bytes 9000000 | tf_op jit(solution)/shard_map/pallas_call | solution.py:179
  345.4 6.3 %all-to-all-start.9 = ((bf16[8,576,256]{2,1,0:T(8,128)(2,1)}), bf16[8,576,256]{2,1,0:T(8,128)(2,1)S(1)}, u32[]{:S(2)}, u32[]{:S(2)}) async-start(bf16[8,576,256]{2,1,0:T(8,128)(2,1)} %get-tuple-element.134.d_ref), calls=%async_computation.9 | async-start | bytes 4718592 | tf_op jit(solution)/shard_map/all_to_all | solution.py:709
  351.7 8.3 %shard_map.225 = (bf16[2,192,1664]{2,1,0:T(8,128)(2,1)}, bf16[2,192,1664]{2,1,0:T(8,128)(2,1)}) custom-call(s32[1]{0:T(128)} %bitcast.me_ref, bf16[8,256,768]{2,1,0:T(8,128)(2,1)} %get-tuple-element.135.first_ref, bf16[8,576,256]{2,1,0:T(8,128)(2,1)} %get-tuple-element.134.d_ref, f32[3,384,256]{2,1,0:T(8,128)} %get-tuple-element.136.band_ref, ...), custom_call_target="tpu_custom_call" | custom-call | flops 72477576 | bytes 216268 | tf_op jit(solution)/shard_map/pallas_call | solution.py:207
  360.0 3.2 collective-permute-done.10
  366.8 15.3 %collective-permute-done.11 = bf16[192,1664]{1,0:T(8,128)(2,1)} collective-permute-done((bf16[192,1664]{1,0:T(8,128)(2,1)S(1)}, bf16[192,1664]{1,0:T(8,128)(2,1)}, u32[]{:S(2)}, u32[]{:S(2)}) %collective-permute-start.11) | collective-permute-done | bytes 639008 | tf_op jit(solution)/shard_map/ppermute | solution.py:696
  384.6 2.1 collective-permute-start.12
  388.2 5.6 %shard_map.224 = bf16[512,768]{1,0:T(8,128)(2,1)} custom-call(f32[512,768]{1,0:T(8,128)} %get-tuple-element.129.mid_ref, s32[512,2]{1,0:T(8,128)} %get-tuple-element.114.slot_ref, f32[512,2]{1,0:T(8,128)} %get-tuple-element.115.gate_ref, bf16[576,768]{1,0:T(8,128)(2,1)} %bitcast.65, bf16[576,768]{1,0:T(8,128)(2,1)} %bitcast.66), custom_call_target="tpu_custom_call" | custom-call | flops 36238784 | bytes 82739 | tf_op jit(solution)/shard_map/pallas_call | solution.py:207
  395.0 9.4 %all-to-all-done.9.d_ref = bf16[8,576,256]{2,1,0:T(8,128)(2,1)S(1)} async-done(((bf16[8,576,256]{2,1,0:T(8,128)(2,1)}), bf16[8,576,256]{2,1,0:T(8,128)(2,1)S(1)}, u32[]{:S(2)}, u32[]{:S(2)}) %all-to-all-start.9) | async-done | bytes 2359328 | tf_op jit(solution)/shard_map/all_to_all | solution.py:709
  405.9 7.4 %shard_map.226 = f32[2,256,768]{2,1,0:T(8,128)} custom-call(bf16[2,256,768]{2,1,0:T(8,128)(2,1)} %tok_ref.3, f32[128,768]{1,0:T(8,128)} %get-tuple-element.83.small_ref, bf16[768,2304]{1,0:T(8,128)(2,1)} %all-gather.8.cloned.1.call-done.w_ref, f32[512,768]{1,0:T(8,128)} %get-tuple-element.133.dmid_ref, bf16[8,576,256]{2,1,0:T(8,128)(2,1)} %copy-done.3), custom_call_target="tpu_custom_call" | custom-call | flops 72477576 | bytes 204472 | tf_op jit(solution)/shard_map/pallas_call | solution.py:207
  413.2 3.4 collective-permute-start.15
  416.6 14.0 %collective-permute-done.15 = bf16[192,896]{1,0:T(8,128)(2,1)S(1)} collective-permute-done((bf16[192,896]{1,0:T(8,128)(2,1)S(1)}, bf16[192,896]{1,0:T(8,128)(2,1)S(1)}, u32[]{:S(2)}, u32[]{:S(2)}) %collective-permute-start.15) | collective-permute-done | bytes 344096 | tf_op jit(solution)/shard_map/ppermute | solution.py:696
  435.1 7.4 %shard_map.227 = (f32[768,2,768]{2,1,0:T(2,128)}, f32[768,2,768]{2,1,0:T(2,128)}) custom-call(bf16[2,768,768]{2,1,0:T(8,128)(2,1)} %bitcast.74, bf16[2,768,768]{2,1,0:T(8,128)(2,1)} %bitcast.75), custom_call_target="tpu_custom_call" | custom-call | flops 1000000 | bytes 1000000 | tf_op jit(solution)/shard_map/pallas_call | solution.py:679
  443.6 5.8 %collective-permute-done.18.refs_3_ = bf16[192,896]{1,0:T(8,128)(2,1)S(1)} collective-permute-done((bf16[192,896]{1,0:T(8,128)(2,1)S(1)}, bf16[192,896]{1,0:T(8,128)(2,1)S(1)}, u32[]{:S(2)}, u32[]{:S(2)}) %collective-permute-start.18) | collective-permute-done | bytes 344096 | tf_op jit(solution)/shard_map/ppermute | solution.py:696
  450.1 3.2 shard_map.228
  (139 shorter events, 44.0 us)
Async XLA Ops:
  7.2 71.8 %copy-start = (s32[2,2048]{1,0:T(2,128)S(1)}, s32[2,2048]{1,0:T(2,128)}, u32[]{:S(2)}) copy-start(s32[2,2048]{1,0:T(2,128)} %param.15) | copy-start | bytes 49156
  7.2 169.8 %all-gather.4.cloned.1.call-start = ((), (), s32[]{:S(2)}) async-start(), calls=%async_computation.12 | async-start | bytes 11796480 | tf_op jit(solution)/shard_map/all_gather | solution.py:847
  13.2 2.1 copy-start.26
  13.2 8.0 %copy-start.4 = (bf16[2,256,768]{2,1,0:T(8,128)(2,1)S(1)}, bf16[2,256,768]{2,1,0:T(8,128)(2,1)}, u32[]{:S(2)}) copy-start(bf16[2,256,768]{2,1,0:T(8,128)(2,1)} %tok_ref.3) | copy-start | bytes 2359300
  13.2 202.0 %all-gather.6.cloned.1.call-start = ((), (), s32[]{:S(2)}) async-start(), calls=%async_computation.13 | async-start | bytes 11796480 | tf_op jit(solution)/shard_map/all_gather | solution.py:847
  18.2 25.2 %collective-permute-start = (bf16[192,1472]{1,0:T(8,128)(2,1)}, bf16[192,1472]{1,0:T(8,128)(2,1)S(1)}, u32[]{:S(2)}, u32[]{:S(2)}) collective-permute-start(bf16[192,1472]{1,0:T(8,128)(2,1)} %shard_map.212.refs_0_), channel_id=1, source_target_pairs={{0,2},{1,3},{2,0},{3,1},{4,6},{5,7},{6,4},{7,5},{8,10},{9,11},{10,... | collective-permute-start | bytes 1695752 | tf_op jit(solution)/shard_map/ppermute | solution.py:696
  21.3 48.7 %copy-start.11 = (bf16[256,768]{1,0:T(8,128)(2,1)}, bf16[256,768]{1,0:T(8,128)(2,1)S(1)}, u32[]{:S(2)}) copy-start(bf16[256,768]{1,0:T(8,128)(2,1)S(1)} %get-tuple-element.205.refs_0_) | copy-start | bytes 1179652
  21.3 20.1 %collective-permute-start.3 = (bf16[256,768]{1,0:T(8,128)(2,1)S(1)}, bf16[256,768]{1,0:T(8,128)(2,1)S(1)}, u32[]{:S(2)}, u32[]{:S(2)}) collective-permute-start(bf16[256,768]{1,0:T(8,128)(2,1)S(1)} %get-tuple-element.206), channel_id=1, source_target_pairs={{0,16},{4,20},{8,24},{12,28},{16,0},{20,4},{24,8},{28,12},{1,17},{... | collective-permute-start | bytes 1179656 | tf_op jit(solution)/shard_map/ppermute | solution.py:696
  23.9 19.5 %collective-permute-start.4 = (bf16[256,768]{1,0:T(8,128)(2,1)S(1)}, bf16[256,768]{1,0:T(8,128)(2,1)S(1)}, u32[]{:S(2)}, u32[]{:S(2)}) collective-permute-start(bf16[256,768]{1,0:T(8,128)(2,1)S(1)} %get-tuple-element.205.refs_0_), channel_id=1, source_target_pairs={{0,4},{4,0},{8,12},{12,8},{16,20},{20,16},{24,28},{28,24},{1,5},{5... | collective-permute-start | bytes 1179656 | tf_op jit(solution)/shard_map/ppermute | solution.py:696
  25.4 19.4 %collective-permute-start.5 = (bf16[256,768]{1,0:T(8,128)(2,1)S(1)}, bf16[256,768]{1,0:T(8,128)(2,1)S(1)}, u32[]{:S(2)}, u32[]{:S(2)}) collective-permute-start(bf16[256,768]{1,0:T(8,128)(2,1)S(1)} %get-tuple-element.205.refs_0_), channel_id=1, source_target_pairs={{0,8},{4,12},{8,0},{12,4},{16,24},{20,28},{24,16},{28,20},{1,9},{5... | collective-permute-start | bytes 1179656 | tf_op jit(solution)/shard_map/ppermute | solution.py:696
  27.0 24.1 %collective-permute-start.6 = (bf16[256,768]{1,0:T(8,128)(2,1)S(1)}, bf16[256,768]{1,0:T(8,128)(2,1)S(1)}, u32[]{:S(2)}, u32[]{:S(2)}) collective-permute-start(bf16[256,768]{1,0:T(8,128)(2,1)S(1)} %get-tuple-element.205.refs_0_), channel_id=1, source_target_pairs={{0,12},{4,8},{8,4},{12,0},{16,28},{20,24},{24,20},{28,16},{1,13},{... | collective-permute-start | bytes 1179656 | tf_op jit(solution)/shard_map/ppermute | solution.py:696
  41.3 38.3 %copy-start.17 = (bf16[256,768]{1,0:T(8,128)(2,1)}, bf16[256,768]{1,0:T(8,128)(2,1)S(1)}, u32[]{:S(2)}) copy-start(bf16[256,768]{1,0:T(8,128)(2,1)S(1)} %collective-permute-done.3.refs_1_) | copy-start | bytes 1179652
  41.3 14.0 %collective-permute-start.1 = (bf16[192,1472]{1,0:T(8,128)(2,1)}, bf16[192,1472]{1,0:T(8,128)(2,1)S(1)}, u32[]{:S(2)}, u32[]{:S(2)}) collective-permute-start(bf16[192,1472]{1,0:T(8,128)(2,1)} %shard_map.212.refs_0_), channel_id=1, source_target_pairs={{0,1},{1,0},{2,3},{3,2},{4,5},{5,4},{6,7},{7,6},{8,9},{9,8},{10,11... | collective-permute-start | bytes 1695752 | tf_op jit(solution)/shard_map/ppermute | solution.py:696
  43.4 12.0 %copy-start.14 = (bf16[192,1472]{1,0:T(8,128)(2,1)}, bf16[192,1472]{1,0:T(8,128)(2,1)S(1)}, u32[]{:S(2)}) copy-start(bf16[192,1472]{1,0:T(8,128)(2,1)S(1)} %collective-permute-done.refs_1_) | copy-start | bytes 1695748
  43.4 12.0 %collective-permute-start.2 = (bf16[192,1472]{1,0:T(8,128)(2,1)S(1)}, bf16[192,1472]{1,0:T(8,128)(2,1)S(1)}, u32[]{:S(2)}, u32[]{:S(2)}) collective-permute-start(bf16[192,1472]{1,0:T(8,128)(2,1)S(1)} %collective-permute-done.refs_1_), channel_id=1, source_target_pairs={{0,1},{1,0},{2,3},{3,2},{4,5},{5,4},{6,7},{7,6},{8,9},{9,8},{10,11... | collective-permute-start | bytes 1695752 | tf_op jit(solution)/shard_map/ppermute | solution.py:696
  43.4 36.2 %copy-start.18 = (bf16[256,768]{1,0:T(8,128)(2,1)}, bf16[256,768]{1,0:T(8,128)(2,1)S(1)}, u32[]{:S(2)}) copy-start(bf16[256,768]{1,0:T(8,128)(2,1)S(1)} %collective-permute-done.4.refs_2_) | copy-start | bytes 1179652
  44.8 34.8 %copy-start.19 = (bf16[256,768]{1,0:T(8,128)(2,1)}, bf16[256,768]{1,0:T(8,128)(2,1)S(1)}, u32[]{:S(2)}) copy-start(bf16[256,768]{1,0:T(8,128)(2,1)S(1)} %collective-permute-done.5.refs_3_) | copy-start | bytes 1179652
  51.9 11.2 %collective-permute-start.7 = (bf16[256,768]{1,0:T(8,128)(2,1)S(1)}, bf16[256,768]{1,0:T(8,128)(2,1)}, u32[]{:S(2)}, u32[]{:S(2)}) collective-permute-start(bf16[256,768]{1,0:T(8,128)(2,1)S(1)} %collective-permute-done.3.refs_1_), channel_id=1, source_target_pairs={{0,4},{4,0},{8,12},{12,8},{16,20},{20,16},{24,28},{28,24},{1,5},{5... | collective-permute-start | bytes 1179656 | tf_op jit(solution)/shard_map/ppermute | solution.py:696
  53.4 20.3 %collective-permute-start.8 = (bf16[256,768]{1,0:T(8,128)(2,1)S(1)}, bf16[256,768]{1,0:T(8,128)(2,1)}, u32[]{:S(2)}, u32[]{:S(2)}) collective-permute-start(bf16[256,768]{1,0:T(8,128)(2,1)S(1)} %collective-permute-done.3.refs_1_), channel_id=1, source_target_pairs={{0,8},{4,12},{8,0},{12,4},{16,24},{20,28},{24,16},{28,20},{1,9},{5... | collective-permute-start | bytes 1179656 | tf_op jit(solution)/shard_map/ppermute | solution.py:696
  53.6 20.1 %collective-permute-start.9 = (bf16[256,768]{1,0:T(8,128)(2,1)S(1)}, bf16[256,768]{1,0:T(8,128)(2,1)}, u32[]{:S(2)}, u32[]{:S(2)}) collective-permute-start(bf16[256,768]{1,0:T(8,128)(2,1)S(1)} %collective-permute-done.3.refs_1_), channel_id=1, source_target_pairs={{0,12},{4,8},{8,4},{12,0},{16,28},{20,24},{24,20},{28,16},{1,13},{... | collective-permute-start | bytes 1179656 | tf_op jit(solution)/shard_map/ppermute | solution.py:696
  63.9 1.7 copy-start.2
  64.2 1.4 copy-start.10
  73.7 43.7 %all-to-all-start = ((bf16[8,152,768]{2,1,0:T(8,128)(2,1)}), bf16[8,152,768]{2,1,0:T(8,128)(2,1)S(1)}, u32[]{:S(2)}, u32[]{:S(2)}) async-start(bf16[8,152,768]{2,1,0:T(8,128)(2,1)} %fusion.2), calls=%async_computation | async-start | bytes 3735552 | tf_op jit(solution)/shard_map/all_to_all | solution.py:709
  78.5 326.0 %all-gather.8.cloned.1.call-start = ((), (), s32[]{:S(2)}) async-start(), calls=%async_computation.14 | async-start | bytes 4423680 | tf_op jit(solution)/shard_map/all_gather | solution.py:850
  145.5 25.5 %all-to-all-start.2 = ((bf16[8,72,768]{2,1,0:T(8,128)(2,1)}), bf16[8,72,768]{2,1,0:T(8,128)(2,1)S(1)}, u32[]{:S(2)}, u32[]{:S(2)}) async-start(bf16[8,72,768]{2,1,0:T(8,128)(2,1)} %bitcast.82), calls=%async_computation.2 | async-start | bytes 1769472 | tf_op jit(solution)/shard_map/all_to_all | solution.py:709
  171.9 35.5 %all-to-all-start.3 = ((bf16[8,72,768]{2,1,0:T(8,128)(2,1)}), bf16[8,72,768]{2,1,0:T(8,128)(2,1)S(1)}, u32[]{:S(2)}, u32[]{:S(2)}) async-start(bf16[8,72,768]{2,1,0:T(8,128)(2,1)} %bitcast.81), calls=%async_computation.3 | async-start | bytes 1769472 | tf_op jit(solution)/shard_map/all_to_all | solution.py:709
  175.5 259.6 %reduce-scatter.3.cloned.1.call-start = ((), (), s32[]{:S(2)}) async-start(), calls=%async_computation.15 | async-start | bytes 11796480 | tf_op jit(solution)/shard_map/reduce_scatter | solution.py:881
  209.2 29.7 %all-to-all-start.4 = ((bf16[8,72,768]{2,1,0:T(8,128)(2,1)}), bf16[8,72,768]{2,1,0:T(8,128)(2,1)S(1)}, u32[]{:S(2)}, u32[]{:S(2)}) async-start(bf16[8,72,768]{2,1,0:T(8,128)(2,1)} %bitcast.25), calls=%async_computation.4 | async-start | bytes 1769472 | tf_op jit(solution)/shard_map/all_to_all | solution.py:709
  238.9 17.7 %copy-start.5 = (bf16[8,72,768]{2,1,0:T(8,128)(2,1)}, bf16[8,72,768]{2,1,0:T(8,128)(2,1)S(1)}, u32[]{:S(2)}) copy-start(bf16[8,72,768]{2,1,0:T(8,128)(2,1)S(1)} %all-to-all-done.4) | copy-start | bytes 2654212
  238.9 28.5 %all-to-all-start.5 = ((bf16[8,80,768]{2,1,0:T(8,128)(2,1)}), bf16[8,80,768]{2,1,0:T(8,128)(2,1)S(1)}, u32[]{:S(2)}, u32[]{:S(2)}) async-start(bf16[8,80,768]{2,1,0:T(8,128)(2,1)} %fusion.4), calls=%async_computation.5 | async-start | bytes 1966080 | tf_op jit(solution)/shard_map/all_to_all | solution.py:709
  244.7 190.4 %reduce-scatter.5.cloned.1.call-start = ((), (), s32[]{:S(2)}) async-start(), calls=%async_computation.16 | async-start | bytes 11796480 | tf_op jit(solution)/shard_map/reduce_scatter | solution.py:881
  268.4 25.5 %all-to-all-start.6 = ((bf16[8,72,768]{2,1,0:T(8,128)(2,1)}), bf16[8,72,768]{2,1,0:T(8,128)(2,1)S(1)}, u32[]{:S(2)}, u32[]{:S(2)}) async-start(bf16[8,72,768]{2,1,0:T(8,128)(2,1)} %bitcast.29), calls=%async_computation.6 | async-start | bytes 1769472 | tf_op jit(solution)/shard_map/all_to_all | solution.py:709
  293.8 50.7 %copy-start.6 = (bf16[8,72,768]{2,1,0:T(8,128)(2,1)}, bf16[8,72,768]{2,1,0:T(8,128)(2,1)S(1)}, u32[]{:S(2)}) copy-start(bf16[8,72,768]{2,1,0:T(8,128)(2,1)S(1)} %all-to-all-done.6) | copy-start | bytes 2654212
  317.7 26.8 %all-to-all-start.8 = ((bf16[8,72,768]{2,1,0:T(8,128)(2,1)}), bf16[8,72,768]{2,1,0:T(8,128)(2,1)S(1)}, u32[]{:S(2)}, u32[]{:S(2)}) async-start(bf16[8,72,768]{2,1,0:T(8,128)(2,1)} %bitcast.31), calls=%async_computation.8 | async-start | bytes 1769472 | tf_op jit(solution)/shard_map/all_to_all | solution.py:709
  345.4 59.0 %all-to-all-start.9 = ((bf16[8,576,256]{2,1,0:T(8,128)(2,1)}), bf16[8,576,256]{2,1,0:T(8,128)(2,1)S(1)}, u32[]{:S(2)}, u32[]{:S(2)}) async-start(bf16[8,576,256]{2,1,0:T(8,128)(2,1)} %get-tuple-element.134.d_ref), calls=%async_computation.9 | async-start | bytes 4718592 | tf_op jit(solution)/shard_map/all_to_all | solution.py:709
  360.0 3.2 collective-permute-start.10
  365.6 16.6 %collective-permute-start.11 = (bf16[192,1664]{1,0:T(8,128)(2,1)S(1)}, bf16[192,1664]{1,0:T(8,128)(2,1)}, u32[]{:S(2)}, u32[]{:S(2)}) collective-permute-start(bf16[192,1664]{1,0:T(8,128)(2,1)S(1)} %fusion.6), channel_id=1, source_target_pairs={{0,2},{1,3},{2,0},{3,1},{4,6},{5,7},{6,4},{7,5},{8,10},{9,11},{10,... | collective-permute-start | bytes 1916936 | tf_op jit(solution)/shard_map/ppermute | solution.py:696
  384.6 9.2 %collective-permute-start.12 = (bf16[192,256]{1,0:T(8,128)(2,1)}, bf16[192,256]{1,0:T(8,128)(2,1)S(1)}, u32[]{:S(2)}, u32[]{:S(2)}) collective-permute-start(bf16[192,256]{1,0:T(8,128)(2,1)} %get-tuple-element.207), channel_id=1, source_target_pairs={{0,4},{4,0},{8,12},{12,8},{16,20},{20,16},{24,28},{28,24},{1,5},{5... | collective-permute-start | bytes 294920 | tf_op jit(solution)/shard_map/ppermute | solution.py:696
  386.7 7.1 %collective-permute-start.13 = (bf16[192,256]{1,0:T(8,128)(2,1)}, bf16[192,256]{1,0:T(8,128)(2,1)}, u32[]{:S(2)}, u32[]{:S(2)}) collective-permute-start(bf16[192,256]{1,0:T(8,128)(2,1)} %get-tuple-element.209), channel_id=1, source_target_pairs={{0,8},{4,12},{8,0},{12,4},{16,24},{20,28},{24,16},{28,20},{1,9},{5... | collective-permute-start | bytes 294920 | tf_op jit(solution)/shard_map/ppermute | solution.py:696
  388.2 5.8 %collective-permute-start.14 = (bf16[192,256]{1,0:T(8,128)(2,1)}, bf16[192,256]{1,0:T(8,128)(2,1)}, u32[]{:S(2)}, u32[]{:S(2)}) collective-permute-start(bf16[192,256]{1,0:T(8,128)(2,1)} %get-tuple-element.208), channel_id=1, source_target_pairs={{0,12},{4,8},{8,4},{12,0},{16,28},{20,24},{24,20},{28,16},{1,13},{... | collective-permute-start | bytes 294920 | tf_op jit(solution)/shard_map/ppermute | solution.py:696
  413.2 17.5 %collective-permute-start.15 = (bf16[192,896]{1,0:T(8,128)(2,1)S(1)}, bf16[192,896]{1,0:T(8,128)(2,1)S(1)}, u32[]{:S(2)}, u32[]{:S(2)}) collective-permute-start(bf16[192,896]{1,0:T(8,128)(2,1)S(1)} %pad_maximum_fusion), channel_id=1, source_target_pairs={{0,16},{4,20},{8,24},{12,28},{16,0},{20,4},{24,8},{28,12},{1,17},{... | collective-permute-start | bytes 1032200 | tf_op jit(solution)/shard_map/ppermute | solution.py:696
  430.8 11.7 %copy-start.12 = (bf16[192,896]{1,0:T(8,128)(2,1)}, bf16[192,896]{1,0:T(8,128)(2,1)S(1)}, u32[]{:S(2)}) copy-start(bf16[192,896]{1,0:T(8,128)(2,1)S(1)} %add_convert_fusion.2.refs_0_) | copy-start | bytes 1032196
  430.8 11.7 %collective-permute-start.16 = (bf16[192,896]{1,0:T(8,128)(2,1)S(1)}, bf16[192,896]{1,0:T(8,128)(2,1)S(1)}, u32[]{:S(2)}, u32[]{:S(2)}) collective-permute-start(bf16[192,896]{1,0:T(8,128)(2,1)S(1)} %add_convert_fusion.2.refs_0_), channel_id=1, source_target_pairs={{0,4},{4,0},{8,12},{12,8},{16,20},{20,16},{24,28},{28,24},{1,5},{5... | collective-permute-start | bytes 1032200 | tf_op jit(solution)/shard_map/ppermute | solution.py:696
  432.6 11.0 %collective-permute-start.17 = (bf16[192,896]{1,0:T(8,128)(2,1)S(1)}, bf16[192,896]{1,0:T(8,128)(2,1)S(1)}, u32[]{:S(2)}, u32[]{:S(2)}) collective-permute-start(bf16[192,896]{1,0:T(8,128)(2,1)S(1)} %add_convert_fusion.2.refs_0_), channel_id=1, source_target_pairs={{0,8},{4,12},{8,0},{12,4},{16,24},{20,28},{24,16},{28,20},{1,9},{5... | collective-permute-start | bytes 1032200 | tf_op jit(solution)/shard_map/ppermute | solution.py:696
  432.6 16.8 %collective-permute-start.18 = (bf16[192,896]{1,0:T(8,128)(2,1)S(1)}, bf16[192,896]{1,0:T(8,128)(2,1)S(1)}, u32[]{:S(2)}, u32[]{:S(2)}) collective-permute-start(bf16[192,896]{1,0:T(8,128)(2,1)S(1)} %add_convert_fusion.2.refs_0_), channel_id=1, source_target_pairs={{0,12},{4,8},{8,4},{12,0},{16,28},{20,24},{24,20},{28,16},{1,13},{... | collective-permute-start | bytes 1032200 | tf_op jit(solution)/shard_map/ppermute | solution.py:696
  435.1 18.3 %copy-start.1 = (s32[2,2048]{1,0:T(2,128)S(1)}, s32[2,2048]{1,0:T(2,128)}, u32[]{:S(2)}) copy-start(s32[2,2048]{1,0:T(2,128)} %param.15) | copy-start | bytes 49156
  442.5 6.9 %copy-start.21 = (bf16[192,896]{1,0:T(8,128)(2,1)}, bf16[192,896]{1,0:T(8,128)(2,1)S(1)}, u32[]{:S(2)}) copy-start(bf16[192,896]{1,0:T(8,128)(2,1)S(1)} %collective-permute-done.16.refs_1_) | copy-start | bytes 1032196
  443.6 5.8 %copy-start.22 = (bf16[192,896]{1,0:T(8,128)(2,1)}, bf16[192,896]{1,0:T(8,128)(2,1)S(1)}, u32[]{:S(2)}) copy-start(bf16[192,896]{1,0:T(8,128)(2,1)S(1)} %collective-permute-done.17.refs_2_) | copy-start | bytes 1032196
  (11 other events, 10.8 us)
Sparse Core Ops, SparseCore 0:
  13.3 73.7 all-gather.3
  88.7 65.7 all-gather.5
  156.1 30.7 all-gather.7
  207.6 78.8 reduce-scatter.2
  288.9 78.4 reduce-scatter.4

commit v2 on v1

--- a/solution.py
+++ b/solution.py
@@ -365,12 +365,12 @@
 
 
 def return_kernel(
-    dgate_ref, slot_ref, col_ref, gate_ref, mid_ref, g_ref, small_ref, w_ref, att_ref,
+    me_ref, dgate_ref, slot_ref, col_ref, gate_ref, mid_ref, g_ref, small_ref, w_ref, att_ref,
     *refs, local, experts,
 ):
     dd_refs, refs = refs[:local], refs[local:]
     gb_refs, refs = refs[:local], refs[local:]
-    dmid_ref, datt_ref, mixed_ref, narrow, total = refs
+    dmid_ref, datt_ref, keep_ref, send_ref, narrow, total = refs
     count = mid_ref.shape[0]
     each = dd_refs[0].shape[0]
     slots = each * local
@@ -409,21 +409,21 @@
         att = att_ref[group * per_group : (group + 1) * per_group].reshape(D, slab)
         term = dot(att, part, 1, 0)
         if group == 0:
-            total[...] = term
+            total[:, 0:D] = term
         else:
-            total[...] += term
+            total[:, 0:D] += term
     narrow[...] = jnp.zeros_like(narrow)
     narrow[0:1, :] = jnp.sum(dsecond * n, 0, keepdims=True)
     for index, ref in enumerate(gb_refs):
         narrow[1 + index : 2 + index, :] = ref[...]
     narrow[ROUTER_ROW : ROUTER_ROW + experts, :] = dot(dlogits, second, 0, 0)
-    mixed_ref[:, 0:D] = total[...].astype(BF)
-    mixed_ref[:, D : D + 128] = narrow[...].T.astype(BF)
-    mixed_ref[:, D + 128 :] = jnp.zeros((D, 128), BF)
+    total[:, D : D + 128] = narrow[...].T
+    total[:, D + 128 :] = jnp.zeros((D, 128), F32)
+    split_rows(me_ref, total, keep_ref, send_ref)
 
 
 def qkv_grad_kernel(
-    me_ref, first_ref, d_ref, band_ref, mixed_ref, keep_ref, send_ref, acc, total
+    me_ref, first_ref, d_ref, band_ref, keep_ref, send_ref, acc, total
 ):
     slabs, rows, _ = d_ref.shape
     pairs = rows // 192
@@ -436,7 +436,6 @@
             to, source = (which * pairs + pair) * 64, pair * 192 + which * 64
             acc[to : to + 64, :] = value[source : source + 64, :]
     total[:, rows : rows + 64] = jnp.zeros((D, 64), F32)
-    total[:, rows + 64 :] = mixed_ref[...].astype(F32)
     total[:, 0:rows] = acc[...].T
     row = lax.broadcasted_iota(jnp.int32, (BAND, QB), 0)
     col = lax.broadcasted_iota(jnp.int32, (BAND, QB), 1)
@@ -664,27 +663,25 @@
     )(*[a for of in operands for a in of])
 
 
-def spread_kernel(*refs):
-    x_refs, (in_ref, out_ref) = refs[:-2], refs[-2:]
-    for index, ref in enumerate(x_refs):
-        in_ref[:, index, :] = ref[0].astype(F32)
-        out_ref[:, index, :] = ref[1].astype(F32)
+def spread_kernel(x_ref, in_ref, out_ref):
+    for index in range(x_ref.shape[0]):
+        in_ref[:, index, :] = x_ref[index, 0].astype(F32)
+        out_ref[:, index, :] = x_ref[index, 1].astype(F32)
 
 
 def spread_grads(owned):
-    local = len(owned)
-    units = owned[0].shape[1]
+    local, _, units, _ = owned.shape
     rows = min(128, units)
     out_s = pl.BlockSpec((rows, local, D), lambda i: (i, 0, 0))
     return pl.pallas_call(
         spread_kernel,
         grid=(units // rows,),
-        in_specs=[pl.BlockSpec((2, rows, D), lambda i: (0, i, 0))] * local,
+        in_specs=[pl.BlockSpec((local, 2, rows, D), lambda i: (0, 0, i, 0))],
         out_specs=(out_s, out_s),
         out_shape=[shape((units, local, D), F32)] * 2,
         compiler_params=params(),
         cost_estimate=cost(1e6, 1e6),
-    )(*owned)
+    )(owned)
 
 
 def after(array, *others):
@@ -851,22 +848,16 @@
     rows, passes = [], []
     for index in range(local):
         rows.append(cross(after(disp[index], *rows)))
-    big = []
     for index in range(local):
         if index:
-            arrived = rows[index]
-            rows[index] = after(arrived, passes[-1][1], big[-1])
-            big[-1] = after(big[-1], arrived)
+            rows[index] = after(rows[index], passes[-1][1])
         passes.append(
             expert_pass(
                 index, local, experts, scalar(me), rows[index], g_part(index),
                 other_part(index), small, weights[index],
             )
         )
-        act, dpre = passes[-1][4], passes[-1][5]
-        act = after(act, passes[-1][1])
-        big.append(weight_grads([(rows[index], passes[-1][3], act, dpre)]))
-    results, dd, dgate, _, _, _, grad_b = map(list, zip(*passes))
+    results, dd, dgate, dslot, act, dpre, grad_b = map(list, zip(*passes))
     parts = jnp.stack([a[0:3] for a in dgate], 1).reshape(3 * local, slabs, capacity)
     parts = parts.swapaxes(0, 1).reshape(slabs, 1, -1)
     parts = jnp.pad(parts, ((0, 0), (0, 7), (0, D - parts.shape[2])))
@@ -877,25 +868,31 @@
     parts = last[:, capacity, : 3 * local * capacity].astype(F32)
     dgate_back = jnp.sum(parts.reshape(slabs, 3, local, capacity), 1)
     dgate_back = dgate_back.swapaxes(0, 1).reshape(1, slots)
-    *dd_back, big[-1] = lax.optimization_barrier((*dd_back, big[-1]))
-    big = [lax.psum_scatter(a, "fsdp", scatter_dimension=0, tiled=True)[0, 0] for a in big]
-    grad_w_in, grad_w_out = spread_grads(big)
-
-    dmid, grad_att, mixed = one_step(
+    act = [after(a, dd[-1]) for a in act]
+    big = weight_grads(list(zip(rows, dslot, act, dpre)))
+    *dd_back, big = lax.optimization_barrier((*dd_back, big))
+    big = lax.psum_scatter(big, "fsdp", scatter_dimension=0, tiled=True)[0]
+
+    dmid, grad_att, keep, send = one_step(
         functools.partial(return_kernel, local=local, experts=experts),
-        [shape((count, D), F32), shape((slabs, width, slab), BF), shape((D, D + 256), BF)],
+        [shape((count, D), F32), shape((slabs, width, slab), BF)]
+        + [shape((owners // 2, part, D + 256), BF)] * 2,
         (
-            dgate_back, slot_col, route_col, gates, mid, grad_flat, small, w_o_full, att,
+            me_f, dgate_back, slot_col, route_col, gates, mid, grad_flat, small, w_o_full, att,
             *dd_back, *grad_b,
         ),
         4 * count * D * (slots + 2 * D),
-        scratch=[pltpu.VMEM((128, D), F32), pltpu.VMEM((D, D), F32)],
+        scratch=[pltpu.VMEM((128, D), F32), pltpu.VMEM((D, D + 256), F32)],
+        smem=1,
     )
     results_back = [cross(after(results[0], *dd_back))]
     grad_heads = exchange(after(grad_att, *results_back))
     for a in results[1:]:
         results_back.append(cross(after(a, grad_heads, *results_back)))
+    mixed = fold_first(after(keep, grad_heads), send)
     d_qkv, band_sums = attention_bwd(qkv, seg, bands, wide, lse, grad_heads)
+    mixed[0] = after(mixed[0], d_qkv)
+    mixed = fold_rest(mixed)
     d_back = exchange(after(d_qkv, *results_back))
     output = one_step(
         output_kernel,
@@ -906,10 +903,10 @@
 
     keep, send = one_step(
         qkv_grad_kernel,
-        [shape((owners // 2, part, 3 * width + D + 320), BF)] * 2,
-        (me_f, first, d_qkv, band_sums, mixed),
+        [shape((owners // 2, part, 3 * width + 64), BF)] * 2,
+        (me_f, first, d_qkv, band_sums),
         4 * SEQ_LEN * D * 3 * width,
-        scratch=[pltpu.VMEM((3 * width, D), F32), pltpu.VMEM((D, 3 * width + D + 320), F32)],
+        scratch=[pltpu.VMEM((3 * width, D), F32), pltpu.VMEM((D, 3 * width + 64), F32)],
         smem=1,
     )
     grad_tokens = one_step(
@@ -919,8 +916,7 @@
         4 * count * D * 3 * D,
         scratch=[pltpu.VMEM((3 * D, slab), BF)],
     )[0]
-    folded = fold_rest(fold_first(keep, send))
-    grad_qkv, mixed = folded[:, : 3 * width + 64], folded[:, 3 * width + 64 :]
+    grad_qkv = fold_rest(fold_first(keep, send))
     grad_b_own = mixed[:, D + 1 : D + 1 + local].astype(F32).T
     quarter = (D + 256) // per_group
 
@@ -928,12 +924,14 @@
         return lax.dynamic_slice_in_dim(mixed, (head_group ^ offset) * quarter, quarter, 1)
 
     mixed = add(quarter_of(0), *[swap(quarter_of(k), "seq", k) for k in range(1, per_group)])
-    block = after(jnp.concatenate([grad_qkv, mixed], 1), grad_tokens)
+    block = jnp.concatenate([grad_qkv, mixed], 1)
     bit = per_group
     while bit < slabs:
         block = add(block, swap(block, "seq", bit))
         bit *= 2
     blocks = [block] + [swap(block, "seq", k) for k in range(1, per_group)]
+    big = after(big, grad_tokens)
+    grad_w_in, grad_w_out = spread_grads(big)
     blocks[0], grad_w_in, grad_w_out = lax.optimization_barrier((blocks[0], grad_w_in, grad_w_out))
     grad_wqkv, grad_gain_attn, grad_bias, grad_wo, grad_gain_ffn, grad_router = one_step(
         functools.partial(finish_kernel, pairs=pairs, experts=experts),

time: 467 us -> 450 us (0.964)
  waiting for transfers between devices: 133 us -> 122 us
    all_to_all x8, waiting for transfers between devices: 66.7 us -> 47.6 us  [exchange(): return lax.all_to_all(array, 'seq', split_axis=0, concat_axis=0, tiled=True)]
    ppermute x19 -> x21, waiting for transfers between devices: 65.4 us -> 72.7 us  [swap(): return lax.ppermute(array, axis, [(i, i ^ bit) for i in range(size)])]
    pallas_call x2 -> x1, Pallas kernels: 23.8 us -> 21.9 us  [weight_grads(): pl.pallas_call(functools.partial(weight_kernel, local=local, parts=parts)...]
    ppermute x19 -> x21, starting transfers between devices: 24.4 us -> 25.1 us  [swap(): return lax.ppermute(array, axis, [(i, i ^ bit) for i in range(size)])]
  transfers between devices with their start and end apart: 32 -> 33, of which waited for: 16 -> 16; matrix products, arithmetic and copies ran while one was open for 5% -> 5% of each run, Pallas kernels for 36% -> 36%
where the time goes in v2:
time: 450 us; the launch traced here: 443 us
  Pallas kernels  164 us (36%)
  waiting for transfers between devices  122 us (27%)
  starting transfers between devices  62.8 us (14%)
  blocking collectives  46.8 us (10%)
  local copies, waits for them, and re-layouts  23.8 us (5%)
  between operations  14.6 us (3%)
  other arithmetic  9.91 us (2%)
    ppermute x21, waiting for transfers between devices, swap(): return lax.ppermute(array, axis, [(i, i ^ bit) for i in range(size)])  72.7 us
    pallas_call x10, Pallas kernels, one_step(): pl.pallas_call(kernel, out_shape=tuple(outs), in_specs=[pl.BlockSpec(memo...  57.7 us
    all_to_all x8, waiting for transfers between devices, exchange(): return lax.all_to_all(array, 'seq', split_axis=0, concat_axis=0, tiled=True)  47.6 us
    all_to_all x2, blocking collectives, exchange(): return lax.all_to_all(array, 'seq', split_axis=0, concat_axis=0, tiled=True)  46.8 us
    all_to_all x8, starting transfers between devices, exchange(): return lax.all_to_all(array, 'seq', split_axis=0, concat_axis=0, tiled=True)  37.5 us
    pallas_call x2, Pallas kernels, expert_pass(): pl.pallas_call(functools.partial(expert_kernel, index=index, local=local,...  37 us
    ppermute x21, starting transfers between devices, swap(): return lax.ppermute(array, axis, [(i, i ^ bit) for i in range(size)])  25.1 us
    pallas_call x1, Pallas kernels, attention_bwd(): pl.pallas_call(bwd_kernel, grid=(pairs,), out_shape=(shape(qkv.shape, BF)...  23.3 us
  transfers between devices with their start and end apart: 33, of which 16 were waited for; matrix products, arithmetic and copies ran while one was open for 5% of the time, Pallas kernels for 36%

profile of v2, /device:TPU:0, one launch (start us, length us, event | category | flops | bytes accessed | tf_op | source)
XLA Modules:
  0.0 443.4 jit_solution(4175760540310020043)
XLA Ops:
  7.2 3.0 copy_bitcast_fusion
  10.7 2.5 fusion.18
  15.8 2.4 shard_map.212.refs_0_
  18.2 3.0 collective-permute-start
  21.3 2.7 collective-permute-start.3
  27.4 13.9 %collective-permute-done.3.refs_1_ = bf16[256,768]{1,0:T(8,128)(2,1)S(1)} collective-permute-done((bf16[256,768]{1,0:T(8,128)(2,1)S(1)}, bf16[256,768]{1,0:T(8,128)(2,1)S(1)}, u32[]{:S(2)}, u32[]{:S(2)}) %collective-permute-start.3) | collective-permute-done | bytes 393248 | tf_op jit(solution)/shard_map/ppermute | solution.py:693
  41.3 2.0 collective-permute-done.refs_1_
  44.8 6.3 %collective-permute-done.6.refs_4_ = bf16[256,768]{1,0:T(8,128)(2,1)S(1)} collective-permute-done((bf16[256,768]{1,0:T(8,128)(2,1)S(1)}, bf16[256,768]{1,0:T(8,128)(2,1)S(1)}, u32[]{:S(2)}, u32[]{:S(2)}) %collective-permute-start.6) | collective-permute-done | bytes 393248 | tf_op jit(solution)/shard_map/ppermute | solution.py:693
  53.6 1.8 collective-permute-start.9
  56.4 4.6 %shard_map.213 = (bf16[768,576]{1,0:T(8,128)(2,1)}, bf16[768,768]{1,0:T(8,128)(2,1)}, f32[128,768]{1,0:T(8,128)}, f32[3,384,256]{2,1,0:T(8,128)}) custom-call(s32[1]{0:T(128)} %bitcast.me_ref, bf16[192,1472]{1,0:T(8,128)(2,1)} %shard_map.212.refs_0_, bf16[192,1472]{1,0:T(8,128)(2,1)} %copy-done.12, bf16[192,1472]{1,0:T(8,128)(2,1)} %copy-done.13, ...), custom_call_target="tpu_custom_call" | custom-call | flops 60000000 | bytes 117964 | tf_op jit(solution)/shard_map/pallas_call | solution.py:207
  61.0 2.0 collective-permute-done.7.refs_5_
  65.6 4.3 shard_map.214
  70.9 2.8 fusion.2
  73.7 5.3 %all-to-all-start = ((bf16[8,152,768]{2,1,0:T(8,128)(2,1)}), bf16[8,152,768]{2,1,0:T(8,128)(2,1)S(1)}, u32[]{:S(2)}, u32[]{:S(2)}) async-start(bf16[8,152,768]{2,1,0:T(8,128)(2,1)} %fusion.2), calls=%async_computation | async-start | bytes 3735552 | tf_op jit(solution)/shard_map/all_to_all | solution.py:706
  79.6 7.1 %shard_map.215 = (bf16[8,576,256]{2,1,0:T(8,128)(2,1)}, bf16[8,256,768]{2,1,0:T(8,128)(2,1)}) custom-call(s32[1]{0:T(128)} %bitcast.8.me_ref.own_ref, f32[128,768]{1,0:T(8,128)} %get-tuple-element.85.small_ref, bf16[768,576]{1,0:T(8,128)(2,1)} %get-tuple-element.90.w_ref, bf16[256,768]{1,0:T(8,128)(2,1)} %copy-done.10, bf16[256,768]{1,0:T(8,128)(2,1)} %copy-done.15, ...), custom_call_target="tpu_custom_call" | custom-call | flops 72477576 | bytes 198574 | tf_op jit(solution)/shard_map/pallas_call | solution.py:207
  86.7 16.5 %shard_map.216 = (bf16[8,192,256]{2,1,0:T(8,128)(2,1)}, f32[3,64,2048]{2,1,0:T(8,128)}, f32[3,1,2048]{2,1,0:T(1,128)}) custom-call(bf16[8,576,256]{2,1,0:T(8,128)(2,1)} %get-tuple-element.91.qkv_ref, s32[1,2048]{1,0:T(1,128)} %constant_dynamic-slice_fusion.3.seg_ref, f32[3,384,256]{2,1,0:T(8,128)} %get-tuple-element.92.band_ref), custom_call_target="tpu_custom_call" | custom-call | flops 17999998976 | bytes 6000000 | tf_op jit(solution)/shard_map/pallas_call | solution.py:154
  103.2 14.7 %all-to-all-done = bf16[8,152,768]{2,1,0:T(8,128)(2,1)S(1)} async-done(((bf16[8,152,768]{2,1,0:T(8,128)(2,1)}), bf16[8,152,768]{2,1,0:T(8,128)(2,1)S(1)}, u32[]{:S(2)}, u32[]{:S(2)}) %all-to-all-start) | async-done | bytes 1867808 | tf_op jit(solution)/shard_map/all_to_all | solution.py:706
  117.9 22.9 %all_to_all.50.chunk_ref.att_ref = bf16[8,192,256]{2,1,0:T(8,128)(2,1)} all-to-all(bf16[8,192,256]{2,1,0:T(8,128)(2,1)} %get-tuple-element.98), channel_id=1, replica_groups=mesh['seq'=8,'fsdp'=4] {'seq'}, dimensions={0} | all-to-all | bytes 1572864 | tf_op jit(solution)/shard_map/all_to_all | solution.py:706
  140.8 5.0 %shard_map.217 = (f32[512,768]{1,0:T(8,128)}, f32[512,2]{1,0:T(8,128)}, bf16[576,768]{1,0:T(8,128)(2,1)}, bf16[576,768]{1,0:T(8,128)(2,1)}) custom-call(bf16[2,256,768]{2,1,0:T(8,128)(2,1)} %tok_ref.3, f32[128,768]{1,0:T(8,128)} %get-tuple-element.85.small_ref, bf16[768,768]{1,0:T(8,128)(2,1)} %get-tuple-element.86.w_ref, s32[512,2]{1,0:T(8,128)} %bitcast.64, ...), custom_call_target="tpu_custom_call" | custom-call | flops 60397976 | bytes 130007 | tf_op jit(solution)/shard_map/pallas_call | solution.py:207
  145.8 3.6 all-to-all-start.2
  151.9 19.4 %all-to-all-done.2 = bf16[8,72,768]{2,1,0:T(8,128)(2,1)S(1)} async-done(((bf16[8,72,768]{2,1,0:T(8,128)(2,1)}), bf16[8,72,768]{2,1,0:T(8,128)(2,1)S(1)}, u32[]{:S(2)}, u32[]{:S(2)}) %all-to-all-start.2) | async-done | bytes 884768 | tf_op jit(solution)/shard_map/all_to_all | solution.py:706
  171.3 4.4 all-to-all-start.3
  177.1 18.5 %shard_map.218 = (bf16[576,768]{1,0:T(8,128)(2,1)}, bf16[576,768]{1,0:T(8,128)(2,1)}, bf16[16,576]{1,0:T(8,128)(2,1)}, bf16[576,768]{1,0:T(8,128)(2,1)}, bf16[4,...) custom-call(s32[1]{0:T(128)} %bitcast.8.me_ref.own_ref, bf16[576,768]{1,0:T(8,128)(2,1)} %bitcast.71, ...), custom_call_target="tpu_custom_call" | custom-call | flops 13589544960 | bytes 28311552 | tf_op jit(solution)/shard_map/pallas_call | solution.py:599
  195.6 2.1 all-to-all-done.3
  197.6 4.0 all-to-all-start.4
  201.6 18.5 %shard_map.219 = (bf16[576,768]{1,0:T(8,128)(2,1)}, bf16[576,768]{1,0:T(8,128)(2,1)}, bf16[16,576]{1,0:T(8,128)(2,1)}, bf16[576,768]{1,0:T(8,128)(2,1)}, bf16[4,...) custom-call(s32[1]{0:T(128)} %bitcast.8.me_ref.own_ref, ...), custom_call_target="tpu_custom_call" | custom-call | flops 13589544960 | bytes 28311552 | tf_op jit(solution)/shard_map/pallas_call | solution.py:599
  221.8 2.2 fusion.3
  224.0 6.0 %all-to-all-start.5 = ((bf16[8,80,768]{2,1,0:T(8,128)(2,1)}), bf16[8,80,768]{2,1,0:T(8,128)(2,1)S(1)}, u32[]{:S(2)}, u32[]{:S(2)}) async-start(bf16[8,80,768]{2,1,0:T(8,128)(2,1)} %fusion.3), calls=%async_computation.5 | async-start | bytes 1966080 | tf_op jit(solution)/shard_map/all_to_all | solution.py:706
  230.0 21.9 %shard_map.220 = bf16[4,2,2,768,768]{4,3,2,1,0:T(8,128)(2,1)} custom-call(bf16[576,768]{1,0:T(8,128)(2,1)} %bitcast.72, bf16[576,768]{1,0:T(8,128)(2,1)} %get-tuple-element.114.refs_1_, bf16[4,576,768]{2,1,0:T(8,128)(2,1)} %get-tuple-element.116.refs_2_, bf16[4,576,768]{2,1,0:T(8,128)(2,1)} %get-tuple-element.117.refs_3_, ...), custom_call_target="tpu_custom_call" | custom-call | flops 1000000 | bytes 1000000 | tf_op jit(solution)/shard_map/pallas_call | solution.py:649
  254.5 4.5 %all-to-all-start.6 = ((bf16[8,72,768]{2,1,0:T(8,128)(2,1)}), bf16[8,72,768]{2,1,0:T(8,128)(2,1)S(1)}, u32[]{:S(2)}, u32[]{:S(2)}) async-start(bf16[8,72,768]{2,1,0:T(8,128)(2,1)} %bitcast.29), calls=%async_computation.6 | async-start | bytes 1769472 | tf_op jit(solution)/shard_map/all_to_all | solution.py:706
  259.9 11.1 %shard_map.221 = (f32[512,768]{1,0:T(8,128)}, bf16[8,192,256]{2,1,0:T(8,128)(2,1)}, bf16[2,192,1024]{2,1,0:T(8,128)(2,1)}, bf16[2,192,1024]{2,1,0:T(8,128)(2,1)}) custom-call(s32[1]{0:T(128)} %bitcast.me_ref, f32[1,1152]{1,0:T(1,128)} %reshape.183.dgate_ref, s32[512,2]{1,0:T(8,128)} %get-tuple-element.112.slot_ref, s32[512,2]{1,0:T(8,128)} %bitcast.65, ...), custom_call_target="tpu_custom_call" | custom-call | flops 84557168 | bytes 208865 | tf_op jit(solution)/shard_map/pallas_call | solution.py:207
  271.0 9.8 %all-to-all-done.6 = bf16[8,72,768]{2,1,0:T(8,128)(2,1)S(1)} async-done(((bf16[8,72,768]{2,1,0:T(8,128)(2,1)}), bf16[8,72,768]{2,1,0:T(8,128)(2,1)S(1)}, u32[]{:S(2)}, u32[]{:S(2)}) %all-to-all-start.6) | async-done | bytes 884768 | tf_op jit(solution)/shard_map/all_to_all | solution.py:706
  280.8 23.8 %all_to_all.51.do_ref = bf16[8,192,256]{2,1,0:T(8,128)(2,1)} all-to-all(bf16[8,192,256]{2,1,0:T(8,128)(2,1)} %get-tuple-element.129), channel_id=1, replica_groups=mesh['seq'=8,'fsdp'=4] {'seq'}, dimensions={0} | all-to-all | bytes 1572864 | tf_op jit(solution)/shard_map/all_to_all | solution.py:706
  304.6 3.6 all-to-all-start.8
  308.2 23.3 %shard_map.222 = (bf16[8,576,256]{2,1,0:T(8,128)(2,1)}, f32[3,384,256]{2,1,0:T(8,128)}) custom-call(bf16[8,576,256]{2,1,0:T(8,128)(2,1)} %get-tuple-element.91.qkv_ref, s32[1,2048]{1,0:T(1,128)} %constant_dynamic-slice_fusion.3.seg_ref, f32[3,384,256]{2,1,0:T(8,128)} %get-tuple-element.92.band_ref, f32[3,64,2048]{2,1,0:T(8,128)} %get-tuple-element.100.wide_ref, ...), custom_call_target="tpu_custom_call" | custom-call | flops 30000001024 | bytes 9000000 | tf_op jit(solution)/shard_map/pallas_call | solution.py:179
  332.4 6.3 %all-to-all-start.9 = ((bf16[8,576,256]{2,1,0:T(8,128)(2,1)}), bf16[8,576,256]{2,1,0:T(8,128)(2,1)S(1)}, u32[]{:S(2)}, u32[]{:S(2)}) async-start(bf16[8,576,256]{2,1,0:T(8,128)(2,1)} %get-tuple-element.136.d_ref), calls=%async_computation.9 | async-start | bytes 4718592 | tf_op jit(solution)/shard_map/all_to_all | solution.py:706
  338.8 2.3 collective-permute-done.12
  343.2 7.0 %shard_map.224 = (bf16[2,192,640]{2,1,0:T(8,128)(2,1)}, bf16[2,192,640]{2,1,0:T(8,128)(2,1)}) custom-call(s32[1]{0:T(128)} %bitcast.me_ref, bf16[8,256,768]{2,1,0:T(8,128)(2,1)} %get-tuple-element.137.first_ref, bf16[8,576,256]{2,1,0:T(8,128)(2,1)} %get-tuple-element.136.d_ref, f32[3,384,256]{2,1,0:T(8,128)} %get-tuple-element.138.band_ref), custom_call_target="tpu_custom_call" | custom-call | flops 72477576 | bytes 153354 | tf_op jit(solution)/shard_map/pallas_call | solution.py:207
  350.1 12.5 %collective-permute-done.13 = bf16[192,1024]{1,0:T(8,128)(2,1)S(1)} collective-permute-done((bf16[192,1024]{1,0:T(8,128)(2,1)S(1)}, bf16[192,1024]{1,0:T(8,128)(2,1)S(1)}, u32[]{:S(2)}, u32[]{:S(2)}) %collective-permute-start.13) | collective-permute-done | bytes 393248 | tf_op jit(solution)/shard_map/ppermute | solution.py:693
  363.6 3.0 collective-permute-start.16
  368.9 10.4 %collective-permute-done.16 = bf16[192,256]{1,0:T(8,128)(2,1)S(1)} collective-permute-done((bf16[192,256]{1,0:T(8,128)(2,1)}, bf16[192,256]{1,0:T(8,128)(2,1)S(1)}, u32[]{:S(2)}, u32[]{:S(2)}) %collective-permute-start.16) | collective-permute-done | bytes 98336 | tf_op jit(solution)/shard_map/ppermute | solution.py:693
  382.8 4.0 collective-permute-start.17
  386.8 19.4 %collective-permute-done.17 = bf16[192,896]{1,0:T(8,128)(2,1)S(1)} collective-permute-done((bf16[192,896]{1,0:T(8,128)(2,1)S(1)}, bf16[192,896]{1,0:T(8,128)(2,1)S(1)}, u32[]{:S(2)}, u32[]{:S(2)}) %collective-permute-start.17) | collective-permute-done | bytes 344096 | tf_op jit(solution)/shard_map/ppermute | solution.py:693
  407.9 2.0 collective-permute-start.20
  410.6 5.6 %shard_map.223 = bf16[512,768]{1,0:T(8,128)(2,1)} custom-call(f32[512,768]{1,0:T(8,128)} %get-tuple-element.131.mid_ref, s32[512,2]{1,0:T(8,128)} %get-tuple-element.112.slot_ref, f32[512,2]{1,0:T(8,128)} %get-tuple-element.113.gate_ref, bf16[576,768]{1,0:T(8,128)(2,1)} %bitcast.69, bf16[576,768]{1,0:T(8,128)(2,1)} %bitcast.70), custom_call_target="tpu_custom_call" | custom-call | flops 36238784 | bytes 82739 | tf_op jit(solution)/shard_map/pallas_call | solution.py:207
  417.6 7.4 %shard_map.225 = f32[2,256,768]{2,1,0:T(8,128)} custom-call(bf16[2,256,768]{2,1,0:T(8,128)(2,1)} %tok_ref.3, f32[128,768]{1,0:T(8,128)} %get-tuple-element.85.small_ref, bf16[768,2304]{1,0:T(8,128)(2,1)} %all-gather.8.cloned.1.call-done.w_ref, f32[512,768]{1,0:T(8,128)} %get-tuple-element.135.dmid_ref, bf16[8,576,256]{2,1,0:T(8,128)(2,1)} %copy-done.3), custom_call_target="tpu_custom_call" | custom-call | flops 72477576 | bytes 204472 | tf_op jit(solution)/shard_map/pallas_call | solution.py:207
  425.0 7.4 %shard_map.226 = (f32[768,2,768]{2,1,0:T(2,128)}, f32[768,2,768]{2,1,0:T(2,128)}) custom-call(bf16[2,2,768,768]{3,2,1,0:T(8,128)(2,1)} %bitcast.66), custom_call_target="tpu_custom_call" | custom-call | flops 1000000 | bytes 1000000 | tf_op jit(solution)/shard_map/pallas_call | solution.py:676
  433.2 3.2 shard_map.227
  (133 shorter events, 39.0 us)
Async XLA Ops:
  7.2 71.8 %copy-start = (s32[2,2048]{1,0:T(2,128)S(1)}, s32[2,2048]{1,0:T(2,128)}, u32[]{:S(2)}) copy-start(s32[2,2048]{1,0:T(2,128)} %param.15) | copy-start | bytes 49156
  7.2 169.9 %all-gather.4.cloned.1.call-start = ((), (), s32[]{:S(2)}) async-start(), calls=%async_computation.11 | async-start | bytes 11796480 | tf_op jit(solution)/shard_map/all_gather | solution.py:844
  13.2 1.9 copy-start.20
  13.2 8.0 %copy-start.4 = (bf16[2,256,768]{2,1,0:T(8,128)(2,1)S(1)}, bf16[2,256,768]{2,1,0:T(8,128)(2,1)}, u32[]{:S(2)}) copy-start(bf16[2,256,768]{2,1,0:T(8,128)(2,1)} %tok_ref.3) | copy-start | bytes 2359300
  13.2 188.4 %all-gather.6.cloned.1.call-start = ((), (), s32[]{:S(2)}) async-start(), calls=%async_computation.12 | async-start | bytes 11796480 | tf_op jit(solution)/shard_map/all_gather | solution.py:844
  18.2 25.1 %collective-permute-start = (bf16[192,1472]{1,0:T(8,128)(2,1)}, bf16[192,1472]{1,0:T(8,128)(2,1)S(1)}, u32[]{:S(2)}, u32[]{:S(2)}) collective-permute-start(bf16[192,1472]{1,0:T(8,128)(2,1)} %shard_map.212.refs_0_), channel_id=1, source_target_pairs={{0,2},{1,3},{2,0},{3,1},{4,6},{5,7},{6,4},{7,5},{8,10},{9,11},{10,... | collective-permute-start | bytes 1695752 | tf_op jit(solution)/shard_map/ppermute | solution.py:693
  21.2 48.7 %copy-start.10 = (bf16[256,768]{1,0:T(8,128)(2,1)}, bf16[256,768]{1,0:T(8,128)(2,1)S(1)}, u32[]{:S(2)}) copy-start(bf16[256,768]{1,0:T(8,128)(2,1)S(1)} %get-tuple-element.211.refs_0_) | copy-start | bytes 1179652
  21.3 20.1 %collective-permute-start.3 = (bf16[256,768]{1,0:T(8,128)(2,1)S(1)}, bf16[256,768]{1,0:T(8,128)(2,1)S(1)}, u32[]{:S(2)}, u32[]{:S(2)}) collective-permute-start(bf16[256,768]{1,0:T(8,128)(2,1)S(1)} %get-tuple-element.212), channel_id=1, source_target_pairs={{0,16},{4,20},{8,24},{12,28},{16,0},{20,4},{24,8},{28,12},{1,17},{... | collective-permute-start | bytes 1179656 | tf_op jit(solution)/shard_map/ppermute | solution.py:693
  23.9 19.5 %collective-permute-start.4 = (bf16[256,768]{1,0:T(8,128)(2,1)S(1)}, bf16[256,768]{1,0:T(8,128)(2,1)S(1)}, u32[]{:S(2)}, u32[]{:S(2)}) collective-permute-start(bf16[256,768]{1,0:T(8,128)(2,1)S(1)} %get-tuple-element.211.refs_0_), channel_id=1, source_target_pairs={{0,4},{4,0},{8,12},{12,8},{16,20},{20,16},{24,28},{28,24},{1,5},{5... | collective-permute-start | bytes 1179656 | tf_op jit(solution)/shard_map/ppermute | solution.py:693
  25.4 19.4 %collective-permute-start.5 = (bf16[256,768]{1,0:T(8,128)(2,1)S(1)}, bf16[256,768]{1,0:T(8,128)(2,1)S(1)}, u32[]{:S(2)}, u32[]{:S(2)}) collective-permute-start(bf16[256,768]{1,0:T(8,128)(2,1)S(1)} %get-tuple-element.211.refs_0_), channel_id=1, source_target_pairs={{0,8},{4,12},{8,0},{12,4},{16,24},{20,28},{24,16},{28,20},{1,9},{5... | collective-permute-start | bytes 1179656 | tf_op jit(solution)/shard_map/ppermute | solution.py:693
  27.0 24.1 %collective-permute-start.6 = (bf16[256,768]{1,0:T(8,128)(2,1)S(1)}, bf16[256,768]{1,0:T(8,128)(2,1)S(1)}, u32[]{:S(2)}, u32[]{:S(2)}) collective-permute-start(bf16[256,768]{1,0:T(8,128)(2,1)S(1)} %get-tuple-element.211.refs_0_), channel_id=1, source_target_pairs={{0,12},{4,8},{8,4},{12,0},{16,28},{20,24},{24,20},{28,16},{1,13},{... | collective-permute-start | bytes 1179656 | tf_op jit(solution)/shard_map/ppermute | solution.py:693
  41.3 38.3 %copy-start.15 = (bf16[256,768]{1,0:T(8,128)(2,1)}, bf16[256,768]{1,0:T(8,128)(2,1)S(1)}, u32[]{:S(2)}) copy-start(bf16[256,768]{1,0:T(8,128)(2,1)S(1)} %collective-permute-done.3.refs_1_) | copy-start | bytes 1179652
  41.3 14.0 %collective-permute-start.1 = (bf16[192,1472]{1,0:T(8,128)(2,1)}, bf16[192,1472]{1,0:T(8,128)(2,1)S(1)}, u32[]{:S(2)}, u32[]{:S(2)}) collective-permute-start(bf16[192,1472]{1,0:T(8,128)(2,1)} %shard_map.212.refs_0_), channel_id=1, source_target_pairs={{0,1},{1,0},{2,3},{3,2},{4,5},{5,4},{6,7},{7,6},{8,9},{9,8},{10,11... | collective-permute-start | bytes 1695752 | tf_op jit(solution)/shard_map/ppermute | solution.py:693
  43.4 12.0 %copy-start.12 = (bf16[192,1472]{1,0:T(8,128)(2,1)}, bf16[192,1472]{1,0:T(8,128)(2,1)S(1)}, u32[]{:S(2)}) copy-start(bf16[192,1472]{1,0:T(8,128)(2,1)S(1)} %collective-permute-done.refs_1_) | copy-start | bytes 1695748
  43.4 12.0 %collective-permute-start.2 = (bf16[192,1472]{1,0:T(8,128)(2,1)S(1)}, bf16[192,1472]{1,0:T(8,128)(2,1)S(1)}, u32[]{:S(2)}, u32[]{:S(2)}) collective-permute-start(bf16[192,1472]{1,0:T(8,128)(2,1)S(1)} %collective-permute-done.refs_1_), channel_id=1, source_target_pairs={{0,1},{1,0},{2,3},{3,2},{4,5},{5,4},{6,7},{7,6},{8,9},{9,8},{10,11... | collective-permute-start | bytes 1695752 | tf_op jit(solution)/shard_map/ppermute | solution.py:693
  43.4 36.2 %copy-start.16 = (bf16[256,768]{1,0:T(8,128)(2,1)}, bf16[256,768]{1,0:T(8,128)(2,1)S(1)}, u32[]{:S(2)}) copy-start(bf16[256,768]{1,0:T(8,128)(2,1)S(1)} %collective-permute-done.4.refs_2_) | copy-start | bytes 1179652
  44.8 34.8 %copy-start.17 = (bf16[256,768]{1,0:T(8,128)(2,1)}, bf16[256,768]{1,0:T(8,128)(2,1)S(1)}, u32[]{:S(2)}) copy-start(bf16[256,768]{1,0:T(8,128)(2,1)S(1)} %collective-permute-done.5.refs_3_) | copy-start | bytes 1179652
  51.9 11.2 %collective-permute-start.7 = (bf16[256,768]{1,0:T(8,128)(2,1)S(1)}, bf16[256,768]{1,0:T(8,128)(2,1)}, u32[]{:S(2)}, u32[]{:S(2)}) collective-permute-start(bf16[256,768]{1,0:T(8,128)(2,1)S(1)} %collective-permute-done.3.refs_1_), channel_id=1, source_target_pairs={{0,4},{4,0},{8,12},{12,8},{16,20},{20,16},{24,28},{28,24},{1,5},{5... | collective-permute-start | bytes 1179656 | tf_op jit(solution)/shard_map/ppermute | solution.py:693
  53.4 20.3 %collective-permute-start.8 = (bf16[256,768]{1,0:T(8,128)(2,1)S(1)}, bf16[256,768]{1,0:T(8,128)(2,1)}, u32[]{:S(2)}, u32[]{:S(2)}) collective-permute-start(bf16[256,768]{1,0:T(8,128)(2,1)S(1)} %collective-permute-done.3.refs_1_), channel_id=1, source_target_pairs={{0,8},{4,12},{8,0},{12,4},{16,24},{20,28},{24,16},{28,20},{1,9},{5... | collective-permute-start | bytes 1179656 | tf_op jit(solution)/shard_map/ppermute | solution.py:693
  53.6 20.1 %collective-permute-start.9 = (bf16[256,768]{1,0:T(8,128)(2,1)S(1)}, bf16[256,768]{1,0:T(8,128)(2,1)}, u32[]{:S(2)}, u32[]{:S(2)}) collective-permute-start(bf16[256,768]{1,0:T(8,128)(2,1)S(1)} %collective-permute-done.3.refs_1_), channel_id=1, source_target_pairs={{0,12},{4,8},{8,4},{12,0},{16,28},{20,24},{24,20},{28,16},{1,13},{... | collective-permute-start | bytes 1179656 | tf_op jit(solution)/shard_map/ppermute | solution.py:693
  63.9 1.7 copy-start.2
  73.7 44.2 %all-to-all-start = ((bf16[8,152,768]{2,1,0:T(8,128)(2,1)}), bf16[8,152,768]{2,1,0:T(8,128)(2,1)S(1)}, u32[]{:S(2)}, u32[]{:S(2)}) async-start(bf16[8,152,768]{2,1,0:T(8,128)(2,1)} %fusion.2), calls=%async_computation | async-start | bytes 3735552 | tf_op jit(solution)/shard_map/all_to_all | solution.py:706
  145.8 25.5 %all-to-all-start.2 = ((bf16[8,72,768]{2,1,0:T(8,128)(2,1)}), bf16[8,72,768]{2,1,0:T(8,128)(2,1)S(1)}, u32[]{:S(2)}, u32[]{:S(2)}) async-start(bf16[8,72,768]{2,1,0:T(8,128)(2,1)} %bitcast.83), calls=%async_computation.2 | async-start | bytes 1769472 | tf_op jit(solution)/shard_map/all_to_all | solution.py:706
  149.4 266.9 %all-gather.8.cloned.1.call-start = ((), (), s32[]{:S(2)}) async-start(), calls=%async_computation.13 | async-start | bytes 4423680 | tf_op jit(solution)/shard_map/all_gather | solution.py:847
  171.3 5.8 %copy-start.8 = (bf16[8,72,768]{2,1,0:T(8,128)(2,1)}, bf16[8,72,768]{2,1,0:T(8,128)(2,1)S(1)}, u32[]{:S(2)}) copy-start(bf16[8,72,768]{2,1,0:T(8,128)(2,1)S(1)} %all-to-all-done.2) | copy-start | bytes 2654212
  171.3 26.3 %all-to-all-start.3 = ((bf16[8,72,768]{2,1,0:T(8,128)(2,1)}), bf16[8,72,768]{2,1,0:T(8,128)(2,1)}, u32[]{:S(2)}, u32[]{:S(2)}) async-start(bf16[8,72,768]{2,1,0:T(8,128)(2,1)} %bitcast.81), calls=%async_computation.3 | async-start | bytes 1769472 | tf_op jit(solution)/shard_map/all_to_all | solution.py:706
  197.6 26.3 %all-to-all-start.4 = ((bf16[8,72,768]{2,1,0:T(8,128)(2,1)}), bf16[8,72,768]{2,1,0:T(8,128)(2,1)S(1)}, u32[]{:S(2)}, u32[]{:S(2)}) async-start(bf16[8,72,768]{2,1,0:T(8,128)(2,1)} %bitcast.82), calls=%async_computation.4 | async-start | bytes 1769472 | tf_op jit(solution)/shard_map/all_to_all | solution.py:706
  224.0 27.9 %copy-start.5 = (bf16[8,72,768]{2,1,0:T(8,128)(2,1)}, bf16[8,72,768]{2,1,0:T(8,128)(2,1)S(1)}, u32[]{:S(2)}) copy-start(bf16[8,72,768]{2,1,0:T(8,128)(2,1)S(1)} %all-to-all-done.4) | copy-start | bytes 2654212
  224.0 29.6 %all-to-all-start.5 = ((bf16[8,80,768]{2,1,0:T(8,128)(2,1)}), bf16[8,80,768]{2,1,0:T(8,128)(2,1)S(1)}, u32[]{:S(2)}, u32[]{:S(2)}) async-start(bf16[8,80,768]{2,1,0:T(8,128)(2,1)} %fusion.3), calls=%async_computation.5 | async-start | bytes 1966080 | tf_op jit(solution)/shard_map/all_to_all | solution.py:706
  229.9 195.1 %reduce-scatter.2.cloned.1.call-start = ((), (), s32[]{:S(2)}) async-start(), calls=%async_computation.14 | async-start | bytes 23592960 | tf_op jit(solution)/shard_map/reduce_scatter | solution.py:874
  254.5 26.3 %all-to-all-start.6 = ((bf16[8,72,768]{2,1,0:T(8,128)(2,1)}), bf16[8,72,768]{2,1,0:T(8,128)(2,1)S(1)}, u32[]{:S(2)}, u32[]{:S(2)}) async-start(bf16[8,72,768]{2,1,0:T(8,128)(2,1)} %bitcast.29), calls=%async_computation.6 | async-start | bytes 1769472 | tf_op jit(solution)/shard_map/all_to_all | solution.py:706
  280.8 50.7 %copy-start.6 = (bf16[8,72,768]{2,1,0:T(8,128)(2,1)}, bf16[8,72,768]{2,1,0:T(8,128)(2,1)S(1)}, u32[]{:S(2)}) copy-start(bf16[8,72,768]{2,1,0:T(8,128)(2,1)S(1)} %all-to-all-done.6) | copy-start | bytes 2654212
  304.6 26.9 %all-to-all-start.8 = ((bf16[8,72,768]{2,1,0:T(8,128)(2,1)}), bf16[8,72,768]{2,1,0:T(8,128)(2,1)S(1)}, u32[]{:S(2)}, u32[]{:S(2)}) async-start(bf16[8,72,768]{2,1,0:T(8,128)(2,1)} %bitcast.31), calls=%async_computation.8 | async-start | bytes 1769472 | tf_op jit(solution)/shard_map/all_to_all | solution.py:706
  331.5 7.2 %copy-start.21 = (bf16[2,192,1024]{2,1,0:T(8,128)(2,1)S(1)}, bf16[2,192,1024]{2,1,0:T(8,128)(2,1)}, u32[]{:S(2)}) copy-start(bf16[2,192,1024]{2,1,0:T(8,128)(2,1)} %get-tuple-element.144) | copy-start | bytes 2359300
  332.4 83.8 %all-to-all-start.9 = ((bf16[8,576,256]{2,1,0:T(8,128)(2,1)}), bf16[8,576,256]{2,1,0:T(8,128)(2,1)S(1)}, u32[]{:S(2)}, u32[]{:S(2)}) async-start(bf16[8,576,256]{2,1,0:T(8,128)(2,1)} %get-tuple-element.136.d_ref), calls=%async_computation.9 | async-start | bytes 4718592 | tf_op jit(solution)/shard_map/all_to_all | solution.py:706
  338.7 2.4 collective-permute-start.12
  342.5 20.2 %collective-permute-start.13 = (bf16[192,1024]{1,0:T(8,128)(2,1)S(1)}, bf16[192,1024]{1,0:T(8,128)(2,1)S(1)}, u32[]{:S(2)}, u32[]{:S(2)}) collective-permute-start(bf16[192,1024]{1,0:T(8,128)(2,1)S(1)} %get-tuple-element.210), channel_id=1, source_target_pairs={{0,2},{1,3},{2,0},{3,1},{4,6},{5,7},{6,4},{7,5},{8,10},{9,11},{10,... | collective-permute-start | bytes 1179656 | tf_op jit(solution)/shard_map/ppermute | solution.py:693
  350.1 17.0 %collective-permute-start.10 = (bf16[2,192,640]{2,1,0:T(8,128)(2,1)}, bf16[2,192,640]{2,1,0:T(8,128)(2,1)}, u32[]{:S(2)}, u32[]{:S(2)}) collective-permute-start(bf16[2,192,640]{2,1,0:T(8,128)(2,1)} %get-tuple-element.141), channel_id=1, source_target_pairs={{0,1},{1,0},{2,3},{3,2},{4,5},{5,4},{6,7},{7,6},{8,9},{9,8},{10,11... | collective-permute-start | bytes 1474568 | tf_op jit(solution)/shard_map/ppermute | solution.py:693
  363.6 15.7 %collective-permute-start.16 = (bf16[192,256]{1,0:T(8,128)(2,1)}, bf16[192,256]{1,0:T(8,128)(2,1)S(1)}, u32[]{:S(2)}, u32[]{:S(2)}) collective-permute-start(bf16[192,256]{1,0:T(8,128)(2,1)} %get-tuple-element.214), channel_id=1, source_target_pairs={{0,12},{4,8},{8,4},{12,0},{16,28},{20,24},{24,20},{28,16},{1,13},{... | collective-permute-start | bytes 294920 | tf_op jit(solution)/shard_map/ppermute | solution.py:693
  366.5 13.8 %collective-permute-start.15 = (bf16[192,256]{1,0:T(8,128)(2,1)}, bf16[192,256]{1,0:T(8,128)(2,1)S(1)}, u32[]{:S(2)}, u32[]{:S(2)}) collective-permute-start(bf16[192,256]{1,0:T(8,128)(2,1)} %get-tuple-element.215), channel_id=1, source_target_pairs={{0,8},{4,12},{8,0},{12,4},{16,24},{20,28},{24,16},{28,20},{1,9},{5... | collective-permute-start | bytes 294920 | tf_op jit(solution)/shard_map/ppermute | solution.py:693
  367.1 13.2 %collective-permute-start.14 = (bf16[192,256]{1,0:T(8,128)(2,1)}, bf16[192,256]{1,0:T(8,128)(2,1)S(1)}, u32[]{:S(2)}, u32[]{:S(2)}) collective-permute-start(bf16[192,256]{1,0:T(8,128)(2,1)} %get-tuple-element.213), channel_id=1, source_target_pairs={{0,4},{4,0},{8,12},{12,8},{16,20},{20,16},{24,28},{28,24},{1,5},{5... | collective-permute-start | bytes 294920 | tf_op jit(solution)/shard_map/ppermute | solution.py:693
  368.2 13.4 %collective-permute-start.11 = (bf16[192,640]{1,0:T(8,128)(2,1)S(1)}, bf16[192,640]{1,0:T(8,128)(2,1)S(1)}, u32[]{:S(2)}, u32[]{:S(2)}) collective-permute-start(bf16[192,640]{1,0:T(8,128)(2,1)S(1)} %fusion.15), channel_id=1, source_target_pairs={{0,2},{1,3},{2,0},{3,1},{4,6},{5,7},{6,4},{7,5},{8,10},{9,11},{10,... | collective-permute-start | bytes 737288 | tf_op jit(solution)/shard_map/ppermute | solution.py:693
  382.8 23.4 %collective-permute-start.17 = (bf16[192,896]{1,0:T(8,128)(2,1)S(1)}, bf16[192,896]{1,0:T(8,128)(2,1)S(1)}, u32[]{:S(2)}, u32[]{:S(2)}) collective-permute-start(bf16[192,896]{1,0:T(8,128)(2,1)S(1)} %pad_maximum_fusion), channel_id=1, source_target_pairs={{0,16},{4,20},{8,24},{12,28},{16,0},{20,4},{24,8},{28,12},{1,17},{... | collective-permute-start | bytes 1032200 | tf_op jit(solution)/shard_map/ppermute | solution.py:693
  406.3 9.9 %copy-start.11 = (bf16[192,896]{1,0:T(8,128)(2,1)}, bf16[192,896]{1,0:T(8,128)(2,1)S(1)}, u32[]{:S(2)}) copy-start(bf16[192,896]{1,0:T(8,128)(2,1)S(1)} %add_convert_fusion.3.refs_0_) | copy-start | bytes 1032196
  406.3 26.1 %collective-permute-start.18 = (bf16[192,896]{1,0:T(8,128)(2,1)S(1)}, bf16[192,896]{1,0:T(8,128)(2,1)S(1)}, u32[]{:S(2)}, u32[]{:S(2)}) collective-permute-start(bf16[192,896]{1,0:T(8,128)(2,1)S(1)} %add_convert_fusion.3.refs_0_), channel_id=1, source_target_pairs={{0,4},{4,0},{8,12},{12,8},{16,20},{20,16},{24,28},{28,24},{1,5},{5... | collective-permute-start | bytes 1032200 | tf_op jit(solution)/shard_map/ppermute | solution.py:693
  407.8 24.6 %collective-permute-start.19 = (bf16[192,896]{1,0:T(8,128)(2,1)S(1)}, bf16[192,896]{1,0:T(8,128)(2,1)}, u32[]{:S(2)}, u32[]{:S(2)}) collective-permute-start(bf16[192,896]{1,0:T(8,128)(2,1)S(1)} %add_convert_fusion.3.refs_0_), channel_id=1, source_target_pairs={{0,8},{4,12},{8,0},{12,4},{16,24},{20,28},{24,16},{28,20},{1,9},{5... | collective-permute-start | bytes 1032200 | tf_op jit(solution)/shard_map/ppermute | solution.py:693
  407.9 24.6 %collective-permute-start.20 = (bf16[192,896]{1,0:T(8,128)(2,1)S(1)}, bf16[192,896]{1,0:T(8,128)(2,1)}, u32[]{:S(2)}, u32[]{:S(2)}) collective-permute-start(bf16[192,896]{1,0:T(8,128)(2,1)S(1)} %add_convert_fusion.3.refs_0_), channel_id=1, source_target_pairs={{0,12},{4,8},{8,4},{12,0},{16,28},{20,24},{24,20},{28,16},{1,13},{... | collective-permute-start | bytes 1032200 | tf_op jit(solution)/shard_map/ppermute | solution.py:693
  425.0 11.4 %copy-start.1 = (s32[2,2048]{1,0:T(2,128)S(1)}, s32[2,2048]{1,0:T(2,128)}, u32[]{:S(2)}) copy-start(s32[2,2048]{1,0:T(2,128)} %param.15) | copy-start | bytes 49156
  (9 other events, 9.3 us)
Sparse Core Ops, SparseCore 0:
  13.3 73.7 all-gather.3
  88.7 65.7 all-gather.5
  156.0 30.7 all-gather.7
  254.7 151.8 reduce-scatter.1

commit v3 on v2

--- a/solution.py
+++ b/solution.py
@@ -221,7 +221,7 @@
 
 def pack_kernel(hg_ref, w_ref, o_ref, attn_ref, ffn_ref, bias_ref, b_ref, router_ref, out_ref, lines):
     part = o_ref.shape[0]
-    local, experts = b_ref.shape[0], router_ref.shape[1]
+    local, experts = b_ref.shape[0], router_ref.shape[0]
     width = (out_ref.shape[1] - D - 128) // 3
     pairs = width // 64
     out_ref[:, 0:D] = o_ref[...]
@@ -229,12 +229,8 @@
     lines[0:1, 0:part] = attn_ref[...].astype(F32)
     lines[1:2, 0:part] = ffn_ref[...].astype(F32)
     lines[B_ROW : B_ROW + local, 0:part] = b_ref[...].astype(F32)
-    turned = lines[...].T
-    column = lax.broadcasted_iota(jnp.int32, (part, 128), 1)
-    router = jnp.concatenate([router_ref[...], jnp.zeros((part, 128 - experts), BF)], 1)
-    router = pltpu.roll(router.astype(F32), ROUTER_ROW, 1)
-    narrow = jnp.where(column < ROUTER_ROW, turned[0:part], router)
-    out_ref[:, D : D + 128] = narrow.astype(BF)
+    lines[ROUTER_ROW : ROUTER_ROW + experts, 0:part] = router_ref[...].astype(F32)
+    out_ref[:, D : D + 128] = lines[...].T[0:part].astype(BF)
     for mine in range(D // width):
 
         @pl.when(hg_ref[0] == mine)
@@ -770,7 +766,7 @@
         [shape((part, D + 128 + 3 * width), BF)],
         (
             scalar(head_group), w_qkv, w_o, norm_attn[None], norm_ffn[None], rel_bias, b_out,
-            router,
+            router.T,
         ),
         1e9,
         scratch=[pltpu.VMEM((128, 256), F32)],
@@ -927,7 +923,7 @@
     block = jnp.concatenate([grad_qkv, mixed], 1)
     bit = per_group
     while bit < slabs:
-        block = add(block, swap(block, "seq", bit))
+        block = add(after(block, output), swap(block, "seq", bit))
         bit *= 2
     blocks = [block] + [swap(block, "seq", k) for k in range(1, per_group)]
     big = after(big, grad_tokens)

time: 450 us -> 444 us (0.987)
  waiting for transfers between devices: 122 us -> 116 us
    ppermute x21, waiting for transfers between devices: 72.7 us -> 67 us  [swap(): return lax.ppermute(array, axis, [(i, i ^ bit) for i in range(size)])]
  transfers between devices with their start and end apart: 33 -> 33, of which waited for: 16 -> 16; matrix products, arithmetic and copies ran while one was open for 5% -> 5% of each run, Pallas kernels for 36% -> 37%
where the time goes in v3:
time: 444 us; the launch traced here: 437 us
  Pallas kernels  164 us (37%)
  waiting for transfers between devices  116 us (26%)
  starting transfers between devices  62.8 us (14%)
  blocking collectives  46.8 us (11%)
  local copies, waits for them, and re-layouts  23.1 us (5%)
  between operations  14.6 us (3%)
  other arithmetic  9.92 us (2%)
    ppermute x21, waiting for transfers between devices, swap(): return lax.ppermute(array, axis, [(i, i ^ bit) for i in range(size)])  67 us
    pallas_call x10, Pallas kernels, one_step(): pl.pallas_call(kernel, out_shape=tuple(outs), in_specs=[pl.BlockSpec(memo...  57.8 us
    all_to_all x8, waiting for transfers between devices, exchange(): return lax.all_to_all(array, 'seq', split_axis=0, concat_axis=0, tiled=True)  47.6 us
    all_to_all x2, blocking collectives, exchange(): return lax.all_to_all(array, 'seq', split_axis=0, concat_axis=0, tiled=True)  46.8 us
    all_to_all x8, starting transfers between devices, exchange(): return lax.all_to_all(array, 'seq', split_axis=0, concat_axis=0, tiled=True)  37.6 us
    pallas_call x2, Pallas kernels, expert_pass(): pl.pallas_call(functools.partial(expert_kernel, index=index, local=local,...  37 us
    ppermute x21, starting transfers between devices, swap(): return lax.ppermute(array, axis, [(i, i ^ bit) for i in range(size)])  25 us
    pallas_call x1, Pallas kernels, attention_bwd(): pl.pallas_call(bwd_kernel, grid=(pairs,), out_shape=(shape(qkv.shape, BF)...  23.3 us
  transfers between devices with their start and end apart: 33, of which 16 were waited for; matrix products, arithmetic and copies ran while one was open for 5% of the time, Pallas kernels for 37%

profile of v3, /device:TPU:0, one launch (start us, length us, event | category | flops | bytes accessed | tf_op | source)
XLA Modules:
  0.0 437.1 jit_solution(11253832244426326989)
XLA Ops:
  7.2 3.0 copy_bitcast_fusion
  10.7 2.5 fusion.18
  15.1 2.3 shard_map.212.refs_0_
  17.4 3.0 collective-permute-start
  20.5 2.7 collective-permute-start.3
  26.6 13.9 %collective-permute-done.3.refs_1_ = bf16[256,768]{1,0:T(8,128)(2,1)S(1)} collective-permute-done((bf16[256,768]{1,0:T(8,128)(2,1)S(1)}, bf16[256,768]{1,0:T(8,128)(2,1)S(1)}, u32[]{:S(2)}, u32[]{:S(2)}) %collective-permute-start.3) | collective-permute-done | bytes 393248 | tf_op jit(solution)/shard_map/ppermute | solution.py:689
  41.8 2.2 collective-permute-done.5.refs_3_
  44.0 6.3 %collective-permute-done.6.refs_4_ = bf16[256,768]{1,0:T(8,128)(2,1)S(1)} collective-permute-done((bf16[256,768]{1,0:T(8,128)(2,1)S(1)}, bf16[256,768]{1,0:T(8,128)(2,1)S(1)}, u32[]{:S(2)}, u32[]{:S(2)}) %collective-permute-start.6) | collective-permute-done | bytes 393248 | tf_op jit(solution)/shard_map/ppermute | solution.py:689
  52.8 1.8 collective-permute-start.9
  55.6 4.6 %shard_map.213 = (bf16[768,576]{1,0:T(8,128)(2,1)}, bf16[768,768]{1,0:T(8,128)(2,1)}, f32[128,768]{1,0:T(8,128)}, f32[3,384,256]{2,1,0:T(8,128)}) custom-call(s32[1]{0:T(128)} %bitcast.me_ref, bf16[192,1472]{1,0:T(8,128)(2,1)} %shard_map.212.refs_0_, bf16[192,1472]{1,0:T(8,128)(2,1)} %copy-done.12, bf16[192,1472]{1,0:T(8,128)(2,1)} %copy-done.13, ...), custom_call_target="tpu_custom_call" | custom-call | flops 60000000 | bytes 117964 | tf_op jit(solution)/shard_map/pallas_call | solution.py:207
  60.2 2.0 collective-permute-done.7.refs_5_
  64.7 4.3 shard_map.214
  70.0 2.8 fusion.2
  72.8 5.3 %all-to-all-start = ((bf16[8,152,768]{2,1,0:T(8,128)(2,1)}), bf16[8,152,768]{2,1,0:T(8,128)(2,1)S(1)}, u32[]{:S(2)}, u32[]{:S(2)}) async-start(bf16[8,152,768]{2,1,0:T(8,128)(2,1)} %fusion.2), calls=%async_computation | async-start | bytes 3735552 | tf_op jit(solution)/shard_map/all_to_all | solution.py:702
  78.8 7.1 %shard_map.215 = (bf16[8,576,256]{2,1,0:T(8,128)(2,1)}, bf16[8,256,768]{2,1,0:T(8,128)(2,1)}) custom-call(s32[1]{0:T(128)} %bitcast.9.me_ref.own_ref, f32[128,768]{1,0:T(8,128)} %get-tuple-element.86.small_ref, bf16[768,576]{1,0:T(8,128)(2,1)} %get-tuple-element.91.w_ref, bf16[256,768]{1,0:T(8,128)(2,1)} %copy-done.10, bf16[256,768]{1,0:T(8,128)(2,1)} %copy-done.15, ...), custom_call_target="tpu_custom_call" | custom-call | flops 72477576 | bytes 198574 | tf_op jit(solution)/shard_map/pallas_call | solution.py:207
  85.9 16.5 %shard_map.216 = (bf16[8,192,256]{2,1,0:T(8,128)(2,1)}, f32[3,64,2048]{2,1,0:T(8,128)}, f32[3,1,2048]{2,1,0:T(1,128)}) custom-call(bf16[8,576,256]{2,1,0:T(8,128)(2,1)} %get-tuple-element.92.qkv_ref, s32[1,2048]{1,0:T(1,128)} %constant_dynamic-slice_fusion.3.seg_ref, f32[3,384,256]{2,1,0:T(8,128)} %get-tuple-element.93.band_ref), custom_call_target="tpu_custom_call" | custom-call | flops 17999998976 | bytes 6000000 | tf_op jit(solution)/shard_map/pallas_call | solution.py:154
  102.4 14.7 %all-to-all-done = bf16[8,152,768]{2,1,0:T(8,128)(2,1)S(1)} async-done(((bf16[8,152,768]{2,1,0:T(8,128)(2,1)}), bf16[8,152,768]{2,1,0:T(8,128)(2,1)S(1)}, u32[]{:S(2)}, u32[]{:S(2)}) %all-to-all-start) | async-done | bytes 1867808 | tf_op jit(solution)/shard_map/all_to_all | solution.py:702
  117.1 22.9 %all_to_all.50.chunk_ref.att_ref = bf16[8,192,256]{2,1,0:T(8,128)(2,1)} all-to-all(bf16[8,192,256]{2,1,0:T(8,128)(2,1)} %get-tuple-element.99), channel_id=1, replica_groups=mesh['seq'=8,'fsdp'=4] {'seq'}, dimensions={0} | all-to-all | bytes 1572864 | tf_op jit(solution)/shard_map/all_to_all | solution.py:702
  140.0 5.0 %shard_map.217 = (f32[512,768]{1,0:T(8,128)}, f32[512,2]{1,0:T(8,128)}, bf16[576,768]{1,0:T(8,128)(2,1)}, bf16[576,768]{1,0:T(8,128)(2,1)}) custom-call(bf16[2,256,768]{2,1,0:T(8,128)(2,1)} %tok_ref.3, f32[128,768]{1,0:T(8,128)} %get-tuple-element.86.small_ref, bf16[768,768]{1,0:T(8,128)(2,1)} %get-tuple-element.87.w_ref, s32[512,2]{1,0:T(8,128)} %bitcast.65, ...), custom_call_target="tpu_custom_call" | custom-call | flops 60397976 | bytes 130007 | tf_op jit(solution)/shard_map/pallas_call | solution.py:207
  145.1 3.6 all-to-all-start.2
  151.2 19.4 %all-to-all-done.2 = bf16[8,72,768]{2,1,0:T(8,128)(2,1)S(1)} async-done(((bf16[8,72,768]{2,1,0:T(8,128)(2,1)}), bf16[8,72,768]{2,1,0:T(8,128)(2,1)S(1)}, u32[]{:S(2)}, u32[]{:S(2)}) %all-to-all-start.2) | async-done | bytes 884768 | tf_op jit(solution)/shard_map/all_to_all | solution.py:702
  170.6 4.4 %all-to-all-start.3 = ((bf16[8,72,768]{2,1,0:T(8,128)(2,1)}), bf16[8,72,768]{2,1,0:T(8,128)(2,1)}, u32[]{:S(2)}, u32[]{:S(2)}) async-start(bf16[8,72,768]{2,1,0:T(8,128)(2,1)} %bitcast.82), calls=%async_computation.3 | async-start | bytes 1769472 | tf_op jit(solution)/shard_map/all_to_all | solution.py:702
  176.4 18.5 %shard_map.218 = (bf16[576,768]{1,0:T(8,128)(2,1)}, bf16[576,768]{1,0:T(8,128)(2,1)}, bf16[16,576]{1,0:T(8,128)(2,1)}, bf16[576,768]{1,0:T(8,128)(2,1)}, bf16[4,...) custom-call(s32[1]{0:T(128)} %bitcast.9.me_ref.own_ref, bf16[576,768]{1,0:T(8,128)(2,1)} %bitcast.72, ...), custom_call_target="tpu_custom_call" | custom-call | flops 13589544960 | bytes 28311552 | tf_op jit(solution)/shard_map/pallas_call | solution.py:595
  194.8 2.0 all-to-all-done.3
  196.9 4.0 all-to-all-start.4
  200.9 18.5 %shard_map.219 = (bf16[576,768]{1,0:T(8,128)(2,1)}, bf16[576,768]{1,0:T(8,128)(2,1)}, bf16[16,576]{1,0:T(8,128)(2,1)}, bf16[576,768]{1,0:T(8,128)(2,1)}, bf16[4,...) custom-call(s32[1]{0:T(128)} %bitcast.9.me_ref.own_ref, ...), custom_call_target="tpu_custom_call" | custom-call | flops 13589544960 | bytes 28311552 | tf_op jit(solution)/shard_map/pallas_call | solution.py:595
  221.0 2.2 fusion.3
  223.2 6.0 %all-to-all-start.5 = ((bf16[8,80,768]{2,1,0:T(8,128)(2,1)}), bf16[8,80,768]{2,1,0:T(8,128)(2,1)S(1)}, u32[]{:S(2)}, u32[]{:S(2)}) async-start(bf16[8,80,768]{2,1,0:T(8,128)(2,1)} %fusion.3), calls=%async_computation.5 | async-start | bytes 1966080 | tf_op jit(solution)/shard_map/all_to_all | solution.py:702
  229.2 21.9 %shard_map.220 = bf16[4,2,2,768,768]{4,3,2,1,0:T(8,128)(2,1)} custom-call(bf16[576,768]{1,0:T(8,128)(2,1)} %bitcast.73, bf16[576,768]{1,0:T(8,128)(2,1)} %get-tuple-element.115.refs_1_, bf16[4,576,768]{2,1,0:T(8,128)(2,1)} %get-tuple-element.117.refs_2_, bf16[4,576,768]{2,1,0:T(8,128)(2,1)} %get-tuple-element.118.refs_3_, ...), custom_call_target="tpu_custom_call" | custom-call | flops 1000000 | bytes 1000000 | tf_op jit(solution)/shard_map/pallas_call | solution.py:645
  253.8 4.5 %all-to-all-start.6 = ((bf16[8,72,768]{2,1,0:T(8,128)(2,1)}), bf16[8,72,768]{2,1,0:T(8,128)(2,1)S(1)}, u32[]{:S(2)}, u32[]{:S(2)}) async-start(bf16[8,72,768]{2,1,0:T(8,128)(2,1)} %bitcast.30), calls=%async_computation.6 | async-start | bytes 1769472 | tf_op jit(solution)/shard_map/all_to_all | solution.py:702
  259.2 11.1 %shard_map.221 = (f32[512,768]{1,0:T(8,128)}, bf16[8,192,256]{2,1,0:T(8,128)(2,1)}, bf16[2,192,1024]{2,1,0:T(8,128)(2,1)}, bf16[2,192,1024]{2,1,0:T(8,128)(2,1)}) custom-call(s32[1]{0:T(128)} %bitcast.me_ref, f32[1,1152]{1,0:T(1,128)} %reshape.183.dgate_ref, s32[512,2]{1,0:T(8,128)} %get-tuple-element.113.slot_ref, s32[512,2]{1,0:T(8,128)} %bitcast.66, ...), custom_call_target="tpu_custom_call" | custom-call | flops 84557168 | bytes 208865 | tf_op jit(solution)/shard_map/pallas_call | solution.py:207
  270.3 9.8 %all-to-all-done.6 = bf16[8,72,768]{2,1,0:T(8,128)(2,1)S(1)} async-done(((bf16[8,72,768]{2,1,0:T(8,128)(2,1)}), bf16[8,72,768]{2,1,0:T(8,128)(2,1)S(1)}, u32[]{:S(2)}, u32[]{:S(2)}) %all-to-all-start.6) | async-done | bytes 884768 | tf_op jit(solution)/shard_map/all_to_all | solution.py:702
  280.1 23.8 %all_to_all.51.do_ref = bf16[8,192,256]{2,1,0:T(8,128)(2,1)} all-to-all(bf16[8,192,256]{2,1,0:T(8,128)(2,1)} %get-tuple-element.130), channel_id=1, replica_groups=mesh['seq'=8,'fsdp'=4] {'seq'}, dimensions={0} | all-to-all | bytes 1572864 | tf_op jit(solution)/shard_map/all_to_all | solution.py:702
  303.9 3.6 all-to-all-start.8
  307.5 23.3 %shard_map.222 = (bf16[8,576,256]{2,1,0:T(8,128)(2,1)}, f32[3,384,256]{2,1,0:T(8,128)}) custom-call(bf16[8,576,256]{2,1,0:T(8,128)(2,1)} %get-tuple-element.92.qkv_ref, s32[1,2048]{1,0:T(1,128)} %constant_dynamic-slice_fusion.3.seg_ref, f32[3,384,256]{2,1,0:T(8,128)} %get-tuple-element.93.band_ref, f32[3,64,2048]{2,1,0:T(8,128)} %get-tuple-element.101.wide_ref, ...), custom_call_target="tpu_custom_call" | custom-call | flops 30000001024 | bytes 9000000 | tf_op jit(solution)/shard_map/pallas_call | solution.py:179
  331.7 6.3 %all-to-all-start.9 = ((bf16[8,576,256]{2,1,0:T(8,128)(2,1)}), bf16[8,576,256]{2,1,0:T(8,128)(2,1)S(1)}, u32[]{:S(2)}, u32[]{:S(2)}) async-start(bf16[8,576,256]{2,1,0:T(8,128)(2,1)} %get-tuple-element.137.d_ref), calls=%async_computation.9 | async-start | bytes 4718592 | tf_op jit(solution)/shard_map/all_to_all | solution.py:702
  338.1 2.3 collective-permute-done.12
  342.4 7.0 %shard_map.224 = (bf16[2,192,640]{2,1,0:T(8,128)(2,1)}, bf16[2,192,640]{2,1,0:T(8,128)(2,1)}) custom-call(s32[1]{0:T(128)} %bitcast.me_ref, bf16[8,256,768]{2,1,0:T(8,128)(2,1)} %get-tuple-element.138.first_ref, bf16[8,576,256]{2,1,0:T(8,128)(2,1)} %get-tuple-element.137.d_ref, f32[3,384,256]{2,1,0:T(8,128)} %get-tuple-element.139.band_ref), custom_call_target="tpu_custom_call" | custom-call | flops 72477576 | bytes 153354 | tf_op jit(solution)/shard_map/pallas_call | solution.py:207
  349.4 12.6 %collective-permute-done.13 = bf16[192,1024]{1,0:T(8,128)(2,1)S(1)} collective-permute-done((bf16[192,1024]{1,0:T(8,128)(2,1)S(1)}, bf16[192,1024]{1,0:T(8,128)(2,1)S(1)}, u32[]{:S(2)}, u32[]{:S(2)}) %collective-permute-start.13) | collective-permute-done | bytes 393248 | tf_op jit(solution)/shard_map/ppermute | solution.py:689
  362.8 3.0 collective-permute-start.16
  368.1 10.4 %collective-permute-done.16 = bf16[192,256]{1,0:T(8,128)(2,1)S(1)} collective-permute-done((bf16[192,256]{1,0:T(8,128)(2,1)}, bf16[192,256]{1,0:T(8,128)(2,1)S(1)}, u32[]{:S(2)}, u32[]{:S(2)}) %collective-permute-start.16) | collective-permute-done | bytes 98336 | tf_op jit(solution)/shard_map/ppermute | solution.py:689
  382.1 4.0 collective-permute-start.17
  386.1 5.7 %shard_map.223 = bf16[512,768]{1,0:T(8,128)(2,1)} custom-call(f32[512,768]{1,0:T(8,128)} %get-tuple-element.132.mid_ref, s32[512,2]{1,0:T(8,128)} %get-tuple-element.113.slot_ref, f32[512,2]{1,0:T(8,128)} %get-tuple-element.114.gate_ref, bf16[576,768]{1,0:T(8,128)(2,1)} %bitcast.70, bf16[576,768]{1,0:T(8,128)(2,1)} %bitcast.71), custom_call_target="tpu_custom_call" | custom-call | flops 36238784 | bytes 82739 | tf_op jit(solution)/shard_map/pallas_call | solution.py:207
  391.8 13.7 %collective-permute-done.17 = bf16[192,896]{1,0:T(8,128)(2,1)S(1)} collective-permute-done((bf16[192,896]{1,0:T(8,128)(2,1)S(1)}, bf16[192,896]{1,0:T(8,128)(2,1)S(1)}, u32[]{:S(2)}, u32[]{:S(2)}) %collective-permute-start.17) | collective-permute-done | bytes 344096 | tf_op jit(solution)/shard_map/ppermute | solution.py:689
  407.1 2.0 collective-permute-start.20
  411.3 7.4 %shard_map.225 = f32[2,256,768]{2,1,0:T(8,128)} custom-call(bf16[2,256,768]{2,1,0:T(8,128)(2,1)} %tok_ref.3, f32[128,768]{1,0:T(8,128)} %get-tuple-element.86.small_ref, bf16[768,2304]{1,0:T(8,128)(2,1)} %all-gather.8.cloned.1.call-done.w_ref, f32[512,768]{1,0:T(8,128)} %get-tuple-element.136.dmid_ref, bf16[8,576,256]{2,1,0:T(8,128)(2,1)} %copy-done.3), custom_call_target="tpu_custom_call" | custom-call | flops 72477576 | bytes 204472 | tf_op jit(solution)/shard_map/pallas_call | solution.py:207
  418.7 7.4 %shard_map.226 = (f32[768,2,768]{2,1,0:T(2,128)}, f32[768,2,768]{2,1,0:T(2,128)}) custom-call(bf16[2,2,768,768]{3,2,1,0:T(8,128)(2,1)} %bitcast.67), custom_call_target="tpu_custom_call" | custom-call | flops 1000000 | bytes 1000000 | tf_op jit(solution)/shard_map/pallas_call | solution.py:672
  426.8 3.3 shard_map.227
  (130 shorter events, 38.0 us)
Async XLA Ops:
  7.2 71.0 %copy-start = (s32[2,2048]{1,0:T(2,128)S(1)}, s32[2,2048]{1,0:T(2,128)}, u32[]{:S(2)}) copy-start(s32[2,2048]{1,0:T(2,128)} %param.15) | copy-start | bytes 49156
  7.2 169.2 %all-gather.4.cloned.1.call-start = ((), (), s32[]{:S(2)}) async-start(), calls=%async_computation.11 | async-start | bytes 11796480 | tf_op jit(solution)/shard_map/all_gather | solution.py:840
  13.2 7.2 %copy-start.4 = (bf16[2,256,768]{2,1,0:T(8,128)(2,1)S(1)}, bf16[2,256,768]{2,1,0:T(8,128)(2,1)}, u32[]{:S(2)}) copy-start(bf16[2,256,768]{2,1,0:T(8,128)(2,1)} %tok_ref.3) | copy-start | bytes 2359300
  13.2 187.7 %all-gather.6.cloned.1.call-start = ((), (), s32[]{:S(2)}) async-start(), calls=%async_computation.12 | async-start | bytes 11796480 | tf_op jit(solution)/shard_map/all_gather | solution.py:840
  17.4 24.4 %collective-permute-start = (bf16[192,1472]{1,0:T(8,128)(2,1)}, bf16[192,1472]{1,0:T(8,128)(2,1)S(1)}, u32[]{:S(2)}, u32[]{:S(2)}) collective-permute-start(bf16[192,1472]{1,0:T(8,128)(2,1)} %shard_map.212.refs_0_), channel_id=1, source_target_pairs={{0,2},{1,3},{2,0},{3,1},{4,6},{5,7},{6,4},{7,5},{8,10},{9,11},{10,... | collective-permute-start | bytes 1695752 | tf_op jit(solution)/shard_map/ppermute | solution.py:689
  20.4 48.6 %copy-start.10 = (bf16[256,768]{1,0:T(8,128)(2,1)}, bf16[256,768]{1,0:T(8,128)(2,1)S(1)}, u32[]{:S(2)}) copy-start(bf16[256,768]{1,0:T(8,128)(2,1)S(1)} %get-tuple-element.213.refs_0_) | copy-start | bytes 1179652
  20.5 20.1 %collective-permute-start.3 = (bf16[256,768]{1,0:T(8,128)(2,1)S(1)}, bf16[256,768]{1,0:T(8,128)(2,1)S(1)}, u32[]{:S(2)}, u32[]{:S(2)}) collective-permute-start(bf16[256,768]{1,0:T(8,128)(2,1)S(1)} %get-tuple-element.214), channel_id=1, source_target_pairs={{0,16},{4,20},{8,24},{12,28},{16,0},{20,4},{24,8},{28,12},{1,17},{... | collective-permute-start | bytes 1179656 | tf_op jit(solution)/shard_map/ppermute | solution.py:689
  23.1 18.7 %collective-permute-start.4 = (bf16[256,768]{1,0:T(8,128)(2,1)S(1)}, bf16[256,768]{1,0:T(8,128)(2,1)S(1)}, u32[]{:S(2)}, u32[]{:S(2)}) collective-permute-start(bf16[256,768]{1,0:T(8,128)(2,1)S(1)} %get-tuple-element.213.refs_0_), channel_id=1, source_target_pairs={{0,4},{4,0},{8,12},{12,8},{16,20},{20,16},{24,28},{28,24},{1,5},{5... | collective-permute-start | bytes 1179656 | tf_op jit(solution)/shard_map/ppermute | solution.py:689
  24.6 19.4 %collective-permute-start.5 = (bf16[256,768]{1,0:T(8,128)(2,1)S(1)}, bf16[256,768]{1,0:T(8,128)(2,1)S(1)}, u32[]{:S(2)}, u32[]{:S(2)}) collective-permute-start(bf16[256,768]{1,0:T(8,128)(2,1)S(1)} %get-tuple-element.213.refs_0_), channel_id=1, source_target_pairs={{0,8},{4,12},{8,0},{12,4},{16,24},{20,28},{24,16},{28,20},{1,9},{5... | collective-permute-start | bytes 1179656 | tf_op jit(solution)/shard_map/ppermute | solution.py:689
  26.2 24.1 %collective-permute-start.6 = (bf16[256,768]{1,0:T(8,128)(2,1)S(1)}, bf16[256,768]{1,0:T(8,128)(2,1)S(1)}, u32[]{:S(2)}, u32[]{:S(2)}) collective-permute-start(bf16[256,768]{1,0:T(8,128)(2,1)S(1)} %get-tuple-element.213.refs_0_), channel_id=1, source_target_pairs={{0,12},{4,8},{8,4},{12,0},{16,28},{20,24},{24,20},{28,16},{1,13},{... | collective-permute-start | bytes 1179656 | tf_op jit(solution)/shard_map/ppermute | solution.py:689
  40.5 38.3 %copy-start.15 = (bf16[256,768]{1,0:T(8,128)(2,1)}, bf16[256,768]{1,0:T(8,128)(2,1)S(1)}, u32[]{:S(2)}) copy-start(bf16[256,768]{1,0:T(8,128)(2,1)S(1)} %collective-permute-done.3.refs_1_) | copy-start | bytes 1179652
  40.5 14.0 %collective-permute-start.1 = (bf16[192,1472]{1,0:T(8,128)(2,1)}, bf16[192,1472]{1,0:T(8,128)(2,1)S(1)}, u32[]{:S(2)}, u32[]{:S(2)}) collective-permute-start(bf16[192,1472]{1,0:T(8,128)(2,1)} %shard_map.212.refs_0_), channel_id=1, source_target_pairs={{0,1},{1,0},{2,3},{3,2},{4,5},{5,4},{6,7},{7,6},{8,9},{9,8},{10,11... | collective-permute-start | bytes 1695752 | tf_op jit(solution)/shard_map/ppermute | solution.py:689
  41.8 12.8 %copy-start.12 = (bf16[192,1472]{1,0:T(8,128)(2,1)}, bf16[192,1472]{1,0:T(8,128)(2,1)S(1)}, u32[]{:S(2)}) copy-start(bf16[192,1472]{1,0:T(8,128)(2,1)S(1)} %collective-permute-done.refs_1_) | copy-start | bytes 1695748
  41.8 12.8 %collective-permute-start.2 = (bf16[192,1472]{1,0:T(8,128)(2,1)S(1)}, bf16[192,1472]{1,0:T(8,128)(2,1)S(1)}, u32[]{:S(2)}, u32[]{:S(2)}) collective-permute-start(bf16[192,1472]{1,0:T(8,128)(2,1)S(1)} %collective-permute-done.refs_1_), channel_id=1, source_target_pairs={{0,1},{1,0},{2,3},{3,2},{4,5},{5,4},{6,7},{7,6},{8,9},{9,8},{10,11... | collective-permute-start | bytes 1695752 | tf_op jit(solution)/shard_map/ppermute | solution.py:689
  41.8 37.0 %copy-start.16 = (bf16[256,768]{1,0:T(8,128)(2,1)}, bf16[256,768]{1,0:T(8,128)(2,1)S(1)}, u32[]{:S(2)}) copy-start(bf16[256,768]{1,0:T(8,128)(2,1)S(1)} %collective-permute-done.4.refs_2_) | copy-start | bytes 1179652
  44.0 34.8 %copy-start.17 = (bf16[256,768]{1,0:T(8,128)(2,1)}, bf16[256,768]{1,0:T(8,128)(2,1)S(1)}, u32[]{:S(2)}) copy-start(bf16[256,768]{1,0:T(8,128)(2,1)S(1)} %collective-permute-done.5.refs_3_) | copy-start | bytes 1179652
  51.1 11.1 %collective-permute-start.7 = (bf16[256,768]{1,0:T(8,128)(2,1)S(1)}, bf16[256,768]{1,0:T(8,128)(2,1)}, u32[]{:S(2)}, u32[]{:S(2)}) collective-permute-start(bf16[256,768]{1,0:T(8,128)(2,1)S(1)} %collective-permute-done.3.refs_1_), channel_id=1, source_target_pairs={{0,4},{4,0},{8,12},{12,8},{16,20},{20,16},{24,28},{28,24},{1,5},{5... | collective-permute-start | bytes 1179656 | tf_op jit(solution)/shard_map/ppermute | solution.py:689
  52.6 20.2 %collective-permute-start.8 = (bf16[256,768]{1,0:T(8,128)(2,1)S(1)}, bf16[256,768]{1,0:T(8,128)(2,1)}, u32[]{:S(2)}, u32[]{:S(2)}) collective-permute-start(bf16[256,768]{1,0:T(8,128)(2,1)S(1)} %collective-permute-done.3.refs_1_), channel_id=1, source_target_pairs={{0,8},{4,12},{8,0},{12,4},{16,24},{20,28},{24,16},{28,20},{1,9},{5... | collective-permute-start | bytes 1179656 | tf_op jit(solution)/shard_map/ppermute | solution.py:689
  52.8 20.1 %collective-permute-start.9 = (bf16[256,768]{1,0:T(8,128)(2,1)S(1)}, bf16[256,768]{1,0:T(8,128)(2,1)}, u32[]{:S(2)}, u32[]{:S(2)}) collective-permute-start(bf16[256,768]{1,0:T(8,128)(2,1)S(1)} %collective-permute-done.3.refs_1_), channel_id=1, source_target_pairs={{0,12},{4,8},{8,4},{12,0},{16,28},{20,24},{24,20},{28,16},{1,13},{... | collective-permute-start | bytes 1179656 | tf_op jit(solution)/shard_map/ppermute | solution.py:689
  63.0 1.7 copy-start.2
  63.3 1.4 copy-start.9
  72.8 44.2 %all-to-all-start = ((bf16[8,152,768]{2,1,0:T(8,128)(2,1)}), bf16[8,152,768]{2,1,0:T(8,128)(2,1)S(1)}, u32[]{:S(2)}, u32[]{:S(2)}) async-start(bf16[8,152,768]{2,1,0:T(8,128)(2,1)} %fusion.2), calls=%async_computation | async-start | bytes 3735552 | tf_op jit(solution)/shard_map/all_to_all | solution.py:702
  145.1 25.5 %all-to-all-start.2 = ((bf16[8,72,768]{2,1,0:T(8,128)(2,1)}), bf16[8,72,768]{2,1,0:T(8,128)(2,1)S(1)}, u32[]{:S(2)}, u32[]{:S(2)}) async-start(bf16[8,72,768]{2,1,0:T(8,128)(2,1)} %bitcast.84), calls=%async_computation.2 | async-start | bytes 1769472 | tf_op jit(solution)/shard_map/all_to_all | solution.py:702
  148.6 261.3 %all-gather.8.cloned.1.call-start = ((), (), s32[]{:S(2)}) async-start(), calls=%async_computation.13 | async-start | bytes 4423680 | tf_op jit(solution)/shard_map/all_gather | solution.py:843
  170.6 5.8 %copy-start.8 = (bf16[8,72,768]{2,1,0:T(8,128)(2,1)}, bf16[8,72,768]{2,1,0:T(8,128)(2,1)S(1)}, u32[]{:S(2)}) copy-start(bf16[8,72,768]{2,1,0:T(8,128)(2,1)S(1)} %all-to-all-done.2) | copy-start | bytes 2654212
  170.6 26.3 %all-to-all-start.3 = ((bf16[8,72,768]{2,1,0:T(8,128)(2,1)}), bf16[8,72,768]{2,1,0:T(8,128)(2,1)}, u32[]{:S(2)}, u32[]{:S(2)}) async-start(bf16[8,72,768]{2,1,0:T(8,128)(2,1)} %bitcast.82), calls=%async_computation.3 | async-start | bytes 1769472 | tf_op jit(solution)/shard_map/all_to_all | solution.py:702
  196.9 26.3 %all-to-all-start.4 = ((bf16[8,72,768]{2,1,0:T(8,128)(2,1)}), bf16[8,72,768]{2,1,0:T(8,128)(2,1)S(1)}, u32[]{:S(2)}, u32[]{:S(2)}) async-start(bf16[8,72,768]{2,1,0:T(8,128)(2,1)} %bitcast.83), calls=%async_computation.4 | async-start | bytes 1769472 | tf_op jit(solution)/shard_map/all_to_all | solution.py:702
  223.2 27.9 %copy-start.5 = (bf16[8,72,768]{2,1,0:T(8,128)(2,1)}, bf16[8,72,768]{2,1,0:T(8,128)(2,1)S(1)}, u32[]{:S(2)}) copy-start(bf16[8,72,768]{2,1,0:T(8,128)(2,1)S(1)} %all-to-all-done.4) | copy-start | bytes 2654212
  223.2 29.6 %all-to-all-start.5 = ((bf16[8,80,768]{2,1,0:T(8,128)(2,1)}), bf16[8,80,768]{2,1,0:T(8,128)(2,1)S(1)}, u32[]{:S(2)}, u32[]{:S(2)}) async-start(bf16[8,80,768]{2,1,0:T(8,128)(2,1)} %fusion.3), calls=%async_computation.5 | async-start | bytes 1966080 | tf_op jit(solution)/shard_map/all_to_all | solution.py:702
  229.2 189.5 %reduce-scatter.2.cloned.1.call-start = ((), (), s32[]{:S(2)}) async-start(), calls=%async_computation.14 | async-start | bytes 23592960 | tf_op jit(solution)/shard_map/reduce_scatter | solution.py:870
  253.8 26.3 %all-to-all-start.6 = ((bf16[8,72,768]{2,1,0:T(8,128)(2,1)}), bf16[8,72,768]{2,1,0:T(8,128)(2,1)S(1)}, u32[]{:S(2)}, u32[]{:S(2)}) async-start(bf16[8,72,768]{2,1,0:T(8,128)(2,1)} %bitcast.30), calls=%async_computation.6 | async-start | bytes 1769472 | tf_op jit(solution)/shard_map/all_to_all | solution.py:702
  280.1 50.7 %copy-start.6 = (bf16[8,72,768]{2,1,0:T(8,128)(2,1)}, bf16[8,72,768]{2,1,0:T(8,128)(2,1)S(1)}, u32[]{:S(2)}) copy-start(bf16[8,72,768]{2,1,0:T(8,128)(2,1)S(1)} %all-to-all-done.6) | copy-start | bytes 2654212
  303.9 26.9 %all-to-all-start.8 = ((bf16[8,72,768]{2,1,0:T(8,128)(2,1)}), bf16[8,72,768]{2,1,0:T(8,128)(2,1)S(1)}, u32[]{:S(2)}, u32[]{:S(2)}) async-start(bf16[8,72,768]{2,1,0:T(8,128)(2,1)} %bitcast.32), calls=%async_computation.8 | async-start | bytes 1769472 | tf_op jit(solution)/shard_map/all_to_all | solution.py:702
  330.8 7.2 %copy-start.20 = (bf16[2,192,1024]{2,1,0:T(8,128)(2,1)S(1)}, bf16[2,192,1024]{2,1,0:T(8,128)(2,1)}, u32[]{:S(2)}) copy-start(bf16[2,192,1024]{2,1,0:T(8,128)(2,1)} %get-tuple-element.145) | copy-start | bytes 2359300
  331.7 78.2 %all-to-all-start.9 = ((bf16[8,576,256]{2,1,0:T(8,128)(2,1)}), bf16[8,576,256]{2,1,0:T(8,128)(2,1)S(1)}, u32[]{:S(2)}, u32[]{:S(2)}) async-start(bf16[8,576,256]{2,1,0:T(8,128)(2,1)} %get-tuple-element.137.d_ref), calls=%async_computation.9 | async-start | bytes 4718592 | tf_op jit(solution)/shard_map/all_to_all | solution.py:702
  338.0 2.4 collective-permute-start.12
  341.8 20.2 %collective-permute-start.13 = (bf16[192,1024]{1,0:T(8,128)(2,1)S(1)}, bf16[192,1024]{1,0:T(8,128)(2,1)S(1)}, u32[]{:S(2)}, u32[]{:S(2)}) collective-permute-start(bf16[192,1024]{1,0:T(8,128)(2,1)S(1)} %get-tuple-element.212), channel_id=1, source_target_pairs={{0,2},{1,3},{2,0},{3,1},{4,6},{5,7},{6,4},{7,5},{8,10},{9,11},{10,... | collective-permute-start | bytes 1179656 | tf_op jit(solution)/shard_map/ppermute | solution.py:689
  349.4 17.0 %collective-permute-start.10 = (bf16[2,192,640]{2,1,0:T(8,128)(2,1)}, bf16[2,192,640]{2,1,0:T(8,128)(2,1)}, u32[]{:S(2)}, u32[]{:S(2)}) collective-permute-start(bf16[2,192,640]{2,1,0:T(8,128)(2,1)} %get-tuple-element.142), channel_id=1, source_target_pairs={{0,1},{1,0},{2,3},{3,2},{4,5},{5,4},{6,7},{7,6},{8,9},{9,8},{10,11... | collective-permute-start | bytes 1474568 | tf_op jit(solution)/shard_map/ppermute | solution.py:689
  362.8 15.7 %collective-permute-start.16 = (bf16[192,256]{1,0:T(8,128)(2,1)}, bf16[192,256]{1,0:T(8,128)(2,1)S(1)}, u32[]{:S(2)}, u32[]{:S(2)}) collective-permute-start(bf16[192,256]{1,0:T(8,128)(2,1)} %get-tuple-element.216), channel_id=1, source_target_pairs={{0,12},{4,8},{8,4},{12,0},{16,28},{20,24},{24,20},{28,16},{1,13},{... | collective-permute-start | bytes 294920 | tf_op jit(solution)/shard_map/ppermute | solution.py:689
  365.8 13.8 %collective-permute-start.15 = (bf16[192,256]{1,0:T(8,128)(2,1)}, bf16[192,256]{1,0:T(8,128)(2,1)S(1)}, u32[]{:S(2)}, u32[]{:S(2)}) collective-permute-start(bf16[192,256]{1,0:T(8,128)(2,1)} %get-tuple-element.217), channel_id=1, source_target_pairs={{0,8},{4,12},{8,0},{12,4},{16,24},{20,28},{24,16},{28,20},{1,9},{5... | collective-permute-start | bytes 294920 | tf_op jit(solution)/shard_map/ppermute | solution.py:689
  366.4 13.2 %collective-permute-start.14 = (bf16[192,256]{1,0:T(8,128)(2,1)}, bf16[192,256]{1,0:T(8,128)(2,1)S(1)}, u32[]{:S(2)}, u32[]{:S(2)}) collective-permute-start(bf16[192,256]{1,0:T(8,128)(2,1)} %get-tuple-element.215), channel_id=1, source_target_pairs={{0,4},{4,0},{8,12},{12,8},{16,20},{20,16},{24,28},{28,24},{1,5},{5... | collective-permute-start | bytes 294920 | tf_op jit(solution)/shard_map/ppermute | solution.py:689
  367.5 13.4 %collective-permute-start.11 = (bf16[192,640]{1,0:T(8,128)(2,1)S(1)}, bf16[192,640]{1,0:T(8,128)(2,1)S(1)}, u32[]{:S(2)}, u32[]{:S(2)}) collective-permute-start(bf16[192,640]{1,0:T(8,128)(2,1)S(1)} %fusion.15), channel_id=1, source_target_pairs={{0,2},{1,3},{2,0},{3,1},{4,6},{5,7},{6,4},{7,5},{8,10},{9,11},{10,... | collective-permute-start | bytes 737288 | tf_op jit(solution)/shard_map/ppermute | solution.py:689
  382.1 23.4 %collective-permute-start.17 = (bf16[192,896]{1,0:T(8,128)(2,1)S(1)}, bf16[192,896]{1,0:T(8,128)(2,1)S(1)}, u32[]{:S(2)}, u32[]{:S(2)}) collective-permute-start(bf16[192,896]{1,0:T(8,128)(2,1)S(1)} %pad_maximum_fusion), channel_id=1, source_target_pairs={{0,16},{4,20},{8,24},{12,28},{16,0},{20,4},{24,8},{28,12},{1,17},{... | collective-permute-start | bytes 1032200 | tf_op jit(solution)/shard_map/ppermute | solution.py:689
  405.6 20.5 %copy-start.11 = (bf16[192,896]{1,0:T(8,128)(2,1)}, bf16[192,896]{1,0:T(8,128)(2,1)S(1)}, u32[]{:S(2)}) copy-start(bf16[192,896]{1,0:T(8,128)(2,1)S(1)} %add_convert_fusion.3.refs_0_) | copy-start | bytes 1032196
  405.6 20.5 %collective-permute-start.18 = (bf16[192,896]{1,0:T(8,128)(2,1)S(1)}, bf16[192,896]{1,0:T(8,128)(2,1)S(1)}, u32[]{:S(2)}, u32[]{:S(2)}) collective-permute-start(bf16[192,896]{1,0:T(8,128)(2,1)S(1)} %add_convert_fusion.3.refs_0_), channel_id=1, source_target_pairs={{0,4},{4,0},{8,12},{12,8},{16,20},{20,16},{24,28},{28,24},{1,5},{5... | collective-permute-start | bytes 1032200 | tf_op jit(solution)/shard_map/ppermute | solution.py:689
  407.1 19.0 %collective-permute-start.19 = (bf16[192,896]{1,0:T(8,128)(2,1)S(1)}, bf16[192,896]{1,0:T(8,128)(2,1)}, u32[]{:S(2)}, u32[]{:S(2)}) collective-permute-start(bf16[192,896]{1,0:T(8,128)(2,1)S(1)} %add_convert_fusion.3.refs_0_), channel_id=1, source_target_pairs={{0,8},{4,12},{8,0},{12,4},{16,24},{20,28},{24,16},{28,20},{1,9},{5... | collective-permute-start | bytes 1032200 | tf_op jit(solution)/shard_map/ppermute | solution.py:689
  407.1 19.0 %collective-permute-start.20 = (bf16[192,896]{1,0:T(8,128)(2,1)S(1)}, bf16[192,896]{1,0:T(8,128)(2,1)}, u32[]{:S(2)}, u32[]{:S(2)}) collective-permute-start(bf16[192,896]{1,0:T(8,128)(2,1)S(1)} %add_convert_fusion.3.refs_0_), channel_id=1, source_target_pairs={{0,12},{4,8},{8,4},{12,0},{16,28},{20,24},{24,20},{28,16},{1,13},{... | collective-permute-start | bytes 1032200 | tf_op jit(solution)/shard_map/ppermute | solution.py:689
  418.7 11.4 %copy-start.1 = (s32[2,2048]{1,0:T(2,128)S(1)}, s32[2,2048]{1,0:T(2,128)}, u32[]{:S(2)}) copy-start(s32[2,2048]{1,0:T(2,128)} %param.15) | copy-start | bytes 49156
  (8 other events, 7.8 us)
Sparse Core Ops, SparseCore 0:
  13.3 72.9 all-gather.3
  87.9 65.7 all-gather.5
  155.3 30.7 all-gather.7
  253.9 151.9 reduce-scatter.1

commit v4 on v3

--- a/solution.py
+++ b/solution.py
@@ -25,7 +25,7 @@
     int(math.ceil(16 * 8 ** (step_k / 16))) for step_k in range(1, 16)
 )
 VMEM_MOST = 56 << 20
-COST_SHARE = 1
+COST_SHARE = 0.4
 FILLER = 0.02
 G_AFTER = 8
 

time: 444 us -> 443 us (level)
  no operation moved by 1% of the time
where the time goes in v4:
time: 443 us; the launch traced here: 436 us
  Pallas kernels  164 us (37%)
  waiting for transfers between devices  115 us (26%)
  starting transfers between devices  64.6 us (15%)
  blocking collectives  45.8 us (10%)
  local copies, waits for them, and re-layouts  23.1 us (5%)
  between operations  14.6 us (3%)
  other arithmetic  9.92 us (2%)
    ppermute x21, waiting for transfers between devices, swap(): return lax.ppermute(array, axis, [(i, i ^ bit) for i in range(size)])  66.8 us
    pallas_call x10, Pallas kernels, one_step(): pl.pallas_call(kernel, out_shape=tuple(outs), in_specs=[pl.BlockSpec(memo...  57.7 us
    all_to_all x8, waiting for transfers between devices, exchange(): return lax.all_to_all(array, 'seq', split_axis=0, concat_axis=0, tiled=True)  46.4 us
    all_to_all x2, blocking collectives, exchange(): return lax.all_to_all(array, 'seq', split_axis=0, concat_axis=0, tiled=True)  45.8 us
    all_to_all x8, starting transfers between devices, exchange(): return lax.all_to_all(array, 'seq', split_axis=0, concat_axis=0, tiled=True)  39.3 us
    pallas_call x2, Pallas kernels, expert_pass(): pl.pallas_call(functools.partial(expert_kernel, index=index, local=local,...  36.9 us
    ppermute x21, starting transfers between devices, swap(): return lax.ppermute(array, axis, [(i, i ^ bit) for i in range(size)])  24.9 us
    pallas_call x1, Pallas kernels, attention_bwd(): pl.pallas_call(bwd_kernel, grid=(pairs,), out_shape=(shape(qkv.shape, BF)...  23.3 us
  transfers between devices with their start and end apart: 33, of which 16 were waited for; matrix products, arithmetic and copies ran while one was open for 5% of the time, Pallas kernels for 37%

profile of v4, /device:TPU:0, one launch (start us, length us, event | category | flops | bytes accessed | tf_op | source)
XLA Modules:
  0.0 436.3 jit_solution(2835660178673354555)
XLA Ops:
  7.2 3.0 copy_bitcast_fusion
  10.7 2.5 fusion.18
  15.1 2.3 shard_map.212.refs_0_
  17.4 3.0 collective-permute-start
  20.5 2.7 collective-permute-start.3
  24.6 1.6 collective-permute-start.5
  26.6 13.9 %collective-permute-done.3.refs_1_ = bf16[256,768]{1,0:T(8,128)(2,1)S(1)} collective-permute-done((bf16[256,768]{1,0:T(8,128)(2,1)S(1)}, bf16[256,768]{1,0:T(8,128)(2,1)S(1)}, u32[]{:S(2)}, u32[]{:S(2)}) %collective-permute-start.3) | collective-permute-done | bytes 393248 | tf_op jit(solution)/shard_map/ppermute | solution.py:689
  41.8 2.2 collective-permute-done.5.refs_3_
  44.0 6.3 %collective-permute-done.6.refs_4_ = bf16[256,768]{1,0:T(8,128)(2,1)S(1)} collective-permute-done((bf16[256,768]{1,0:T(8,128)(2,1)S(1)}, bf16[256,768]{1,0:T(8,128)(2,1)S(1)}, u32[]{:S(2)}, u32[]{:S(2)}) %collective-permute-start.6) | collective-permute-done | bytes 393248 | tf_op jit(solution)/shard_map/ppermute | solution.py:689
  52.8 1.8 collective-permute-start.9
  55.6 4.6 %shard_map.213 = (bf16[768,576]{1,0:T(8,128)(2,1)}, bf16[768,768]{1,0:T(8,128)(2,1)}, f32[128,768]{1,0:T(8,128)}, f32[3,384,256]{2,1,0:T(8,128)}) custom-call(s32[1]{0:T(128)} %bitcast.me_ref, bf16[192,1472]{1,0:T(8,128)(2,1)} %shard_map.212.refs_0_, bf16[192,1472]{1,0:T(8,128)(2,1)} %copy-done.12, bf16[192,1472]{1,0:T(8,128)(2,1)} %copy-done.13, ...), custom_call_target="tpu_custom_call" | custom-call | flops 24000000 | bytes 47185 | tf_op jit(solution)/shard_map/pallas_call | solution.py:207
  60.2 2.0 collective-permute-done.7.refs_5_
  64.7 4.3 shard_map.214
  70.0 2.8 fusion.2
  72.8 5.3 %all-to-all-start = ((bf16[8,152,768]{2,1,0:T(8,128)(2,1)}), bf16[8,152,768]{2,1,0:T(8,128)(2,1)S(1)}, u32[]{:S(2)}, u32[]{:S(2)}) async-start(bf16[8,152,768]{2,1,0:T(8,128)(2,1)} %fusion.2), calls=%async_computation | async-start | bytes 3735552 | tf_op jit(solution)/shard_map/all_to_all | solution.py:702
  78.8 7.1 %shard_map.215 = (bf16[8,576,256]{2,1,0:T(8,128)(2,1)}, bf16[8,256,768]{2,1,0:T(8,128)(2,1)}) custom-call(s32[1]{0:T(128)} %bitcast.9.me_ref.own_ref, f32[128,768]{1,0:T(8,128)} %get-tuple-element.86.small_ref, bf16[768,576]{1,0:T(8,128)(2,1)} %get-tuple-element.91.w_ref, bf16[256,768]{1,0:T(8,128)(2,1)} %copy-done.10, bf16[256,768]{1,0:T(8,128)(2,1)} %copy-done.15, ...), custom_call_target="tpu_custom_call" | custom-call | flops 28991028 | bytes 79429 | tf_op jit(solution)/shard_map/pallas_call | solution.py:207
  85.9 16.5 %shard_map.216 = (bf16[8,192,256]{2,1,0:T(8,128)(2,1)}, f32[3,64,2048]{2,1,0:T(8,128)}, f32[3,1,2048]{2,1,0:T(1,128)}) custom-call(bf16[8,576,256]{2,1,0:T(8,128)(2,1)} %get-tuple-element.92.qkv_ref, s32[1,2048]{1,0:T(1,128)} %constant_dynamic-slice_fusion.3.seg_ref, f32[3,384,256]{2,1,0:T(8,128)} %get-tuple-element.93.band_ref), custom_call_target="tpu_custom_call" | custom-call | flops 7200000000 | bytes 2400000 | tf_op jit(solution)/shard_map/pallas_call | solution.py:154
  102.4 14.7 %all-to-all-done = bf16[8,152,768]{2,1,0:T(8,128)(2,1)S(1)} async-done(((bf16[8,152,768]{2,1,0:T(8,128)(2,1)}), bf16[8,152,768]{2,1,0:T(8,128)(2,1)S(1)}, u32[]{:S(2)}, u32[]{:S(2)}) %all-to-all-start) | async-done | bytes 1867808 | tf_op jit(solution)/shard_map/all_to_all | solution.py:702
  117.1 22.9 %all_to_all.50.chunk_ref.att_ref = bf16[8,192,256]{2,1,0:T(8,128)(2,1)} all-to-all(bf16[8,192,256]{2,1,0:T(8,128)(2,1)} %get-tuple-element.99), channel_id=1, replica_groups=mesh['seq'=8,'fsdp'=4] {'seq'}, dimensions={0} | all-to-all | bytes 1572864 | tf_op jit(solution)/shard_map/all_to_all | solution.py:702
  140.0 5.0 %shard_map.217 = (f32[512,768]{1,0:T(8,128)}, f32[512,2]{1,0:T(8,128)}, bf16[576,768]{1,0:T(8,128)(2,1)}, bf16[576,768]{1,0:T(8,128)(2,1)}) custom-call(bf16[2,256,768]{2,1,0:T(8,128)(2,1)} %tok_ref.3, f32[128,768]{1,0:T(8,128)} %get-tuple-element.86.small_ref, bf16[768,768]{1,0:T(8,128)(2,1)} %get-tuple-element.87.w_ref, s32[512,2]{1,0:T(8,128)} %bitcast.65, ...), custom_call_target="tpu_custom_call" | custom-call | flops 24159192 | bytes 52002 | tf_op jit(solution)/shard_map/pallas_call | solution.py:207
  145.1 3.6 all-to-all-start.2
  149.4 21.2 %all-to-all-done.2 = bf16[8,72,768]{2,1,0:T(8,128)(2,1)S(1)} async-done(((bf16[8,72,768]{2,1,0:T(8,128)(2,1)}), bf16[8,72,768]{2,1,0:T(8,128)(2,1)S(1)}, u32[]{:S(2)}, u32[]{:S(2)}) %all-to-all-start.2) | async-done | bytes 884768 | tf_op jit(solution)/shard_map/all_to_all | solution.py:702
  170.6 4.4 %all-to-all-start.3 = ((bf16[8,72,768]{2,1,0:T(8,128)(2,1)}), bf16[8,72,768]{2,1,0:T(8,128)(2,1)}, u32[]{:S(2)}, u32[]{:S(2)}) async-start(bf16[8,72,768]{2,1,0:T(8,128)(2,1)} %bitcast.83), calls=%async_computation.3 | async-start | bytes 1769472 | tf_op jit(solution)/shard_map/all_to_all | solution.py:702
  177.3 18.5 %shard_map.218 = (bf16[576,768]{1,0:T(8,128)(2,1)}, bf16[576,768]{1,0:T(8,128)(2,1)}, bf16[16,576]{1,0:T(8,128)(2,1)}, bf16[576,768]{1,0:T(8,128)(2,1)}, bf16[4,...) custom-call(s32[1]{0:T(128)} %bitcast.9.me_ref.own_ref, bf16[576,768]{1,0:T(8,128)(2,1)} %bitcast.72, ...), custom_call_target="tpu_custom_call" | custom-call | flops 5435817984 | bytes 11324620 | tf_op jit(solution)/shard_map/pallas_call | solution.py:595
  196.9 4.9 %all-to-all-start.4 = ((bf16[8,72,768]{2,1,0:T(8,128)(2,1)}), bf16[8,72,768]{2,1,0:T(8,128)(2,1)S(1)}, u32[]{:S(2)}, u32[]{:S(2)}) async-start(bf16[8,72,768]{2,1,0:T(8,128)(2,1)} %bitcast.82), calls=%async_computation.4 | async-start | bytes 1769472 | tf_op jit(solution)/shard_map/all_to_all | solution.py:702
  202.7 18.4 %shard_map.219 = (bf16[576,768]{1,0:T(8,128)(2,1)}, bf16[576,768]{1,0:T(8,128)(2,1)}, bf16[16,576]{1,0:T(8,128)(2,1)}, bf16[576,768]{1,0:T(8,128)(2,1)}, bf16[4,...) custom-call(s32[1]{0:T(128)} %bitcast.9.me_ref.own_ref, ...), custom_call_target="tpu_custom_call" | custom-call | flops 5435817984 | bytes 11324620 | tf_op jit(solution)/shard_map/pallas_call | solution.py:595
  222.7 2.2 fusion.3
  224.9 6.0 %all-to-all-start.5 = ((bf16[8,80,768]{2,1,0:T(8,128)(2,1)}), bf16[8,80,768]{2,1,0:T(8,128)(2,1)S(1)}, u32[]{:S(2)}, u32[]{:S(2)}) async-start(bf16[8,80,768]{2,1,0:T(8,128)(2,1)} %fusion.3), calls=%async_computation.5 | async-start | bytes 1966080 | tf_op jit(solution)/shard_map/all_to_all | solution.py:702
  231.2 21.9 %shard_map.220 = bf16[4,2,2,768,768]{4,3,2,1,0:T(8,128)(2,1)} custom-call(bf16[576,768]{1,0:T(8,128)(2,1)} %bitcast.73, bf16[576,768]{1,0:T(8,128)(2,1)} %get-tuple-element.115.refs_1_, bf16[4,576,768]{2,1,0:T(8,128)(2,1)} %get-tuple-element.117.refs_2_, bf16[4,576,768]{2,1,0:T(8,128)(2,1)} %get-tuple-element.118.refs_3_, ...), custom_call_target="tpu_custom_call" | custom-call | flops 400000 | bytes 400000 | tf_op jit(solution)/shard_map/pallas_call | solution.py:645
  254.8 5.3 %all-to-all-start.6 = ((bf16[8,72,768]{2,1,0:T(8,128)(2,1)}), bf16[8,72,768]{2,1,0:T(8,128)(2,1)S(1)}, u32[]{:S(2)}, u32[]{:S(2)}) async-start(bf16[8,72,768]{2,1,0:T(8,128)(2,1)} %bitcast.30), calls=%async_computation.6 | async-start | bytes 1769472 | tf_op jit(solution)/shard_map/all_to_all | solution.py:702
  260.9 10.9 %shard_map.221 = (f32[512,768]{1,0:T(8,128)}, bf16[8,192,256]{2,1,0:T(8,128)(2,1)}, bf16[2,192,1024]{2,1,0:T(8,128)(2,1)}, bf16[2,192,1024]{2,1,0:T(8,128)(2,1)}) custom-call(s32[1]{0:T(128)} %bitcast.me_ref, f32[1,1152]{1,0:T(1,128)} %reshape.183.dgate_ref, s32[512,2]{1,0:T(8,128)} %get-tuple-element.113.slot_ref, s32[512,2]{1,0:T(8,128)} %bitcast.66, ...), custom_call_target="tpu_custom_call" | custom-call | flops 33822868 | bytes 83546 | tf_op jit(solution)/shard_map/pallas_call | solution.py:207
  271.8 8.7 %all-to-all-done.6 = bf16[8,72,768]{2,1,0:T(8,128)(2,1)S(1)} async-done(((bf16[8,72,768]{2,1,0:T(8,128)(2,1)}), bf16[8,72,768]{2,1,0:T(8,128)(2,1)S(1)}, u32[]{:S(2)}, u32[]{:S(2)}) %all-to-all-start.6) | async-done | bytes 884768 | tf_op jit(solution)/shard_map/all_to_all | solution.py:702
  280.5 22.8 %all_to_all.51.do_ref = bf16[8,192,256]{2,1,0:T(8,128)(2,1)} all-to-all(bf16[8,192,256]{2,1,0:T(8,128)(2,1)} %get-tuple-element.130), channel_id=1, replica_groups=mesh['seq'=8,'fsdp'=4] {'seq'}, dimensions={0} | all-to-all | bytes 1572864 | tf_op jit(solution)/shard_map/all_to_all | solution.py:702
  303.3 3.6 all-to-all-start.8
  306.9 23.3 %shard_map.222 = (bf16[8,576,256]{2,1,0:T(8,128)(2,1)}, f32[3,384,256]{2,1,0:T(8,128)}) custom-call(bf16[8,576,256]{2,1,0:T(8,128)(2,1)} %get-tuple-element.92.qkv_ref, s32[1,2048]{1,0:T(1,128)} %constant_dynamic-slice_fusion.3.seg_ref, f32[3,384,256]{2,1,0:T(8,128)} %get-tuple-element.93.band_ref, f32[3,64,2048]{2,1,0:T(8,128)} %get-tuple-element.101.wide_ref, ...), custom_call_target="tpu_custom_call" | custom-call | flops 12000000000 | bytes 3600000 | tf_op jit(solution)/shard_map/pallas_call | solution.py:179
  331.1 6.3 %all-to-all-start.9 = ((bf16[8,576,256]{2,1,0:T(8,128)(2,1)}), bf16[8,576,256]{2,1,0:T(8,128)(2,1)S(1)}, u32[]{:S(2)}, u32[]{:S(2)}) async-start(bf16[8,576,256]{2,1,0:T(8,128)(2,1)} %get-tuple-element.137.d_ref), calls=%async_computation.9 | async-start | bytes 4718592 | tf_op jit(solution)/shard_map/all_to_all | solution.py:702
  337.4 2.3 collective-permute-done.12
  341.7 7.2 %shard_map.224 = (bf16[2,192,640]{2,1,0:T(8,128)(2,1)}, bf16[2,192,640]{2,1,0:T(8,128)(2,1)}) custom-call(s32[1]{0:T(128)} %bitcast.me_ref, bf16[8,256,768]{2,1,0:T(8,128)(2,1)} %get-tuple-element.138.first_ref, bf16[8,576,256]{2,1,0:T(8,128)(2,1)} %get-tuple-element.137.d_ref, f32[3,384,256]{2,1,0:T(8,128)} %get-tuple-element.139.band_ref), custom_call_target="tpu_custom_call" | custom-call | flops 28991028 | bytes 61341 | tf_op jit(solution)/shard_map/pallas_call | solution.py:207
  349.0 12.3 %collective-permute-done.13 = bf16[192,1024]{1,0:T(8,128)(2,1)S(1)} collective-permute-done((bf16[192,1024]{1,0:T(8,128)(2,1)S(1)}, bf16[192,1024]{1,0:T(8,128)(2,1)S(1)}, u32[]{:S(2)}, u32[]{:S(2)}) %collective-permute-start.13) | collective-permute-done | bytes 393248 | tf_op jit(solution)/shard_map/ppermute | solution.py:689
  362.2 2.9 collective-permute-start.16
  367.4 10.3 %collective-permute-done.16 = bf16[192,256]{1,0:T(8,128)(2,1)S(1)} collective-permute-done((bf16[192,256]{1,0:T(8,128)(2,1)}, bf16[192,256]{1,0:T(8,128)(2,1)S(1)}, u32[]{:S(2)}, u32[]{:S(2)}) %collective-permute-start.16) | collective-permute-done | bytes 98336 | tf_op jit(solution)/shard_map/ppermute | solution.py:689
  381.4 4.0 collective-permute-start.17
  385.4 5.6 %shard_map.223 = bf16[512,768]{1,0:T(8,128)(2,1)} custom-call(f32[512,768]{1,0:T(8,128)} %get-tuple-element.132.mid_ref, s32[512,2]{1,0:T(8,128)} %get-tuple-element.113.slot_ref, f32[512,2]{1,0:T(8,128)} %get-tuple-element.114.gate_ref, bf16[576,768]{1,0:T(8,128)(2,1)} %bitcast.70, bf16[576,768]{1,0:T(8,128)(2,1)} %bitcast.71), custom_call_target="tpu_custom_call" | custom-call | flops 14495514 | bytes 33095 | tf_op jit(solution)/shard_map/pallas_call | solution.py:207
  391.0 13.7 %collective-permute-done.17 = bf16[192,896]{1,0:T(8,128)(2,1)S(1)} collective-permute-done((bf16[192,896]{1,0:T(8,128)(2,1)S(1)}, bf16[192,896]{1,0:T(8,128)(2,1)S(1)}, u32[]{:S(2)}, u32[]{:S(2)}) %collective-permute-start.17) | collective-permute-done | bytes 344096 | tf_op jit(solution)/shard_map/ppermute | solution.py:689
  406.4 2.0 collective-permute-start.20
  410.5 7.4 %shard_map.225 = f32[2,256,768]{2,1,0:T(8,128)} custom-call(bf16[2,256,768]{2,1,0:T(8,128)(2,1)} %tok_ref.3, f32[128,768]{1,0:T(8,128)} %get-tuple-element.86.small_ref, bf16[768,2304]{1,0:T(8,128)(2,1)} %all-gather.8.cloned.1.call-done.w_ref, f32[512,768]{1,0:T(8,128)} %get-tuple-element.136.dmid_ref, bf16[8,576,256]{2,1,0:T(8,128)(2,1)} %copy-done.3), custom_call_target="tpu_custom_call" | custom-call | flops 28991028 | bytes 81788 | tf_op jit(solution)/shard_map/pallas_call | solution.py:207
  417.9 7.4 %shard_map.226 = (f32[768,2,768]{2,1,0:T(2,128)}, f32[768,2,768]{2,1,0:T(2,128)}) custom-call(bf16[2,2,768,768]{3,2,1,0:T(8,128)(2,1)} %bitcast.67), custom_call_target="tpu_custom_call" | custom-call | flops 400000 | bytes 400000 | tf_op jit(solution)/shard_map/pallas_call | solution.py:672
  426.1 3.3 shard_map.227
  (130 shorter events, 36.9 us)
Async XLA Ops:
  7.2 71.0 %copy-start = (s32[2,2048]{1,0:T(2,128)S(1)}, s32[2,2048]{1,0:T(2,128)}, u32[]{:S(2)}) copy-start(s32[2,2048]{1,0:T(2,128)} %param.15) | copy-start | bytes 49156
  7.2 170.1 %all-gather.4.cloned.1.call-start = ((), (), s32[]{:S(2)}) async-start(), calls=%async_computation.11 | async-start | bytes 11796480 | tf_op jit(solution)/shard_map/all_gather | solution.py:840
  13.2 7.2 %copy-start.4 = (bf16[2,256,768]{2,1,0:T(8,128)(2,1)S(1)}, bf16[2,256,768]{2,1,0:T(8,128)(2,1)}, u32[]{:S(2)}) copy-start(bf16[2,256,768]{2,1,0:T(8,128)(2,1)} %tok_ref.3) | copy-start | bytes 2359300
  13.2 189.5 %all-gather.6.cloned.1.call-start = ((), (), s32[]{:S(2)}) async-start(), calls=%async_computation.12 | async-start | bytes 11796480 | tf_op jit(solution)/shard_map/all_gather | solution.py:840
  17.4 24.4 %collective-permute-start = (bf16[192,1472]{1,0:T(8,128)(2,1)}, bf16[192,1472]{1,0:T(8,128)(2,1)S(1)}, u32[]{:S(2)}, u32[]{:S(2)}) collective-permute-start(bf16[192,1472]{1,0:T(8,128)(2,1)} %shard_map.212.refs_0_), channel_id=1, source_target_pairs={{0,2},{1,3},{2,0},{3,1},{4,6},{5,7},{6,4},{7,5},{8,10},{9,11},{10,... | collective-permute-start | bytes 1695752 | tf_op jit(solution)/shard_map/ppermute | solution.py:689
  20.4 48.6 %copy-start.10 = (bf16[256,768]{1,0:T(8,128)(2,1)}, bf16[256,768]{1,0:T(8,128)(2,1)S(1)}, u32[]{:S(2)}) copy-start(bf16[256,768]{1,0:T(8,128)(2,1)S(1)} %get-tuple-element.213.refs_0_) | copy-start | bytes 1179652
  20.5 20.1 %collective-permute-start.3 = (bf16[256,768]{1,0:T(8,128)(2,1)S(1)}, bf16[256,768]{1,0:T(8,128)(2,1)S(1)}, u32[]{:S(2)}, u32[]{:S(2)}) collective-permute-start(bf16[256,768]{1,0:T(8,128)(2,1)S(1)} %get-tuple-element.214), channel_id=1, source_target_pairs={{0,16},{4,20},{8,24},{12,28},{16,0},{20,4},{24,8},{28,12},{1,17},{... | collective-permute-start | bytes 1179656 | tf_op jit(solution)/shard_map/ppermute | solution.py:689
  23.1 18.7 %collective-permute-start.4 = (bf16[256,768]{1,0:T(8,128)(2,1)S(1)}, bf16[256,768]{1,0:T(8,128)(2,1)S(1)}, u32[]{:S(2)}, u32[]{:S(2)}) collective-permute-start(bf16[256,768]{1,0:T(8,128)(2,1)S(1)} %get-tuple-element.213.refs_0_), channel_id=1, source_target_pairs={{0,4},{4,0},{8,12},{12,8},{16,20},{20,16},{24,28},{28,24},{1,5},{5... | collective-permute-start | bytes 1179656 | tf_op jit(solution)/shard_map/ppermute | solution.py:689
  24.6 19.4 %collective-permute-start.5 = (bf16[256,768]{1,0:T(8,128)(2,1)S(1)}, bf16[256,768]{1,0:T(8,128)(2,1)S(1)}, u32[]{:S(2)}, u32[]{:S(2)}) collective-permute-start(bf16[256,768]{1,0:T(8,128)(2,1)S(1)} %get-tuple-element.213.refs_0_), channel_id=1, source_target_pairs={{0,8},{4,12},{8,0},{12,4},{16,24},{20,28},{24,16},{28,20},{1,9},{5... | collective-permute-start | bytes 1179656 | tf_op jit(solution)/shard_map/ppermute | solution.py:689
  26.2 24.1 %collective-permute-start.6 = (bf16[256,768]{1,0:T(8,128)(2,1)S(1)}, bf16[256,768]{1,0:T(8,128)(2,1)S(1)}, u32[]{:S(2)}, u32[]{:S(2)}) collective-permute-start(bf16[256,768]{1,0:T(8,128)(2,1)S(1)} %get-tuple-element.213.refs_0_), channel_id=1, source_target_pairs={{0,12},{4,8},{8,4},{12,0},{16,28},{20,24},{24,20},{28,16},{1,13},{... | collective-permute-start | bytes 1179656 | tf_op jit(solution)/shard_map/ppermute | solution.py:689
  40.5 38.3 %copy-start.15 = (bf16[256,768]{1,0:T(8,128)(2,1)}, bf16[256,768]{1,0:T(8,128)(2,1)S(1)}, u32[]{:S(2)}) copy-start(bf16[256,768]{1,0:T(8,128)(2,1)S(1)} %collective-permute-done.3.refs_1_) | copy-start | bytes 1179652
  40.5 14.0 %collective-permute-start.1 = (bf16[192,1472]{1,0:T(8,128)(2,1)}, bf16[192,1472]{1,0:T(8,128)(2,1)S(1)}, u32[]{:S(2)}, u32[]{:S(2)}) collective-permute-start(bf16[192,1472]{1,0:T(8,128)(2,1)} %shard_map.212.refs_0_), channel_id=1, source_target_pairs={{0,1},{1,0},{2,3},{3,2},{4,5},{5,4},{6,7},{7,6},{8,9},{9,8},{10,11... | collective-permute-start | bytes 1695752 | tf_op jit(solution)/shard_map/ppermute | solution.py:689
  41.8 12.8 %copy-start.12 = (bf16[192,1472]{1,0:T(8,128)(2,1)}, bf16[192,1472]{1,0:T(8,128)(2,1)S(1)}, u32[]{:S(2)}) copy-start(bf16[192,1472]{1,0:T(8,128)(2,1)S(1)} %collective-permute-done.refs_1_) | copy-start | bytes 1695748
  41.8 12.8 %collective-permute-start.2 = (bf16[192,1472]{1,0:T(8,128)(2,1)S(1)}, bf16[192,1472]{1,0:T(8,128)(2,1)S(1)}, u32[]{:S(2)}, u32[]{:S(2)}) collective-permute-start(bf16[192,1472]{1,0:T(8,128)(2,1)S(1)} %collective-permute-done.refs_1_), channel_id=1, source_target_pairs={{0,1},{1,0},{2,3},{3,2},{4,5},{5,4},{6,7},{7,6},{8,9},{9,8},{10,11... | collective-permute-start | bytes 1695752 | tf_op jit(solution)/shard_map/ppermute | solution.py:689
  41.8 37.0 %copy-start.16 = (bf16[256,768]{1,0:T(8,128)(2,1)}, bf16[256,768]{1,0:T(8,128)(2,1)S(1)}, u32[]{:S(2)}) copy-start(bf16[256,768]{1,0:T(8,128)(2,1)S(1)} %collective-permute-done.4.refs_2_) | copy-start | bytes 1179652
  44.0 34.8 %copy-start.17 = (bf16[256,768]{1,0:T(8,128)(2,1)}, bf16[256,768]{1,0:T(8,128)(2,1)S(1)}, u32[]{:S(2)}) copy-start(bf16[256,768]{1,0:T(8,128)(2,1)S(1)} %collective-permute-done.5.refs_3_) | copy-start | bytes 1179652
  51.1 11.1 %collective-permute-start.7 = (bf16[256,768]{1,0:T(8,128)(2,1)S(1)}, bf16[256,768]{1,0:T(8,128)(2,1)}, u32[]{:S(2)}, u32[]{:S(2)}) collective-permute-start(bf16[256,768]{1,0:T(8,128)(2,1)S(1)} %collective-permute-done.3.refs_1_), channel_id=1, source_target_pairs={{0,4},{4,0},{8,12},{12,8},{16,20},{20,16},{24,28},{28,24},{1,5},{5... | collective-permute-start | bytes 1179656 | tf_op jit(solution)/shard_map/ppermute | solution.py:689
  52.6 20.2 %collective-permute-start.8 = (bf16[256,768]{1,0:T(8,128)(2,1)S(1)}, bf16[256,768]{1,0:T(8,128)(2,1)}, u32[]{:S(2)}, u32[]{:S(2)}) collective-permute-start(bf16[256,768]{1,0:T(8,128)(2,1)S(1)} %collective-permute-done.3.refs_1_), channel_id=1, source_target_pairs={{0,8},{4,12},{8,0},{12,4},{16,24},{20,28},{24,16},{28,20},{1,9},{5... | collective-permute-start | bytes 1179656 | tf_op jit(solution)/shard_map/ppermute | solution.py:689
  52.8 20.1 %collective-permute-start.9 = (bf16[256,768]{1,0:T(8,128)(2,1)S(1)}, bf16[256,768]{1,0:T(8,128)(2,1)}, u32[]{:S(2)}, u32[]{:S(2)}) collective-permute-start(bf16[256,768]{1,0:T(8,128)(2,1)S(1)} %collective-permute-done.3.refs_1_), channel_id=1, source_target_pairs={{0,12},{4,8},{8,4},{12,0},{16,28},{20,24},{24,20},{28,16},{1,13},{... | collective-permute-start | bytes 1179656 | tf_op jit(solution)/shard_map/ppermute | solution.py:689
  63.0 1.7 copy-start.2
  63.3 1.4 copy-start.9
  72.8 44.2 %all-to-all-start = ((bf16[8,152,768]{2,1,0:T(8,128)(2,1)}), bf16[8,152,768]{2,1,0:T(8,128)(2,1)S(1)}, u32[]{:S(2)}, u32[]{:S(2)}) async-start(bf16[8,152,768]{2,1,0:T(8,128)(2,1)} %fusion.2), calls=%async_computation | async-start | bytes 3735552 | tf_op jit(solution)/shard_map/all_to_all | solution.py:702
  145.1 25.5 %all-to-all-start.2 = ((bf16[8,72,768]{2,1,0:T(8,128)(2,1)}), bf16[8,72,768]{2,1,0:T(8,128)(2,1)S(1)}, u32[]{:S(2)}, u32[]{:S(2)}) async-start(bf16[8,72,768]{2,1,0:T(8,128)(2,1)} %bitcast.84), calls=%async_computation.2 | async-start | bytes 1769472 | tf_op jit(solution)/shard_map/all_to_all | solution.py:702
  148.6 260.5 %all-gather.8.cloned.1.call-start = ((), (), s32[]{:S(2)}) async-start(), calls=%async_computation.13 | async-start | bytes 4423680 | tf_op jit(solution)/shard_map/all_gather | solution.py:843
  170.6 6.7 %copy-start.8 = (bf16[8,72,768]{2,1,0:T(8,128)(2,1)}, bf16[8,72,768]{2,1,0:T(8,128)(2,1)S(1)}, u32[]{:S(2)}) copy-start(bf16[8,72,768]{2,1,0:T(8,128)(2,1)S(1)} %all-to-all-done.2) | copy-start | bytes 2654212
  170.6 26.3 %all-to-all-start.3 = ((bf16[8,72,768]{2,1,0:T(8,128)(2,1)}), bf16[8,72,768]{2,1,0:T(8,128)(2,1)}, u32[]{:S(2)}, u32[]{:S(2)}) async-start(bf16[8,72,768]{2,1,0:T(8,128)(2,1)} %bitcast.83), calls=%async_computation.3 | async-start | bytes 1769472 | tf_op jit(solution)/shard_map/all_to_all | solution.py:702
  196.9 28.0 %all-to-all-start.4 = ((bf16[8,72,768]{2,1,0:T(8,128)(2,1)}), bf16[8,72,768]{2,1,0:T(8,128)(2,1)S(1)}, u32[]{:S(2)}, u32[]{:S(2)}) async-start(bf16[8,72,768]{2,1,0:T(8,128)(2,1)} %bitcast.82), calls=%async_computation.4 | async-start | bytes 1769472 | tf_op jit(solution)/shard_map/all_to_all | solution.py:702
  224.9 28.2 %copy-start.5 = (bf16[8,72,768]{2,1,0:T(8,128)(2,1)}, bf16[8,72,768]{2,1,0:T(8,128)(2,1)S(1)}, u32[]{:S(2)}) copy-start(bf16[8,72,768]{2,1,0:T(8,128)(2,1)S(1)} %all-to-all-done.4) | copy-start | bytes 2654212
  224.9 28.9 %all-to-all-start.5 = ((bf16[8,80,768]{2,1,0:T(8,128)(2,1)}), bf16[8,80,768]{2,1,0:T(8,128)(2,1)S(1)}, u32[]{:S(2)}, u32[]{:S(2)}) async-start(bf16[8,80,768]{2,1,0:T(8,128)(2,1)} %fusion.3), calls=%async_computation.5 | async-start | bytes 1966080 | tf_op jit(solution)/shard_map/all_to_all | solution.py:702
  230.9 187.0 %reduce-scatter.2.cloned.1.call-start = ((), (), s32[]{:S(2)}) async-start(), calls=%async_computation.14 | async-start | bytes 23592960 | tf_op jit(solution)/shard_map/reduce_scatter | solution.py:870
  254.8 25.7 %all-to-all-start.6 = ((bf16[8,72,768]{2,1,0:T(8,128)(2,1)}), bf16[8,72,768]{2,1,0:T(8,128)(2,1)S(1)}, u32[]{:S(2)}, u32[]{:S(2)}) async-start(bf16[8,72,768]{2,1,0:T(8,128)(2,1)} %bitcast.30), calls=%async_computation.6 | async-start | bytes 1769472 | tf_op jit(solution)/shard_map/all_to_all | solution.py:702
  280.5 49.7 %copy-start.6 = (bf16[8,72,768]{2,1,0:T(8,128)(2,1)}, bf16[8,72,768]{2,1,0:T(8,128)(2,1)S(1)}, u32[]{:S(2)}) copy-start(bf16[8,72,768]{2,1,0:T(8,128)(2,1)S(1)} %all-to-all-done.6) | copy-start | bytes 2654212
  303.3 26.9 %all-to-all-start.8 = ((bf16[8,72,768]{2,1,0:T(8,128)(2,1)}), bf16[8,72,768]{2,1,0:T(8,128)(2,1)S(1)}, u32[]{:S(2)}, u32[]{:S(2)}) async-start(bf16[8,72,768]{2,1,0:T(8,128)(2,1)} %bitcast.32), calls=%async_computation.8 | async-start | bytes 1769472 | tf_op jit(solution)/shard_map/all_to_all | solution.py:702
  330.2 7.2 %copy-start.20 = (bf16[2,192,1024]{2,1,0:T(8,128)(2,1)S(1)}, bf16[2,192,1024]{2,1,0:T(8,128)(2,1)}, u32[]{:S(2)}) copy-start(bf16[2,192,1024]{2,1,0:T(8,128)(2,1)} %get-tuple-element.145) | copy-start | bytes 2359300
  331.1 78.1 %all-to-all-start.9 = ((bf16[8,576,256]{2,1,0:T(8,128)(2,1)}), bf16[8,576,256]{2,1,0:T(8,128)(2,1)S(1)}, u32[]{:S(2)}, u32[]{:S(2)}) async-start(bf16[8,576,256]{2,1,0:T(8,128)(2,1)} %get-tuple-element.137.d_ref), calls=%async_computation.9 | async-start | bytes 4718592 | tf_op jit(solution)/shard_map/all_to_all | solution.py:702
  337.4 2.4 collective-permute-start.12
  341.1 20.2 %collective-permute-start.13 = (bf16[192,1024]{1,0:T(8,128)(2,1)S(1)}, bf16[192,1024]{1,0:T(8,128)(2,1)S(1)}, u32[]{:S(2)}, u32[]{:S(2)}) collective-permute-start(bf16[192,1024]{1,0:T(8,128)(2,1)S(1)} %get-tuple-element.212), channel_id=1, source_target_pairs={{0,2},{1,3},{2,0},{3,1},{4,6},{5,7},{6,4},{7,5},{8,10},{9,11},{10,... | collective-permute-start | bytes 1179656 | tf_op jit(solution)/shard_map/ppermute | solution.py:689
  348.9 16.7 %collective-permute-start.10 = (bf16[2,192,640]{2,1,0:T(8,128)(2,1)}, bf16[2,192,640]{2,1,0:T(8,128)(2,1)}, u32[]{:S(2)}, u32[]{:S(2)}) collective-permute-start(bf16[2,192,640]{2,1,0:T(8,128)(2,1)} %get-tuple-element.142), channel_id=1, source_target_pairs={{0,1},{1,0},{2,3},{3,2},{4,5},{5,4},{6,7},{7,6},{8,9},{9,8},{10,11... | collective-permute-start | bytes 1474568 | tf_op jit(solution)/shard_map/ppermute | solution.py:689
  362.2 15.6 %collective-permute-start.16 = (bf16[192,256]{1,0:T(8,128)(2,1)}, bf16[192,256]{1,0:T(8,128)(2,1)S(1)}, u32[]{:S(2)}, u32[]{:S(2)}) collective-permute-start(bf16[192,256]{1,0:T(8,128)(2,1)} %get-tuple-element.216), channel_id=1, source_target_pairs={{0,12},{4,8},{8,4},{12,0},{16,28},{20,24},{24,20},{28,16},{1,13},{... | collective-permute-start | bytes 294920 | tf_op jit(solution)/shard_map/ppermute | solution.py:689
  365.1 13.7 %collective-permute-start.15 = (bf16[192,256]{1,0:T(8,128)(2,1)}, bf16[192,256]{1,0:T(8,128)(2,1)S(1)}, u32[]{:S(2)}, u32[]{:S(2)}) collective-permute-start(bf16[192,256]{1,0:T(8,128)(2,1)} %get-tuple-element.217), channel_id=1, source_target_pairs={{0,8},{4,12},{8,0},{12,4},{16,24},{20,28},{24,16},{28,20},{1,9},{5... | collective-permute-start | bytes 294920 | tf_op jit(solution)/shard_map/ppermute | solution.py:689
  365.6 13.1 %collective-permute-start.14 = (bf16[192,256]{1,0:T(8,128)(2,1)}, bf16[192,256]{1,0:T(8,128)(2,1)S(1)}, u32[]{:S(2)}, u32[]{:S(2)}) collective-permute-start(bf16[192,256]{1,0:T(8,128)(2,1)} %get-tuple-element.215), channel_id=1, source_target_pairs={{0,4},{4,0},{8,12},{12,8},{16,20},{20,16},{24,28},{28,24},{1,5},{5... | collective-permute-start | bytes 294920 | tf_op jit(solution)/shard_map/ppermute | solution.py:689
  366.8 13.4 %collective-permute-start.11 = (bf16[192,640]{1,0:T(8,128)(2,1)S(1)}, bf16[192,640]{1,0:T(8,128)(2,1)S(1)}, u32[]{:S(2)}, u32[]{:S(2)}) collective-permute-start(bf16[192,640]{1,0:T(8,128)(2,1)S(1)} %fusion.15), channel_id=1, source_target_pairs={{0,2},{1,3},{2,0},{3,1},{4,6},{5,7},{6,4},{7,5},{8,10},{9,11},{10,... | collective-permute-start | bytes 737288 | tf_op jit(solution)/shard_map/ppermute | solution.py:689
  381.4 23.3 %collective-permute-start.17 = (bf16[192,896]{1,0:T(8,128)(2,1)S(1)}, bf16[192,896]{1,0:T(8,128)(2,1)S(1)}, u32[]{:S(2)}, u32[]{:S(2)}) collective-permute-start(bf16[192,896]{1,0:T(8,128)(2,1)S(1)} %pad_maximum_fusion), channel_id=1, source_target_pairs={{0,16},{4,20},{8,24},{12,28},{16,0},{20,4},{24,8},{28,12},{1,17},{... | collective-permute-start | bytes 1032200 | tf_op jit(solution)/shard_map/ppermute | solution.py:689
  404.8 20.5 %copy-start.11 = (bf16[192,896]{1,0:T(8,128)(2,1)}, bf16[192,896]{1,0:T(8,128)(2,1)S(1)}, u32[]{:S(2)}) copy-start(bf16[192,896]{1,0:T(8,128)(2,1)S(1)} %add_convert_fusion.3.refs_0_) | copy-start | bytes 1032196
  404.8 20.5 %collective-permute-start.18 = (bf16[192,896]{1,0:T(8,128)(2,1)S(1)}, bf16[192,896]{1,0:T(8,128)(2,1)S(1)}, u32[]{:S(2)}, u32[]{:S(2)}) collective-permute-start(bf16[192,896]{1,0:T(8,128)(2,1)S(1)} %add_convert_fusion.3.refs_0_), channel_id=1, source_target_pairs={{0,4},{4,0},{8,12},{12,8},{16,20},{20,16},{24,28},{28,24},{1,5},{5... | collective-permute-start | bytes 1032200 | tf_op jit(solution)/shard_map/ppermute | solution.py:689
  406.4 19.0 %collective-permute-start.19 = (bf16[192,896]{1,0:T(8,128)(2,1)S(1)}, bf16[192,896]{1,0:T(8,128)(2,1)}, u32[]{:S(2)}, u32[]{:S(2)}) collective-permute-start(bf16[192,896]{1,0:T(8,128)(2,1)S(1)} %add_convert_fusion.3.refs_0_), channel_id=1, source_target_pairs={{0,8},{4,12},{8,0},{12,4},{16,24},{20,28},{24,16},{28,20},{1,9},{5... | collective-permute-start | bytes 1032200 | tf_op jit(solution)/shard_map/ppermute | solution.py:689
  406.4 19.0 %collective-permute-start.20 = (bf16[192,896]{1,0:T(8,128)(2,1)S(1)}, bf16[192,896]{1,0:T(8,128)(2,1)}, u32[]{:S(2)}, u32[]{:S(2)}) collective-permute-start(bf16[192,896]{1,0:T(8,128)(2,1)S(1)} %add_convert_fusion.3.refs_0_), channel_id=1, source_target_pairs={{0,12},{4,8},{8,4},{12,0},{16,28},{20,24},{24,20},{28,16},{1,13},{... | collective-permute-start | bytes 1032200 | tf_op jit(solution)/shard_map/ppermute | solution.py:689
  417.9 11.4 %copy-start.1 = (s32[2,2048]{1,0:T(2,128)S(1)}, s32[2,2048]{1,0:T(2,128)}, u32[]{:S(2)}) copy-start(s32[2,2048]{1,0:T(2,128)} %param.15) | copy-start | bytes 49156
  (8 other events, 7.8 us)
Sparse Core Ops, SparseCore 0:
  13.3 72.9 all-gather.3
  87.9 65.7 all-gather.5
  155.3 30.7 all-gather.7
  254.9 152.8 reduce-scatter.1

commit v5 on v4

--- a/solution.py
+++ b/solution.py
@@ -26,7 +26,7 @@
 )
 VMEM_MOST = 56 << 20
 COST_SHARE = 0.4
-FILLER = 0.02
+FILLER = 0.2
 G_AFTER = 8
 
 

time: 443 us -> 443 us (level)
  no operation moved by 1% of the time
where the time goes in v5:
time: 443 us; the launch traced here: 436 us
  Pallas kernels  164 us (37%)
  waiting for transfers between devices  115 us (26%)
  starting transfers between devices  64.6 us (15%)
  blocking collectives  45.8 us (10%)
  local copies, waits for them, and re-layouts  23.1 us (5%)
  between operations  14.6 us (3%)
  other arithmetic  9.92 us (2%)
    ppermute x21, waiting for transfers between devices, swap(): return lax.ppermute(array, axis, [(i, i ^ bit) for i in range(size)])  66.8 us
    pallas_call x10, Pallas kernels, one_step(): pl.pallas_call(kernel, out_shape=tuple(outs), in_specs=[pl.BlockSpec(memo...  57.7 us
    all_to_all x8, waiting for transfers between devices, exchange(): return lax.all_to_all(array, 'seq', split_axis=0, concat_axis=0, tiled=True)  46.4 us
    all_to_all x2, blocking collectives, exchange(): return lax.all_to_all(array, 'seq', split_axis=0, concat_axis=0, tiled=True)  45.8 us
    all_to_all x8, starting transfers between devices, exchange(): return lax.all_to_all(array, 'seq', split_axis=0, concat_axis=0, tiled=True)  39.3 us
    pallas_call x2, Pallas kernels, expert_pass(): pl.pallas_call(functools.partial(expert_kernel, index=index, local=local,...  36.9 us
    ppermute x21, starting transfers between devices, swap(): return lax.ppermute(array, axis, [(i, i ^ bit) for i in range(size)])  24.9 us
    pallas_call x1, Pallas kernels, attention_bwd(): pl.pallas_call(bwd_kernel, grid=(pairs,), out_shape=(shape(qkv.shape, BF)...  23.3 us
  transfers between devices with their start and end apart: 33, of which 16 were waited for; matrix products, arithmetic and copies ran while one was open for 5% of the time, Pallas kernels for 37%

profile of v5, /device:TPU:0, one launch (start us, length us, event | category | flops | bytes accessed | tf_op | source)
XLA Modules:
  0.0 436.3 jit_solution(2835660178673354555)
XLA Ops:
  7.2 3.0 copy_bitcast_fusion
  10.7 2.5 fusion.18
  15.1 2.3 shard_map.212.refs_0_
  17.4 3.0 collective-permute-start
  20.5 2.7 collective-permute-start.3
  24.6 1.6 collective-permute-start.5
  26.6 13.9 %collective-permute-done.3.refs_1_ = bf16[256,768]{1,0:T(8,128)(2,1)S(1)} collective-permute-done((bf16[256,768]{1,0:T(8,128)(2,1)S(1)}, bf16[256,768]{1,0:T(8,128)(2,1)S(1)}, u32[]{:S(2)}, u32[]{:S(2)}) %collective-permute-start.3) | collective-permute-done | bytes 393248 | tf_op jit(solution)/shard_map/ppermute | solution.py:689
  41.8 2.2 collective-permute-done.5.refs_3_
  44.0 6.3 %collective-permute-done.6.refs_4_ = bf16[256,768]{1,0:T(8,128)(2,1)S(1)} collective-permute-done((bf16[256,768]{1,0:T(8,128)(2,1)S(1)}, bf16[256,768]{1,0:T(8,128)(2,1)S(1)}, u32[]{:S(2)}, u32[]{:S(2)}) %collective-permute-start.6) | collective-permute-done | bytes 393248 | tf_op jit(solution)/shard_map/ppermute | solution.py:689
  52.8 1.8 collective-permute-start.9
  55.6 4.6 %shard_map.213 = (bf16[768,576]{1,0:T(8,128)(2,1)}, bf16[768,768]{1,0:T(8,128)(2,1)}, f32[128,768]{1,0:T(8,128)}, f32[3,384,256]{2,1,0:T(8,128)}) custom-call(s32[1]{0:T(128)} %bitcast.me_ref, bf16[192,1472]{1,0:T(8,128)(2,1)} %shard_map.212.refs_0_, bf16[192,1472]{1,0:T(8,128)(2,1)} %copy-done.12, bf16[192,1472]{1,0:T(8,128)(2,1)} %copy-done.13, ...), custom_call_target="tpu_custom_call" | custom-call | flops 240000000 | bytes 471859 | tf_op jit(solution)/shard_map/pallas_call | solution.py:207
  60.2 2.0 collective-permute-done.7.refs_5_
  64.7 4.3 shard_map.214
  70.0 2.8 fusion.2
  72.8 5.3 %all-to-all-start = ((bf16[8,152,768]{2,1,0:T(8,128)(2,1)}), bf16[8,152,768]{2,1,0:T(8,128)(2,1)S(1)}, u32[]{:S(2)}, u32[]{:S(2)}) async-start(bf16[8,152,768]{2,1,0:T(8,128)(2,1)} %fusion.2), calls=%async_computation | async-start | bytes 3735552 | tf_op jit(solution)/shard_map/all_to_all | solution.py:702
  78.8 7.1 %shard_map.215 = (bf16[8,576,256]{2,1,0:T(8,128)(2,1)}, bf16[8,256,768]{2,1,0:T(8,128)(2,1)}) custom-call(s32[1]{0:T(128)} %bitcast.9.me_ref.own_ref, f32[128,768]{1,0:T(8,128)} %get-tuple-element.86.small_ref, bf16[768,576]{1,0:T(8,128)(2,1)} %get-tuple-element.91.w_ref, bf16[256,768]{1,0:T(8,128)(2,1)} %copy-done.9, bf16[256,768]{1,0:T(8,128)(2,1)} %copy-done.15, ...), custom_call_target="tpu_custom_call" | custom-call | flops 289910304 | bytes 794296 | tf_op jit(solution)/shard_map/pallas_call | solution.py:207
  85.9 16.5 %shard_map.216 = (bf16[8,192,256]{2,1,0:T(8,128)(2,1)}, f32[3,64,2048]{2,1,0:T(8,128)}, f32[3,1,2048]{2,1,0:T(1,128)}) custom-call(bf16[8,576,256]{2,1,0:T(8,128)(2,1)} %get-tuple-element.92.qkv_ref, s32[1,2048]{1,0:T(1,128)} %constant_dynamic-slice_fusion.3.seg_ref, f32[3,384,256]{2,1,0:T(8,128)} %get-tuple-element.93.band_ref), custom_call_target="tpu_custom_call" | custom-call | flops 7200000000 | bytes 2400000 | tf_op jit(solution)/shard_map/pallas_call | solution.py:154
  102.4 14.7 %all-to-all-done = bf16[8,152,768]{2,1,0:T(8,128)(2,1)S(1)} async-done(((bf16[8,152,768]{2,1,0:T(8,128)(2,1)}), bf16[8,152,768]{2,1,0:T(8,128)(2,1)S(1)}, u32[]{:S(2)}, u32[]{:S(2)}) %all-to-all-start) | async-done | bytes 1867808 | tf_op jit(solution)/shard_map/all_to_all | solution.py:702
  117.1 22.9 %all_to_all.50.chunk_ref.att_ref = bf16[8,192,256]{2,1,0:T(8,128)(2,1)} all-to-all(bf16[8,192,256]{2,1,0:T(8,128)(2,1)} %get-tuple-element.99), channel_id=1, replica_groups=mesh['seq'=8,'fsdp'=4] {'seq'}, dimensions={0} | all-to-all | bytes 1572864 | tf_op jit(solution)/shard_map/all_to_all | solution.py:702
  140.0 5.0 %shard_map.217 = (f32[512,768]{1,0:T(8,128)}, f32[512,2]{1,0:T(8,128)}, bf16[576,768]{1,0:T(8,128)(2,1)}, bf16[576,768]{1,0:T(8,128)(2,1)}) custom-call(bf16[2,256,768]{2,1,0:T(8,128)(2,1)} %tok_ref.3, f32[128,768]{1,0:T(8,128)} %get-tuple-element.86.small_ref, bf16[768,768]{1,0:T(8,128)(2,1)} %get-tuple-element.87.w_ref, s32[512,2]{1,0:T(8,128)} %bitcast.65, ...), custom_call_target="tpu_custom_call" | custom-call | flops 241591904 | bytes 520028 | tf_op jit(solution)/shard_map/pallas_call | solution.py:207
  145.1 3.6 all-to-all-start.2
  149.4 21.2 %all-to-all-done.2 = bf16[8,72,768]{2,1,0:T(8,128)(2,1)S(1)} async-done(((bf16[8,72,768]{2,1,0:T(8,128)(2,1)}), bf16[8,72,768]{2,1,0:T(8,128)(2,1)S(1)}, u32[]{:S(2)}, u32[]{:S(2)}) %all-to-all-start.2) | async-done | bytes 884768 | tf_op jit(solution)/shard_map/all_to_all | solution.py:702
  170.6 4.4 %all-to-all-start.3 = ((bf16[8,72,768]{2,1,0:T(8,128)(2,1)}), bf16[8,72,768]{2,1,0:T(8,128)(2,1)}, u32[]{:S(2)}, u32[]{:S(2)}) async-start(bf16[8,72,768]{2,1,0:T(8,128)(2,1)} %bitcast.81), calls=%async_computation.3 | async-start | bytes 1769472 | tf_op jit(solution)/shard_map/all_to_all | solution.py:702
  177.3 18.5 %shard_map.218 = (bf16[576,768]{1,0:T(8,128)(2,1)}, bf16[576,768]{1,0:T(8,128)(2,1)}, bf16[16,576]{1,0:T(8,128)(2,1)}, bf16[576,768]{1,0:T(8,128)(2,1)}, bf16[4,...) custom-call(s32[1]{0:T(128)} %bitcast.9.me_ref.own_ref, bf16[576,768]{1,0:T(8,128)(2,1)} %bitcast.72, ...), custom_call_target="tpu_custom_call" | custom-call | flops 5435817984 | bytes 11324620 | tf_op jit(solution)/shard_map/pallas_call | solution.py:595
  196.9 4.9 %all-to-all-start.4 = ((bf16[8,72,768]{2,1,0:T(8,128)(2,1)}), bf16[8,72,768]{2,1,0:T(8,128)(2,1)S(1)}, u32[]{:S(2)}, u32[]{:S(2)}) async-start(bf16[8,72,768]{2,1,0:T(8,128)(2,1)} %bitcast.80), calls=%async_computation.4 | async-start | bytes 1769472 | tf_op jit(solution)/shard_map/all_to_all | solution.py:702
  202.7 18.4 %shard_map.219 = (bf16[576,768]{1,0:T(8,128)(2,1)}, bf16[576,768]{1,0:T(8,128)(2,1)}, bf16[16,576]{1,0:T(8,128)(2,1)}, bf16[576,768]{1,0:T(8,128)(2,1)}, bf16[4,...) custom-call(s32[1]{0:T(128)} %bitcast.9.me_ref.own_ref, ...), custom_call_target="tpu_custom_call" | custom-call | flops 5435817984 | bytes 11324620 | tf_op jit(solution)/shard_map/pallas_call | solution.py:595
  222.7 2.2 fusion.3
  224.9 6.0 %all-to-all-start.5 = ((bf16[8,80,768]{2,1,0:T(8,128)(2,1)}), bf16[8,80,768]{2,1,0:T(8,128)(2,1)S(1)}, u32[]{:S(2)}, u32[]{:S(2)}) async-start(bf16[8,80,768]{2,1,0:T(8,128)(2,1)} %fusion.3), calls=%async_computation.5 | async-start | bytes 1966080 | tf_op jit(solution)/shard_map/all_to_all | solution.py:702
  231.2 21.9 %shard_map.220 = bf16[4,2,2,768,768]{4,3,2,1,0:T(8,128)(2,1)} custom-call(bf16[576,768]{1,0:T(8,128)(2,1)} %bitcast.73, bf16[576,768]{1,0:T(8,128)(2,1)} %get-tuple-element.115.refs_1_, bf16[4,576,768]{2,1,0:T(8,128)(2,1)} %get-tuple-element.117.refs_2_, bf16[4,576,768]{2,1,0:T(8,128)(2,1)} %get-tuple-element.118.refs_3_, ...), custom_call_target="tpu_custom_call" | custom-call | flops 400000 | bytes 400000 | tf_op jit(solution)/shard_map/pallas_call | solution.py:645
  254.8 5.3 %all-to-all-start.6 = ((bf16[8,72,768]{2,1,0:T(8,128)(2,1)}), bf16[8,72,768]{2,1,0:T(8,128)(2,1)S(1)}, u32[]{:S(2)}, u32[]{:S(2)}) async-start(bf16[8,72,768]{2,1,0:T(8,128)(2,1)} %bitcast.30), calls=%async_computation.6 | async-start | bytes 1769472 | tf_op jit(solution)/shard_map/all_to_all | solution.py:702
  260.9 10.9 %shard_map.221 = (f32[512,768]{1,0:T(8,128)}, bf16[8,192,256]{2,1,0:T(8,128)(2,1)}, bf16[2,192,1024]{2,1,0:T(8,128)(2,1)}, bf16[2,192,1024]{2,1,0:T(8,128)(2,1)}) custom-call(s32[1]{0:T(128)} %bitcast.me_ref, f32[1,1152]{1,0:T(1,128)} %reshape.183.dgate_ref, s32[512,2]{1,0:T(8,128)} %get-tuple-element.113.slot_ref, s32[512,2]{1,0:T(8,128)} %bitcast.66, ...), custom_call_target="tpu_custom_call" | custom-call | flops 338228672 | bytes 835461 | tf_op jit(solution)/shard_map/pallas_call | solution.py:207
  271.8 8.7 %all-to-all-done.6 = bf16[8,72,768]{2,1,0:T(8,128)(2,1)S(1)} async-done(((bf16[8,72,768]{2,1,0:T(8,128)(2,1)}), bf16[8,72,768]{2,1,0:T(8,128)(2,1)S(1)}, u32[]{:S(2)}, u32[]{:S(2)}) %all-to-all-start.6) | async-done | bytes 884768 | tf_op jit(solution)/shard_map/all_to_all | solution.py:702
  280.5 22.8 %all_to_all.51.do_ref = bf16[8,192,256]{2,1,0:T(8,128)(2,1)} all-to-all(bf16[8,192,256]{2,1,0:T(8,128)(2,1)} %get-tuple-element.130), channel_id=1, replica_groups=mesh['seq'=8,'fsdp'=4] {'seq'}, dimensions={0} | all-to-all | bytes 1572864 | tf_op jit(solution)/shard_map/all_to_all | solution.py:702
  303.3 3.6 all-to-all-start.8
  306.9 23.3 %shard_map.222 = (bf16[8,576,256]{2,1,0:T(8,128)(2,1)}, f32[3,384,256]{2,1,0:T(8,128)}) custom-call(bf16[8,576,256]{2,1,0:T(8,128)(2,1)} %get-tuple-element.92.qkv_ref, s32[1,2048]{1,0:T(1,128)} %constant_dynamic-slice_fusion.3.seg_ref, f32[3,384,256]{2,1,0:T(8,128)} %get-tuple-element.93.band_ref, f32[3,64,2048]{2,1,0:T(8,128)} %get-tuple-element.101.wide_ref, ...), custom_call_target="tpu_custom_call" | custom-call | flops 12000000000 | bytes 3600000 | tf_op jit(solution)/shard_map/pallas_call | solution.py:179
  331.1 6.3 %all-to-all-start.9 = ((bf16[8,576,256]{2,1,0:T(8,128)(2,1)}), bf16[8,576,256]{2,1,0:T(8,128)(2,1)S(1)}, u32[]{:S(2)}, u32[]{:S(2)}) async-start(bf16[8,576,256]{2,1,0:T(8,128)(2,1)} %get-tuple-element.137.d_ref), calls=%async_computation.9 | async-start | bytes 4718592 | tf_op jit(solution)/shard_map/all_to_all | solution.py:702
  337.4 2.3 collective-permute-done.12
  341.7 7.2 %shard_map.224 = (bf16[2,192,640]{2,1,0:T(8,128)(2,1)}, bf16[2,192,640]{2,1,0:T(8,128)(2,1)}) custom-call(s32[1]{0:T(128)} %bitcast.me_ref, bf16[8,256,768]{2,1,0:T(8,128)(2,1)} %get-tuple-element.138.first_ref, bf16[8,576,256]{2,1,0:T(8,128)(2,1)} %get-tuple-element.137.d_ref, f32[3,384,256]{2,1,0:T(8,128)} %get-tuple-element.139.band_ref), custom_call_target="tpu_custom_call" | custom-call | flops 289910304 | bytes 613417 | tf_op jit(solution)/shard_map/pallas_call | solution.py:207
  349.0 12.3 %collective-permute-done.13 = bf16[192,1024]{1,0:T(8,128)(2,1)S(1)} collective-permute-done((bf16[192,1024]{1,0:T(8,128)(2,1)S(1)}, bf16[192,1024]{1,0:T(8,128)(2,1)S(1)}, u32[]{:S(2)}, u32[]{:S(2)}) %collective-permute-start.13) | collective-permute-done | bytes 393248 | tf_op jit(solution)/shard_map/ppermute | solution.py:689
  362.2 2.9 collective-permute-start.16
  367.4 10.3 %collective-permute-done.16 = bf16[192,256]{1,0:T(8,128)(2,1)S(1)} collective-permute-done((bf16[192,256]{1,0:T(8,128)(2,1)}, bf16[192,256]{1,0:T(8,128)(2,1)S(1)}, u32[]{:S(2)}, u32[]{:S(2)}) %collective-permute-start.16) | collective-permute-done | bytes 98336 | tf_op jit(solution)/shard_map/ppermute | solution.py:689
  381.4 4.0 collective-permute-start.17
  385.4 5.6 %shard_map.223 = bf16[512,768]{1,0:T(8,128)(2,1)} custom-call(f32[512,768]{1,0:T(8,128)} %get-tuple-element.132.mid_ref, s32[512,2]{1,0:T(8,128)} %get-tuple-element.113.slot_ref, f32[512,2]{1,0:T(8,128)} %get-tuple-element.114.gate_ref, bf16[576,768]{1,0:T(8,128)(2,1)} %bitcast.70, bf16[576,768]{1,0:T(8,128)(2,1)} %bitcast.71), custom_call_target="tpu_custom_call" | custom-call | flops 144955152 | bytes 330956 | tf_op jit(solution)/shard_map/pallas_call | solution.py:207
  391.0 13.7 %collective-permute-done.17 = bf16[192,896]{1,0:T(8,128)(2,1)S(1)} collective-permute-done((bf16[192,896]{1,0:T(8,128)(2,1)S(1)}, bf16[192,896]{1,0:T(8,128)(2,1)S(1)}, u32[]{:S(2)}, u32[]{:S(2)}) %collective-permute-start.17) | collective-permute-done | bytes 344096 | tf_op jit(solution)/shard_map/ppermute | solution.py:689
  406.4 2.0 collective-permute-start.20
  410.5 7.4 %shard_map.225 = f32[2,256,768]{2,1,0:T(8,128)} custom-call(bf16[2,256,768]{2,1,0:T(8,128)(2,1)} %tok_ref.3, f32[128,768]{1,0:T(8,128)} %get-tuple-element.86.small_ref, bf16[768,2304]{1,0:T(8,128)(2,1)} %all-gather.8.cloned.1.call-done.w_ref, f32[512,768]{1,0:T(8,128)} %get-tuple-element.136.dmid_ref, bf16[8,576,256]{2,1,0:T(8,128)(2,1)} %copy-done.2), custom_call_target="tpu_custom_call" | custom-call | flops 289910304 | bytes 817889 | tf_op jit(solution)/shard_map/pallas_call | solution.py:207
  417.9 7.4 %shard_map.226 = (f32[768,2,768]{2,1,0:T(2,128)}, f32[768,2,768]{2,1,0:T(2,128)}) custom-call(bf16[2,2,768,768]{3,2,1,0:T(8,128)(2,1)} %bitcast.67), custom_call_target="tpu_custom_call" | custom-call | flops 400000 | bytes 400000 | tf_op jit(solution)/shard_map/pallas_call | solution.py:672
  426.1 3.3 shard_map.227
  (130 shorter events, 36.9 us)
Async XLA Ops:
  7.2 71.0 %copy-start = (s32[2,2048]{1,0:T(2,128)S(1)}, s32[2,2048]{1,0:T(2,128)}, u32[]{:S(2)}) copy-start(s32[2,2048]{1,0:T(2,128)} %param.15) | copy-start | bytes 49156
  7.2 170.1 %all-gather.4.cloned.1.call-start = ((), (), s32[]{:S(2)}) async-start(), calls=%async_computation.11 | async-start | bytes 11796480 | tf_op jit(solution)/shard_map/all_gather | solution.py:840
  13.2 7.2 %copy-start.3 = (bf16[2,256,768]{2,1,0:T(8,128)(2,1)S(1)}, bf16[2,256,768]{2,1,0:T(8,128)(2,1)}, u32[]{:S(2)}) copy-start(bf16[2,256,768]{2,1,0:T(8,128)(2,1)} %tok_ref.3) | copy-start | bytes 2359300
  13.2 189.5 %all-gather.6.cloned.1.call-start = ((), (), s32[]{:S(2)}) async-start(), calls=%async_computation.12 | async-start | bytes 11796480 | tf_op jit(solution)/shard_map/all_gather | solution.py:840
  17.4 24.4 %collective-permute-start = (bf16[192,1472]{1,0:T(8,128)(2,1)}, bf16[192,1472]{1,0:T(8,128)(2,1)S(1)}, u32[]{:S(2)}, u32[]{:S(2)}) collective-permute-start(bf16[192,1472]{1,0:T(8,128)(2,1)} %shard_map.212.refs_0_), channel_id=1, source_target_pairs={{0,2},{1,3},{2,0},{3,1},{4,6},{5,7},{6,4},{7,5},{8,10},{9,11},{10,... | collective-permute-start | bytes 1695752 | tf_op jit(solution)/shard_map/ppermute | solution.py:689
  20.4 48.6 %copy-start.9 = (bf16[256,768]{1,0:T(8,128)(2,1)}, bf16[256,768]{1,0:T(8,128)(2,1)S(1)}, u32[]{:S(2)}) copy-start(bf16[256,768]{1,0:T(8,128)(2,1)S(1)} %get-tuple-element.213.refs_0_) | copy-start | bytes 1179652
  20.5 20.1 %collective-permute-start.3 = (bf16[256,768]{1,0:T(8,128)(2,1)S(1)}, bf16[256,768]{1,0:T(8,128)(2,1)S(1)}, u32[]{:S(2)}, u32[]{:S(2)}) collective-permute-start(bf16[256,768]{1,0:T(8,128)(2,1)S(1)} %get-tuple-element.214), channel_id=1, source_target_pairs={{0,16},{4,20},{8,24},{12,28},{16,0},{20,4},{24,8},{28,12},{1,17},{... | collective-permute-start | bytes 1179656 | tf_op jit(solution)/shard_map/ppermute | solution.py:689
  23.1 18.7 %collective-permute-start.4 = (bf16[256,768]{1,0:T(8,128)(2,1)S(1)}, bf16[256,768]{1,0:T(8,128)(2,1)S(1)}, u32[]{:S(2)}, u32[]{:S(2)}) collective-permute-start(bf16[256,768]{1,0:T(8,128)(2,1)S(1)} %get-tuple-element.213.refs_0_), channel_id=1, source_target_pairs={{0,4},{4,0},{8,12},{12,8},{16,20},{20,16},{24,28},{28,24},{1,5},{5... | collective-permute-start | bytes 1179656 | tf_op jit(solution)/shard_map/ppermute | solution.py:689
  24.6 19.4 %collective-permute-start.5 = (bf16[256,768]{1,0:T(8,128)(2,1)S(1)}, bf16[256,768]{1,0:T(8,128)(2,1)S(1)}, u32[]{:S(2)}, u32[]{:S(2)}) collective-permute-start(bf16[256,768]{1,0:T(8,128)(2,1)S(1)} %get-tuple-element.213.refs_0_), channel_id=1, source_target_pairs={{0,8},{4,12},{8,0},{12,4},{16,24},{20,28},{24,16},{28,20},{1,9},{5... | collective-permute-start | bytes 1179656 | tf_op jit(solution)/shard_map/ppermute | solution.py:689
  26.2 24.1 %collective-permute-start.6 = (bf16[256,768]{1,0:T(8,128)(2,1)S(1)}, bf16[256,768]{1,0:T(8,128)(2,1)S(1)}, u32[]{:S(2)}, u32[]{:S(2)}) collective-permute-start(bf16[256,768]{1,0:T(8,128)(2,1)S(1)} %get-tuple-element.213.refs_0_), channel_id=1, source_target_pairs={{0,12},{4,8},{8,4},{12,0},{16,28},{20,24},{24,20},{28,16},{1,13},{... | collective-permute-start | bytes 1179656 | tf_op jit(solution)/shard_map/ppermute | solution.py:689
  40.5 38.3 %copy-start.15 = (bf16[256,768]{1,0:T(8,128)(2,1)}, bf16[256,768]{1,0:T(8,128)(2,1)S(1)}, u32[]{:S(2)}) copy-start(bf16[256,768]{1,0:T(8,128)(2,1)S(1)} %collective-permute-done.3.refs_1_) | copy-start | bytes 1179652
  40.5 14.0 %collective-permute-start.1 = (bf16[192,1472]{1,0:T(8,128)(2,1)}, bf16[192,1472]{1,0:T(8,128)(2,1)S(1)}, u32[]{:S(2)}, u32[]{:S(2)}) collective-permute-start(bf16[192,1472]{1,0:T(8,128)(2,1)} %shard_map.212.refs_0_), channel_id=1, source_target_pairs={{0,1},{1,0},{2,3},{3,2},{4,5},{5,4},{6,7},{7,6},{8,9},{9,8},{10,11... | collective-permute-start | bytes 1695752 | tf_op jit(solution)/shard_map/ppermute | solution.py:689
  41.8 12.8 %copy-start.12 = (bf16[192,1472]{1,0:T(8,128)(2,1)}, bf16[192,1472]{1,0:T(8,128)(2,1)S(1)}, u32[]{:S(2)}) copy-start(bf16[192,1472]{1,0:T(8,128)(2,1)S(1)} %collective-permute-done.refs_1_) | copy-start | bytes 1695748
  41.8 12.8 %collective-permute-start.2 = (bf16[192,1472]{1,0:T(8,128)(2,1)S(1)}, bf16[192,1472]{1,0:T(8,128)(2,1)S(1)}, u32[]{:S(2)}, u32[]{:S(2)}) collective-permute-start(bf16[192,1472]{1,0:T(8,128)(2,1)S(1)} %collective-permute-done.refs_1_), channel_id=1, source_target_pairs={{0,1},{1,0},{2,3},{3,2},{4,5},{5,4},{6,7},{7,6},{8,9},{9,8},{10,11... | collective-permute-start | bytes 1695752 | tf_op jit(solution)/shard_map/ppermute | solution.py:689
  41.8 37.0 %copy-start.16 = (bf16[256,768]{1,0:T(8,128)(2,1)}, bf16[256,768]{1,0:T(8,128)(2,1)S(1)}, u32[]{:S(2)}) copy-start(bf16[256,768]{1,0:T(8,128)(2,1)S(1)} %collective-permute-done.4.refs_2_) | copy-start | bytes 1179652
  44.0 34.8 %copy-start.17 = (bf16[256,768]{1,0:T(8,128)(2,1)}, bf16[256,768]{1,0:T(8,128)(2,1)S(1)}, u32[]{:S(2)}) copy-start(bf16[256,768]{1,0:T(8,128)(2,1)S(1)} %collective-permute-done.5.refs_3_) | copy-start | bytes 1179652
  51.1 11.1 %collective-permute-start.7 = (bf16[256,768]{1,0:T(8,128)(2,1)S(1)}, bf16[256,768]{1,0:T(8,128)(2,1)}, u32[]{:S(2)}, u32[]{:S(2)}) collective-permute-start(bf16[256,768]{1,0:T(8,128)(2,1)S(1)} %collective-permute-done.3.refs_1_), channel_id=1, source_target_pairs={{0,4},{4,0},{8,12},{12,8},{16,20},{20,16},{24,28},{28,24},{1,5},{5... | collective-permute-start | bytes 1179656 | tf_op jit(solution)/shard_map/ppermute | solution.py:689
  52.6 20.2 %collective-permute-start.8 = (bf16[256,768]{1,0:T(8,128)(2,1)S(1)}, bf16[256,768]{1,0:T(8,128)(2,1)}, u32[]{:S(2)}, u32[]{:S(2)}) collective-permute-start(bf16[256,768]{1,0:T(8,128)(2,1)S(1)} %collective-permute-done.3.refs_1_), channel_id=1, source_target_pairs={{0,8},{4,12},{8,0},{12,4},{16,24},{20,28},{24,16},{28,20},{1,9},{5... | collective-permute-start | bytes 1179656 | tf_op jit(solution)/shard_map/ppermute | solution.py:689
  52.8 20.1 %collective-permute-start.9 = (bf16[256,768]{1,0:T(8,128)(2,1)S(1)}, bf16[256,768]{1,0:T(8,128)(2,1)}, u32[]{:S(2)}, u32[]{:S(2)}) collective-permute-start(bf16[256,768]{1,0:T(8,128)(2,1)S(1)} %collective-permute-done.3.refs_1_), channel_id=1, source_target_pairs={{0,12},{4,8},{8,4},{12,0},{16,28},{20,24},{24,20},{28,16},{1,13},{... | collective-permute-start | bytes 1179656 | tf_op jit(solution)/shard_map/ppermute | solution.py:689
  63.0 1.7 copy-start.4
  63.3 1.4 copy-start.11
  72.8 44.2 %all-to-all-start = ((bf16[8,152,768]{2,1,0:T(8,128)(2,1)}), bf16[8,152,768]{2,1,0:T(8,128)(2,1)S(1)}, u32[]{:S(2)}, u32[]{:S(2)}) async-start(bf16[8,152,768]{2,1,0:T(8,128)(2,1)} %fusion.2), calls=%async_computation | async-start | bytes 3735552 | tf_op jit(solution)/shard_map/all_to_all | solution.py:702
  145.1 25.5 %all-to-all-start.2 = ((bf16[8,72,768]{2,1,0:T(8,128)(2,1)}), bf16[8,72,768]{2,1,0:T(8,128)(2,1)S(1)}, u32[]{:S(2)}, u32[]{:S(2)}) async-start(bf16[8,72,768]{2,1,0:T(8,128)(2,1)} %bitcast.82), calls=%async_computation.2 | async-start | bytes 1769472 | tf_op jit(solution)/shard_map/all_to_all | solution.py:702
  148.6 260.5 %all-gather.8.cloned.1.call-start = ((), (), s32[]{:S(2)}) async-start(), calls=%async_computation.13 | async-start | bytes 4423680 | tf_op jit(solution)/shard_map/all_gather | solution.py:843
  170.6 6.7 %copy-start.8 = (bf16[8,72,768]{2,1,0:T(8,128)(2,1)}, bf16[8,72,768]{2,1,0:T(8,128)(2,1)S(1)}, u32[]{:S(2)}) copy-start(bf16[8,72,768]{2,1,0:T(8,128)(2,1)S(1)} %all-to-all-done.2) | copy-start | bytes 2654212
  170.6 26.3 %all-to-all-start.3 = ((bf16[8,72,768]{2,1,0:T(8,128)(2,1)}), bf16[8,72,768]{2,1,0:T(8,128)(2,1)}, u32[]{:S(2)}, u32[]{:S(2)}) async-start(bf16[8,72,768]{2,1,0:T(8,128)(2,1)} %bitcast.81), calls=%async_computation.3 | async-start | bytes 1769472 | tf_op jit(solution)/shard_map/all_to_all | solution.py:702
  196.9 28.0 %all-to-all-start.4 = ((bf16[8,72,768]{2,1,0:T(8,128)(2,1)}), bf16[8,72,768]{2,1,0:T(8,128)(2,1)S(1)}, u32[]{:S(2)}, u32[]{:S(2)}) async-start(bf16[8,72,768]{2,1,0:T(8,128)(2,1)} %bitcast.80), calls=%async_computation.4 | async-start | bytes 1769472 | tf_op jit(solution)/shard_map/all_to_all | solution.py:702
  224.9 28.2 %copy-start.5 = (bf16[8,72,768]{2,1,0:T(8,128)(2,1)}, bf16[8,72,768]{2,1,0:T(8,128)(2,1)S(1)}, u32[]{:S(2)}) copy-start(bf16[8,72,768]{2,1,0:T(8,128)(2,1)S(1)} %all-to-all-done.4) | copy-start | bytes 2654212
  224.9 28.9 %all-to-all-start.5 = ((bf16[8,80,768]{2,1,0:T(8,128)(2,1)}), bf16[8,80,768]{2,1,0:T(8,128)(2,1)S(1)}, u32[]{:S(2)}, u32[]{:S(2)}) async-start(bf16[8,80,768]{2,1,0:T(8,128)(2,1)} %fusion.3), calls=%async_computation.5 | async-start | bytes 1966080 | tf_op jit(solution)/shard_map/all_to_all | solution.py:702
  230.9 187.0 %reduce-scatter.2.cloned.1.call-start = ((), (), s32[]{:S(2)}) async-start(), calls=%async_computation.14 | async-start | bytes 23592960 | tf_op jit(solution)/shard_map/reduce_scatter | solution.py:870
  254.8 25.7 %all-to-all-start.6 = ((bf16[8,72,768]{2,1,0:T(8,128)(2,1)}), bf16[8,72,768]{2,1,0:T(8,128)(2,1)S(1)}, u32[]{:S(2)}, u32[]{:S(2)}) async-start(bf16[8,72,768]{2,1,0:T(8,128)(2,1)} %bitcast.30), calls=%async_computation.6 | async-start | bytes 1769472 | tf_op jit(solution)/shard_map/all_to_all | solution.py:702
  280.5 49.7 %copy-start.6 = (bf16[8,72,768]{2,1,0:T(8,128)(2,1)}, bf16[8,72,768]{2,1,0:T(8,128)(2,1)S(1)}, u32[]{:S(2)}) copy-start(bf16[8,72,768]{2,1,0:T(8,128)(2,1)S(1)} %all-to-all-done.6) | copy-start | bytes 2654212
  303.3 26.9 %all-to-all-start.8 = ((bf16[8,72,768]{2,1,0:T(8,128)(2,1)}), bf16[8,72,768]{2,1,0:T(8,128)(2,1)S(1)}, u32[]{:S(2)}, u32[]{:S(2)}) async-start(bf16[8,72,768]{2,1,0:T(8,128)(2,1)} %bitcast.32), calls=%async_computation.8 | async-start | bytes 1769472 | tf_op jit(solution)/shard_map/all_to_all | solution.py:702
  330.2 7.2 %copy-start.20 = (bf16[2,192,1024]{2,1,0:T(8,128)(2,1)S(1)}, bf16[2,192,1024]{2,1,0:T(8,128)(2,1)}, u32[]{:S(2)}) copy-start(bf16[2,192,1024]{2,1,0:T(8,128)(2,1)} %get-tuple-element.145) | copy-start | bytes 2359300
  331.1 78.1 %all-to-all-start.9 = ((bf16[8,576,256]{2,1,0:T(8,128)(2,1)}), bf16[8,576,256]{2,1,0:T(8,128)(2,1)S(1)}, u32[]{:S(2)}, u32[]{:S(2)}) async-start(bf16[8,576,256]{2,1,0:T(8,128)(2,1)} %get-tuple-element.137.d_ref), calls=%async_computation.9 | async-start | bytes 4718592 | tf_op jit(solution)/shard_map/all_to_all | solution.py:702
  337.4 2.4 collective-permute-start.12
  341.1 20.2 %collective-permute-start.13 = (bf16[192,1024]{1,0:T(8,128)(2,1)S(1)}, bf16[192,1024]{1,0:T(8,128)(2,1)S(1)}, u32[]{:S(2)}, u32[]{:S(2)}) collective-permute-start(bf16[192,1024]{1,0:T(8,128)(2,1)S(1)} %get-tuple-element.212), channel_id=1, source_target_pairs={{0,2},{1,3},{2,0},{3,1},{4,6},{5,7},{6,4},{7,5},{8,10},{9,11},{10,... | collective-permute-start | bytes 1179656 | tf_op jit(solution)/shard_map/ppermute | solution.py:689
  348.9 16.7 %collective-permute-start.10 = (bf16[2,192,640]{2,1,0:T(8,128)(2,1)}, bf16[2,192,640]{2,1,0:T(8,128)(2,1)}, u32[]{:S(2)}, u32[]{:S(2)}) collective-permute-start(bf16[2,192,640]{2,1,0:T(8,128)(2,1)} %get-tuple-element.142), channel_id=1, source_target_pairs={{0,1},{1,0},{2,3},{3,2},{4,5},{5,4},{6,7},{7,6},{8,9},{9,8},{10,11... | collective-permute-start | bytes 1474568 | tf_op jit(solution)/shard_map/ppermute | solution.py:689
  362.2 15.6 %collective-permute-start.16 = (bf16[192,256]{1,0:T(8,128)(2,1)}, bf16[192,256]{1,0:T(8,128)(2,1)S(1)}, u32[]{:S(2)}, u32[]{:S(2)}) collective-permute-start(bf16[192,256]{1,0:T(8,128)(2,1)} %get-tuple-element.216), channel_id=1, source_target_pairs={{0,12},{4,8},{8,4},{12,0},{16,28},{20,24},{24,20},{28,16},{1,13},{... | collective-permute-start | bytes 294920 | tf_op jit(solution)/shard_map/ppermute | solution.py:689
  365.1 13.7 %collective-permute-start.15 = (bf16[192,256]{1,0:T(8,128)(2,1)}, bf16[192,256]{1,0:T(8,128)(2,1)S(1)}, u32[]{:S(2)}, u32[]{:S(2)}) collective-permute-start(bf16[192,256]{1,0:T(8,128)(2,1)} %get-tuple-element.217), channel_id=1, source_target_pairs={{0,8},{4,12},{8,0},{12,4},{16,24},{20,28},{24,16},{28,20},{1,9},{5... | collective-permute-start | bytes 294920 | tf_op jit(solution)/shard_map/ppermute | solution.py:689
  365.6 13.1 %collective-permute-start.14 = (bf16[192,256]{1,0:T(8,128)(2,1)}, bf16[192,256]{1,0:T(8,128)(2,1)S(1)}, u32[]{:S(2)}, u32[]{:S(2)}) collective-permute-start(bf16[192,256]{1,0:T(8,128)(2,1)} %get-tuple-element.215), channel_id=1, source_target_pairs={{0,4},{4,0},{8,12},{12,8},{16,20},{20,16},{24,28},{28,24},{1,5},{5... | collective-permute-start | bytes 294920 | tf_op jit(solution)/shard_map/ppermute | solution.py:689
  366.8 13.4 %collective-permute-start.11 = (bf16[192,640]{1,0:T(8,128)(2,1)S(1)}, bf16[192,640]{1,0:T(8,128)(2,1)S(1)}, u32[]{:S(2)}, u32[]{:S(2)}) collective-permute-start(bf16[192,640]{1,0:T(8,128)(2,1)S(1)} %fusion.15), channel_id=1, source_target_pairs={{0,2},{1,3},{2,0},{3,1},{4,6},{5,7},{6,4},{7,5},{8,10},{9,11},{10,... | collective-permute-start | bytes 737288 | tf_op jit(solution)/shard_map/ppermute | solution.py:689
  381.4 23.3 %collective-permute-start.17 = (bf16[192,896]{1,0:T(8,128)(2,1)S(1)}, bf16[192,896]{1,0:T(8,128)(2,1)S(1)}, u32[]{:S(2)}, u32[]{:S(2)}) collective-permute-start(bf16[192,896]{1,0:T(8,128)(2,1)S(1)} %pad_maximum_fusion), channel_id=1, source_target_pairs={{0,16},{4,20},{8,24},{12,28},{16,0},{20,4},{24,8},{28,12},{1,17},{... | collective-permute-start | bytes 1032200 | tf_op jit(solution)/shard_map/ppermute | solution.py:689
  404.8 20.5 %copy-start.10 = (bf16[192,896]{1,0:T(8,128)(2,1)}, bf16[192,896]{1,0:T(8,128)(2,1)S(1)}, u32[]{:S(2)}) copy-start(bf16[192,896]{1,0:T(8,128)(2,1)S(1)} %add_convert_fusion.3.refs_0_) | copy-start | bytes 1032196
  404.8 20.5 %collective-permute-start.18 = (bf16[192,896]{1,0:T(8,128)(2,1)S(1)}, bf16[192,896]{1,0:T(8,128)(2,1)S(1)}, u32[]{:S(2)}, u32[]{:S(2)}) collective-permute-start(bf16[192,896]{1,0:T(8,128)(2,1)S(1)} %add_convert_fusion.3.refs_0_), channel_id=1, source_target_pairs={{0,4},{4,0},{8,12},{12,8},{16,20},{20,16},{24,28},{28,24},{1,5},{5... | collective-permute-start | bytes 1032200 | tf_op jit(solution)/shard_map/ppermute | solution.py:689
  406.4 19.0 %collective-permute-start.19 = (bf16[192,896]{1,0:T(8,128)(2,1)S(1)}, bf16[192,896]{1,0:T(8,128)(2,1)}, u32[]{:S(2)}, u32[]{:S(2)}) collective-permute-start(bf16[192,896]{1,0:T(8,128)(2,1)S(1)} %add_convert_fusion.3.refs_0_), channel_id=1, source_target_pairs={{0,8},{4,12},{8,0},{12,4},{16,24},{20,28},{24,16},{28,20},{1,9},{5... | collective-permute-start | bytes 1032200 | tf_op jit(solution)/shard_map/ppermute | solution.py:689
  406.4 19.0 %collective-permute-start.20 = (bf16[192,896]{1,0:T(8,128)(2,1)S(1)}, bf16[192,896]{1,0:T(8,128)(2,1)}, u32[]{:S(2)}, u32[]{:S(2)}) collective-permute-start(bf16[192,896]{1,0:T(8,128)(2,1)S(1)} %add_convert_fusion.3.refs_0_), channel_id=1, source_target_pairs={{0,12},{4,8},{8,4},{12,0},{16,28},{20,24},{24,20},{28,16},{1,13},{... | collective-permute-start | bytes 1032200 | tf_op jit(solution)/shard_map/ppermute | solution.py:689
  417.9 11.4 %copy-start.1 = (s32[2,2048]{1,0:T(2,128)S(1)}, s32[2,2048]{1,0:T(2,128)}, u32[]{:S(2)}) copy-start(s32[2,2048]{1,0:T(2,128)} %param.15) | copy-start | bytes 49156
  (8 other events, 7.8 us)
Sparse Core Ops, SparseCore 0:
  13.3 72.9 all-gather.3
  87.9 65.7 all-gather.5
  155.3 30.7 all-gather.7
  254.9 152.8 reduce-scatter.1
